TPU v7x, 512 devices: a whole 4x8x8 slice. The times are simulated.
512 devices in a mesh: gx: 8 (over y), gy: 8 (over z_lo, core), gz: 8 (over x, z_hi).
Axes of the slice: x: 4, y: 8, z: 8 (z_hi: 2, z_lo: 4; z = z_hi * 4 + z_lo), core: 2. Of those that a mesh axis runs over, the one named last changes fastest.
Arguments:
- coords: float32 [8, 8, 8, 3, 128], P('gx', 'gy', 'gz'), may hold values from 0 to 16, as said below
- species: int32 [8, 8, 8, 128], P('gx', 'gy', 'gz'), may hold values from 0 to 1
- pair_ids: int32 [8, 8, 8, 2, 256], P('gx', 'gy', 'gz'), may hold values from 0 to 3455, as said below
- live_counts: int32 [8, 8, 8, 2], P('gx', 'gy', 'gz'), may hold values from 4 to 128, as said below
- w_two_in: bfloat16 [512, 12], replicated, may hold values from -1.75 to 1.75
- w_two_hid: bfloat16 [512, 512], replicated, may hold values from -0.25 to 0.25
- w_env: bfloat16 [64, 512], replicated, may hold values from -0.25 to 0.25
- w_latent: bfloat16 [512, 704], replicated, may hold values from -0.21875 to 0.21875
- w_out: bfloat16 [1, 512], replicated, may hold values from -0.25 to 0.25
Outputs:
- forces: float32 [8, 8, 8, 3, 128], P('gx', 'gy', 'gz')
- energy: float32 [], replicated
Inputs may be any that keep to these rules, and one draw needn't show every extreme that they name: `coords`: each atom lies inside its domain: x and y below 16, z below 4. `pair_ids`: row 0 holds centres: slots of the first 128 of a domain's list name atoms below 64, the others atoms at or above it. Row 1 is s * 128 + a for atom a of slot s, never the centre itself in slot 13; every neighbour lies within 6 Angstrom of its centre. `live_counts`: slots of a half at or beyond its count are padding and carry no weight.
All inputs are finite; a program needn't handle non-finite values.
Results may differ from a plain program's by a relative error of at most 0.017.
Values sent between devices are 32-bit elements; how exact they have to be, the bound alone decides.
No kernel may reach another device: no remote copies, remote signals or barrier semaphores. Data moves between devices by JAX's collectives and lax.ppermute only.
A program may use at most 64 MiB of HBM per device.

v0:
```python
import math

import jax
import jax.numpy as jnp
from jax import lax
from jax.sharding import PartitionSpec as P

SIDE = 8
NB = 8
NS = 2
TILE = 128


cutoff_radius = 6.0
spacing = 2.0
soften = 0.01
env_norm = 0.25


def extended(cells, sides, width):
    for axis, dim in sides:
        count = lax.axis_size(axis)
        head = lax.slice_in_dim(cells, 0, width, axis=dim)
        tail = lax.slice_in_dim(cells, cells.shape[dim] - width, cells.shape[dim], axis=dim)
        cells = jnp.concatenate(
            [
                lax.ppermute(tail, axis, [(i, (i + 1) % count) for i in range(count)]),
                cells,
                lax.ppermute(head, axis, [((i + 1) % count, i) for i in range(count)]),
            ],
            axis=dim,
        )
    return cells


def envelope(ratio):
    poly = 1.0 - 28.0 * ratio**6 + 48.0 * ratio**7 - 21.0 * ratio**8
    return jnp.where(ratio < 1.0, poly, 0.0 * ratio)


def harmonics(direction):
    along_x, along_y, along_z = (direction[0], direction[1], direction[2])
    root3 = math.sqrt(3.0)
    root15 = math.sqrt(15.0)
    root5 = math.sqrt(5.0)
    rows = [
        jnp.ones_like(along_x),
        root3 * along_x,
        root3 * along_y,
        root3 * along_z,
        root15 * along_x * along_y,
        root15 * along_y * along_z,
        0.5 * root5 * (2.0 * along_z * along_z - along_x * along_x - along_y * along_y),
        root15 * along_x * along_z,
        0.5 * root15 * (along_x * along_x - along_y * along_y),
    ]
    return jnp.stack(rows, axis=0)


def placed(coords_block):
    atoms = coords_block.shape[-1]
    planes = atoms // (SIDE * SIDE)
    slots = jnp.arange(27)
    steps_grid = jnp.stack([slots // 9 - 1, slots // 3 % 3 - 1, slots % 3 - 1], axis=1).astype(
        jnp.float32
    )
    extent = jnp.array([spacing * SIDE, spacing * SIDE, spacing * planes], jnp.float32)
    moved = coords_block + (steps_grid * extent[None, :])[:, :, None]
    return jnp.transpose(moved, (1, 0, 2)).reshape(3, 27 * atoms)


def edge_terms(coords_flat, species_flat, centre, neighbour, live_mask, w_two_in, w_two_hid, w_env):
    atoms = species_flat.shape[0] // 27
    own_coords = coords_flat[:, 13 * atoms : 14 * atoms]
    own_species = species_flat[13 * atoms : 14 * atoms]
    delta = jnp.take(coords_flat, neighbour, axis=1) - jnp.take(own_coords, centre, axis=1)
    radius = jnp.sqrt(jnp.sum(delta * delta, axis=0) + soften)
    weight_cut = envelope(radius / cutoff_radius) * live_mask
    orders = jnp.arange(1, NB + 1).astype(jnp.float32)[:, None]
    bessel = (
        math.sqrt(2.0 / cutoff_radius)
        * jnp.sin(orders * (math.pi / cutoff_radius) * radius[None, :])
        / radius[None, :]
    )
    kinds = jnp.arange(NS).astype(jnp.float32)[:, None]
    centre_kind = (jnp.take(own_species, centre)[None, :] == kinds).astype(jnp.float32)
    neighbour_kind = (jnp.take(species_flat, neighbour)[None, :] == kinds).astype(jnp.float32)
    features = jnp.concatenate(
        [bessel * weight_cut[None, :], centre_kind, neighbour_kind], axis=0
    ).astype(jnp.bfloat16)
    first_hidden = jax.nn.silu(
        jnp.dot(w_two_in, features, preferred_element_type=jnp.float32)
    ).astype(jnp.bfloat16)
    latent = (
        jax.nn.silu(jnp.dot(w_two_hid, first_hidden, preferred_element_type=jnp.float32))
        * weight_cut[None, :]
    ).astype(jnp.bfloat16)
    env_weight = jnp.dot(w_env, latent, preferred_element_type=jnp.float32)
    vectors = env_weight[:, None, :] * harmonics(delta / radius[None, :])[None, :, :]
    return (latent, vectors, weight_cut)


def pair_energy(latent, vectors, weight_cut, env_at, w_latent, w_out):
    product = env_at * vectors
    invariants = jnp.concatenate(
        [
            jnp.sum(product[:, 0:1], axis=1),
            jnp.sum(product[:, 1:4], axis=1),
            jnp.sum(product[:, 4:9], axis=1),
        ],
        axis=0,
    ).astype(jnp.bfloat16)
    joined = jnp.concatenate([latent, invariants], axis=0)
    update = (
        jax.nn.silu(jnp.dot(w_latent, joined, preferred_element_type=jnp.float32))
        * weight_cut[None, :]
    )
    updated = (latent.astype(jnp.float32) + update).astype(jnp.bfloat16)
    return jnp.sum(jnp.dot(w_out, updated, preferred_element_type=jnp.float32))


def block_energy(coords_block, species_block, centre, neighbour, count, weights):
    w_two_in, w_two_hid, w_env, w_latent, w_out = weights
    atoms = coords_block.shape[-1]
    channels = w_env.shape[0]
    width = w_two_hid.shape[0]
    coords_flat = placed(coords_block.reshape(27, 3, atoms))
    species_flat = species_block.reshape(27 * atoms)
    tiles = centre.shape[0] // TILE
    centre_tiles = centre.reshape(tiles, TILE)
    neighbour_tiles = neighbour.reshape(tiles, TILE)

    def collect_edges(env_sum, index):
        start = index * TILE

        def collect_active(operand):
            live_mask = (start + jnp.arange(TILE) < count).astype(jnp.float32)
            return edge_terms(
                coords_flat,
                species_flat,
                centre_tiles[index],
                neighbour_tiles[index],
                live_mask,
                w_two_in,
                w_two_hid,
                w_env,
            )

        def collect_resting(operand):
            return (
                jnp.zeros((width, TILE), jnp.bfloat16),
                jnp.zeros((channels, 9, TILE), jnp.float32),
                jnp.zeros((TILE,), jnp.float32),
            )

        latent, vectors, weight_cut = lax.cond(start < count, collect_active, collect_resting, 0)
        env_sum = env_sum + jax.ops.segment_sum(
            vectors.reshape(channels * 9, TILE).T, centre_tiles[index], num_segments=atoms
        )
        return (env_sum, (latent, vectors, weight_cut))

    env_sum, stored = lax.scan(
        collect_edges, jnp.zeros((atoms, channels * 9), jnp.float32), jnp.arange(tiles)
    )
    environment = env_norm * env_sum

    def tile_energy(total, index):

        def tile_active(operand):
            env_at = jnp.take(environment, centre_tiles[index], axis=0).T.reshape(channels, 9, TILE)
            return pair_energy(
                stored[0][index], stored[1][index], stored[2][index], env_at, w_latent, w_out
            )

        def tile_resting(operand):
            return jnp.zeros((), jnp.float32)

        return (total + lax.cond(index * TILE < count, tile_active, tile_resting, 0), None)

    total, unused = lax.scan(tile_energy, jnp.zeros((), jnp.float32), jnp.arange(tiles))
    return total


def energy_and_grad(frame_block, centre, neighbour, count, weights):
    species_block = frame_block[:, :, :, 3, :]

    def energy_of(coords_block):
        return block_energy(coords_block, species_block, centre, neighbour, count, weights)

    energy_part, backward = jax.vjp(energy_of, frame_block[:, :, :, 0:3, :])
    return (energy_part, backward(jnp.ones((), jnp.float32))[0])


def body(coords, species, pair_ids, live_counts, w_two_in, w_two_hid, w_env, w_latent, w_out):
    weights = (w_two_in, w_two_hid, w_env, w_latent, w_out)
    atoms = coords.shape[-1]
    half_slots = pair_ids.shape[-1] // 2
    frame = jnp.concatenate([coords, species.astype(jnp.float32)[:, :, :, None, :]], axis=3)
    frame_ext = extended(frame, (("gx", 0), ("gy", 1), ("gz", 2)), 1)
    ids = pair_ids[0, 0, 0]
    counts = live_counts[0, 0, 0]
    first_energy, first_grad = energy_and_grad(
        frame_ext, ids[0, :half_slots], ids[1, :half_slots], counts[0], weights
    )
    second_energy, second_grad = energy_and_grad(
        frame_ext, ids[0, half_slots:], ids[1, half_slots:], counts[1], weights
    )
    grad_ext = first_grad + second_grad
    returned = extended(grad_ext, (("gx", 0), ("gy", 1), ("gz", 2)), 1)
    picked = returned[0::2, 0::2, 0::2]
    forces = -jnp.sum(picked, axis=(0, 1, 2))[None, None, None]
    total = lax.psum(first_energy + second_energy, ("gx", "gy", "gz"))
    domains = lax.axis_size("gx") * lax.axis_size("gy") * lax.axis_size("gz")
    return (forces, total / (atoms * domains))


def solution(mesh):
    in_specs = (
        P("gx", "gy", "gz", None, None),
        P("gx", "gy", "gz", None),
        P("gx", "gy", "gz", None, None),
        P("gx", "gy", "gz", None),
        P(),
        P(),
        P(),
        P(),
        P(),
    )
    out_specs = (P("gx", "gy", "gz", None, None), P())
    return jax.shard_map(body, mesh=mesh, in_specs=in_specs, out_specs=out_specs, check_vma=False)
```

profile of v0, /device:TPU:1, one launch (start us, length us, event | category | flops | bytes accessed | tf_op | source)
XLA Modules:
  0.0 313.4 jit_solution(1936935603437942184)
XLA Ops:
  5.3 5.9 %collective-permute-start.1 = (f32[1,1,1,4,128]{4,2,3,1,0:T(1,128)S(1)}, f32[1,1,1,4,128]{4,2,3,1,0:T(1,128)S(1)}, u32[]{:S(2)}, u32[]{:S(2)}) collective-permute-start(f32[1,1,1,4,128]{4,2,3,1,0:T(1,128)S(1)} %pad_maximum_fusion.5), channel_id=1, source_target_pairs={{64,0},{128,64},{192,128},{256,192},{320,256},{384,320},{448,384},... | collective-permute-start | bytes 6152 | tf_op jit(solution)/shard_map/ppermute | solution.py:29
  11.2 1.9 collective-permute-start
  15.1 1.6 collective-permute-done
  17.4 5.9 %collective-permute-start.3 = (f32[3,1,1,4,128]{4,2,3,1,0:T(1,128)S(1)}, f32[3,1,1,4,128]{4,2,3,1,0:T(1,128)S(1)}, u32[]{:S(2)}, u32[]{:S(2)}) collective-permute-start(f32[3,1,1,4,128]{4,2,3,1,0:T(1,128)S(1)} %pad_maximum_fusion.4), channel_id=1, source_target_pairs={{8,0},{16,8},{24,16},{32,24},{40,32},{48,40},{56,48},{0,56},{9,1},... | collective-permute-start | bytes 18440 | tf_op jit(solution)/shard_map/ppermute | solution.py:29
  23.3 2.0 collective-permute-start.2
  25.9 2.1 collective-permute-done.2
  28.7 10.1 %collective-permute-start.5 = (f32[3,3,1,4,128]{4,2,3,1,0:T(1,128)S(1)}, f32[3,3,1,4,128]{4,2,3,1,0:T(1,128)S(1)}, u32[]{:S(2)}, u32[]{:S(2)}) collective-permute-start(f32[3,3,1,4,128]{4,2,3,1,0:T(1,128)S(1)} %pad_maximum_fusion.3), channel_id=1, source_target_pairs={{1,0},{2,1},{3,2},{4,3},{5,4},{6,5},{7,6},{0,7},{9,8},{10,9},{11,1... | collective-permute-start | bytes 55304 | tf_op jit(solution)/shard_map/ppermute | solution.py:29
  38.8 1.9 collective-permute-start.4
  43.5 6.0 %collective-permute-done.4 = f32[3,3,1,4,128]{4,2,3,1,0:T(1,128)S(1)} collective-permute-done((f32[3,3,1,4,128]{4,2,3,1,0:T(1,128)S(1)}, f32[3,3,1,4,128]{4,2,3,1,0:T(1,128)S(1)}, u32[]{:S(2)}, u32[]{:S(2)}) %collective-permute-start.4) | collective-permute-done | bytes 18464 | tf_op jit(solution)/shard_map/ppermute | solution.py:27
  52.2 21.5 %conditional.8 = (f32[64,9,128]{2,1,0:T(8,128)S(1)}, f32[128]{0:T(128)S(1)}, s32[128,1]{0,1:T(1,128)S(1)}, s32[128,1]{0,1:T(1,128)S(1)}, f32[3,128]{1,0:T(4,128)...) conditional(s32[]{:T(128)} %convert_element_type.294, ...), branch_computations={%region_0.1_spmd, %region_1.7_spmd} | conditional | flops 78289456 | bytes 5745920 | solution.py:156
  54.9 2.1 gather_fusion
  61.7 2.1 convolution_bitcast_fusion
  63.7 1.9 fusion.109
  65.6 1.8 fusion.110
  71.4 1.7 subtract_multiply_fusion
  76.2 10.7 %conditional.9 = (f32[]{:T(128)}, s32[128,1]{0,1:T(1,128)S(1)}, f32[64,9,128]{0,2,1:T(8,128)S(1)}, f32[64,9,128]{2,1,0:T(8,128)S(1)}, bf16[512,704]{1,0:T(8,128)...) conditional(s32[]{:T(128)} %convert_element_type.294, ...), branch_computations={%region_4.9_spmd, %region_5.14_spmd} | conditional | flops 94054272 | bytes 14679044 | solution.py:178
  81.4 1.9 mul.1567
  83.3 1.8 fusion.111
  87.0 13.3 %conditional.10 = (f32[128,576]{1,0:T(8,128)S(1)}, bf16[512,128]{1,0:T(8,128)(2,1)}, f32[64,9,128]{2,0,1:T(8,128)}, f32[128]{0:T(128)}) conditional(s32[]{:T(128)} %convert_element_type.294, () %tuple.180, (bf16[1,512]{1,0:T(2,128)(2,1)S(1)}, f32[1,128]{1,0:T(1,128)S(1)}, f32[512,128]{0,1:T(8,128)}, f32[512,128]{0,1:T(8,128)}, ...), branch_computations={%region_9.15_spmd, %region_10.18_spmd} | conditional | flops 93282688 | bytes 10592002 | solution.py:178
  92.2 1.7 fusion.154
  96.0 1.6 scatter_custom_fusion
  100.3 24.9 %conditional.12 = (f32[64,9,128]{2,1,0:T(8,128)S(1)}, f32[128]{0:T(128)S(1)}, s32[128,1]{0,1:T(1,128)}, s32[128,1]{0,1:T(1,128)}, f32[3,128]{1,0:T(4,128)}, /*in...) conditional(s32[]{:T(128)} %convert_element_type.297, ...), branch_computations={%region_24.30_spmd, %region_25.32_spmd} | conditional | flops 78289456 | bytes 4336672 | solution.py:156
  104.3 2.1 gather_fusion.5
  113.3 1.7 subtract_multiply_fusion.5
  115.1 2.1 convolution_bitcast_fusion.4
  117.1 1.8 fusion.139
  119.0 1.8 fusion.140
  127.6 1.6 scatter_custom_fusion.7
  129.2 11.4 %conditional.13 = (f32[]{:T(128)}, s32[128,1]{0,1:T(1,128)S(1)}, f32[64,9,128]{0,2,1:T(8,128)S(1)}, f32[64,9,128]{2,1,0:T(8,128)S(1)}, bf16[512,704]{1,0:T(8,128...) conditional(s32[]{:T(128)} %convert_element_type.297, ...), branch_computations={%region_28.34_spmd, %region_29.38_spmd} | conditional | flops 94054272 | bytes 20450420 | solution.py:178
  134.0 1.9 mul.1716
  135.9 1.8 fusion.141
  137.7 2.3 copy.425
  140.5 9.1 %conditional.14 = (f32[128,576]{1,0:T(8,128)S(1)}, bf16[512,128]{1,0:T(8,128)(2,1)S(1)}, f32[64,9,128]{2,0,1:T(8,128)S(1)}, f32[128]{0:T(128)S(1)}) conditional(s32[]{:T(128)} %convert_element_type.297, () %tuple.188, (bf16[1,512]{1,0:T(2,128)(2,1)}, f32[1,128]{1,0:T(1,128)S(1)}, f32[512,128]{0,1:T(8,128)}, f32[512,128]{0,1:T(8,128)}, ...), branch_computations={%region_33.39_spmd, %region_34.42_spmd} | conditional | flops 93282688 | bytes 9125466 | solution.py:178
  144.1 1.7 fusion.164
  146.6 1.6 scatter_custom_fusion.3
  151.1 14.3 %conditional.11 = (f32[3,3456]{0,1:T(8,128)}) conditional(s32[]{:T(128)} %convert_element_type.294, () %tuple.177, (f32[64,1,128]{2,0,1:T(8,128)}, s32[1,128]{1,0:T(1,128)S(1)}, s32[128]{0:T(128)S(1)}, f32[576,128]{0,1:T(8,128)S(1)}, f32[576,128]{1,0:T(8,128)S(1)}, /*index=5*/f32[64,9,128]{2,0,1:T(8,128)}, f32[128]{0:T(128)S(1)}, ...), branch_computations={%region_13.19_spmd, %region_14.29_spmd} | conditional | flops 78513664 | bytes 6192620 | solution.py:156
  154.9 1.9 fusion.5
  161.6 3.8 %scatter_fusion = f32[3,3456]{0,1:T(8,128)} fusion(f32[3,3456]{0,1:T(8,128)} %pad.48, s32[128]{0:T(128)S(1)} %bitcast.380, f32[128,3]{1,0:T(8,128)S(1)} %copy.394), kind=kCustom, calls=%fused_computation.14 | custom fusion | flops 384 | bytes 5120 | tf_op jit(solution)/shard_map/transpose(jvp())/while/body/eval_jaxpr/cond/branch_1_fun/jit(_take)/scatter-add | solution.py:76
  167.0 13.2 %conditional.15 = (f32[3,3456]{0,1:T(8,128)}) conditional(s32[]{:T(128)} %convert_element_type.297, () %tuple.185, (f32[64,1,128]{2,0,1:T(8,128)}, s32[1,128]{1,0:T(1,128)S(1)}, s32[128]{0:T(128)S(1)}, f32[576,128]{0,1:T(8,128)S(1)}, f32[576,128]{1,0:T(8,128)S(1)}, /*index=5*/f32[64,9,128]{2,0,1:T(8,128)S(1)}, f32[128]{0:T(128)S(1)}, ...), branch_computations={%region_37.43_spmd, %region_38.53_spmd} | conditional | flops 78513664 | bytes 6192620 | solution.py:156
  176.1 4.0 %scatter_fusion.1 = f32[3,3456]{0,1:T(8,128)} fusion(f32[3,3456]{0,1:T(8,128)} %pad.55, s32[128]{0:T(128)} %bitcast.110, f32[128,3]{1,0:T(8,128)S(1)} %copy.398), kind=kCustom, calls=%fused_computation.17 | custom fusion | flops 384 | bytes 5120 | tf_op jit(solution)/shard_map/transpose(jvp())/while/body/eval_jaxpr/cond/branch_1_fun/jit(_take)/scatter-add | solution.py:76
  180.1 2.2 add.479
  183.0 1.9 collective-permute-start.6
  185.0 4.6 %collective-permute-start.7 = (f32[1,3,3,3,128]{4,0,3,2,1:T(1,128)S(1)}, f32[1,3,3,3,128]{4,0,3,2,1:T(1,128)S(1)}, u32[]{:S(2)}, u32[]{:S(2)}) collective-permute-start(f32[1,3,3,3,128]{4,0,3,2,1:T(1,128)S(1)} %copy.455), channel_id=1, source_target_pairs={{64,0},{128,64},{192,128},{256,192},{320,256},{384,320},{448,384},... | collective-permute-start | bytes 41480 | tf_op jit(solution)/shard_map/ppermute | solution.py:29
  190.5 8.5 %collective-permute-start.9 = (f32[5,1,3,3,128]{4,1,3,2,0:T(1,128)S(1)}, f32[5,1,3,3,128]{4,1,3,2,0:T(1,128)S(1)}, u32[]{:S(2)}, u32[]{:S(2)}) collective-permute-start(f32[5,1,3,3,128]{4,1,3,2,0:T(1,128)S(1)} %copy.442), channel_id=1, source_target_pairs={{8,0},{16,8},{24,16},{32,24},{40,32},{48,40},{56,48},{0,56},{9,1},... | collective-permute-start | bytes 69128 | tf_op jit(solution)/shard_map/ppermute | solution.py:29
  199.0 1.9 collective-permute-start.8
  202.3 2.7 collective-permute-start.11
  205.0 6.5 %collective-permute-start.10 = (f32[5,5,1,3,128]{4,2,3,1,0:T(1,128)S(1)}, f32[5,5,1,3,128]{4,2,3,1,0:T(1,128)S(1)}, u32[]{:S(2)}, u32[]{:S(2)}) collective-permute-start(f32[5,5,1,3,128]{4,2,3,1,0:T(1,128)S(1)} %copy.445), channel_id=1, source_target_pairs={{0,1},{1,2},{2,3},{3,4},{4,5},{5,6},{6,7},{7,0},{8,9},{9,10},{10,1... | collective-permute-start | bytes 115208 | tf_op jit(solution)/shard_map/ppermute | solution.py:27
  211.5 99.1 %psum.7 = f32[]{:T(128)} all-reduce(f32[]{:T(128)S(6)} %add.483), channel_id=1, replica_groups=mesh['gx'=8,'gy'=8,'gz'=8] {'gx','gy','gz'}, use_global_device_ids=true, to_apply=%region_49.55 | all-reduce | flops 1 | bytes 8 | tf_op jit(solution)/shard_map/psum | solution.py:212
  (495 shorter events, 94.0 us)
Async XLA Ops:
  1.3 49.7 %copy-start.21 = (bf16[512,12]{0,1:T(8,128)(2,1)}, bf16[512,12]{0,1:T(8,128)(2,1)S(1)}, u32[]{:S(2)}) copy-start(bf16[512,12]{0,1:T(8,128)(2,1)S(1)} %copy.691) | copy-start | bytes 36868
  3.9 72.3 %copy-start.27 = (bf16[1,512]{1,0:T(2,128)(2,1)}, bf16[1,512]{1,0:T(2,128)(2,1)S(1)}, u32[]{:S(2)}) copy-start(bf16[1,512]{1,0:T(2,128)(2,1)S(1)} %copy.694) | copy-start | bytes 3076
  5.3 9.8 %collective-permute-start.1 = (f32[1,1,1,4,128]{4,2,3,1,0:T(1,128)S(1)}, f32[1,1,1,4,128]{4,2,3,1,0:T(1,128)S(1)}, u32[]{:S(2)}, u32[]{:S(2)}) collective-permute-start(f32[1,1,1,4,128]{4,2,3,1,0:T(1,128)S(1)} %pad_maximum_fusion.5), channel_id=1, source_target_pairs={{64,0},{128,64},{192,128},{256,192},{320,256},{384,320},{448,384},... | collective-permute-start | bytes 6152 | tf_op jit(solution)/shard_map/ppermute | solution.py:29
  11.2 5.5 %collective-permute-start = (f32[1,1,1,4,128]{4,2,3,1,0:T(1,128)S(1)}, f32[1,1,1,4,128]{4,2,3,1,0:T(1,128)S(1)}, u32[]{:S(2)}, u32[]{:S(2)}) collective-permute-start(f32[1,1,1,4,128]{4,2,3,1,0:T(1,128)S(1)} %pad_maximum_fusion.5), channel_id=1, source_target_pairs={{0,64},{64,128},{128,192},{192,256},{256,320},{320,384},{384,448},... | collective-permute-start | bytes 6152 | tf_op jit(solution)/shard_map/ppermute | solution.py:27
  15.1 27.6 %copy-start.66 = (s32[128]{0:T(128)}, s32[128]{0:T(128)S(1)}, u32[]{:S(2)}) copy-start(s32[128]{0:T(128)S(1)} %get-tuple-element.3570) | copy-start | bytes 1540
  15.1 61.1 %copy-start.68 = (s32[1,128]{1,0:T(1,128)}, s32[1,128]{1,0:T(1,128)S(1)}, u32[]{:S(2)}) copy-start(s32[1,128]{1,0:T(1,128)S(1)} %get-tuple-element.3573) | copy-start | bytes 1540
  17.4 8.5 %collective-permute-start.3 = (f32[3,1,1,4,128]{4,2,3,1,0:T(1,128)S(1)}, f32[3,1,1,4,128]{4,2,3,1,0:T(1,128)S(1)}, u32[]{:S(2)}, u32[]{:S(2)}) collective-permute-start(f32[3,1,1,4,128]{4,2,3,1,0:T(1,128)S(1)} %pad_maximum_fusion.4), channel_id=1, source_target_pairs={{8,0},{16,8},{24,16},{32,24},{40,32},{48,40},{56,48},{0,56},{9,1},... | collective-permute-start | bytes 18440 | tf_op jit(solution)/shard_map/ppermute | solution.py:29
  23.3 4.6 %collective-permute-start.2 = (f32[3,1,1,4,128]{4,2,3,1,0:T(1,128)S(1)}, f32[3,1,1,4,128]{4,2,3,1,0:T(1,128)S(1)}, u32[]{:S(2)}, u32[]{:S(2)}) collective-permute-start(f32[3,1,1,4,128]{4,2,3,1,0:T(1,128)S(1)} %pad_maximum_fusion.4), channel_id=1, source_target_pairs={{0,8},{8,16},{16,24},{24,32},{32,40},{40,48},{48,56},{56,0},{1,9},... | collective-permute-start | bytes 18440 | tf_op jit(solution)/shard_map/ppermute | solution.py:27
  28.7 14.8 %collective-permute-start.5 = (f32[3,3,1,4,128]{4,2,3,1,0:T(1,128)S(1)}, f32[3,3,1,4,128]{4,2,3,1,0:T(1,128)S(1)}, u32[]{:S(2)}, u32[]{:S(2)}) collective-permute-start(f32[3,3,1,4,128]{4,2,3,1,0:T(1,128)S(1)} %pad_maximum_fusion.3), channel_id=1, source_target_pairs={{1,0},{2,1},{3,2},{4,3},{5,4},{6,5},{7,6},{0,7},{9,8},{10,9},{11,1... | collective-permute-start | bytes 55304 | tf_op jit(solution)/shard_map/ppermute | solution.py:29
  38.8 10.6 %collective-permute-start.4 = (f32[3,3,1,4,128]{4,2,3,1,0:T(1,128)S(1)}, f32[3,3,1,4,128]{4,2,3,1,0:T(1,128)S(1)}, u32[]{:S(2)}, u32[]{:S(2)}) collective-permute-start(f32[3,3,1,4,128]{4,2,3,1,0:T(1,128)S(1)} %pad_maximum_fusion.3), channel_id=1, source_target_pairs={{0,1},{1,2},{2,3},{3,4},{4,5},{5,6},{6,7},{7,0},{8,9},{9,10},{10,1... | collective-permute-start | bytes 55304 | tf_op jit(solution)/shard_map/ppermute | solution.py:27
  54.2 9.5 %copy-start.58 = (s32[128]{0:T(128)}, s32[128]{0:T(128)S(1)}, u32[]{:S(2)}) copy-start(s32[128]{0:T(128)S(1)} %get-tuple-element.3538) | copy-start | bytes 1540 | tf_op jit(solution)/shard_map/jvp()/while/body/eval_jaxpr/cond
  54.2 9.5 %copy-start.84 = (s32[128]{0:T(128)}, s32[128]{0:T(128)S(1)}, u32[]{:S(2)}) copy-start(s32[128]{0:T(128)S(1)} %get-tuple-element.3465) | copy-start | bytes 1540 | tf_op jit(solution)/shard_map/jvp()/while/body/eval_jaxpr/cond
  57.2 6.6 %copy-start.29 = (f32[3,128]{1,0:T(4,128)}, f32[3,128]{1,0:T(4,128)S(1)}, u32[]{:S(2)}) copy-start(f32[3,128]{1,0:T(4,128)S(1)} %get-tuple-element.3620) | copy-start | bytes 4612 | tf_op jit(solution)/shard_map/jvp()/while/body/eval_jaxpr/cond
  57.9 9.5 %copy-start.23 = (f32[9,128]{1,0:T(8,128)}, f32[9,128]{1,0:T(8,128)S(1)}, u32[]{:S(2)}) copy-start(f32[9,128]{1,0:T(8,128)S(1)} %stack.9) | copy-start | bytes 13828 | tf_op jit(solution)/shard_map/jvp()/while/body/eval_jaxpr/cond
  65.6 8.1 %copy-start.30 = (f32[3,128]{1,0:T(4,128)S(1)}, f32[3,128]{1,0:T(4,128)}, u32[]{:S(2)}) copy-start(f32[3,128]{1,0:T(4,128)} %copy-done.29) | copy-start | bytes 4612 | tf_op jit(solution)/shard_map/jvp()/while/body/eval_jaxpr/cond
  65.6 8.1 %copy-start.59 = (s32[128]{0:T(128)S(1)}, s32[128]{0:T(128)}, u32[]{:S(2)}) copy-start(s32[128]{0:T(128)} %copy-done.58) | copy-start | bytes 1540 | tf_op jit(solution)/shard_map/jvp()/while/body/eval_jaxpr/cond
  65.6 8.1 %copy-start.85 = (s32[128]{0:T(128)S(1)}, s32[128]{0:T(128)}, u32[]{:S(2)}) copy-start(s32[128]{0:T(128)} %copy-done.84) | copy-start | bytes 1540 | tf_op jit(solution)/shard_map/jvp()/while/body/eval_jaxpr/cond
  73.9 2.3 copy-start.56
  73.9 2.3 copy-start.60
  74.0 2.2 copy-start.8
  77.5 2.7 copy-start.6
  78.8 2.6 copy-start.2
  81.4 4.9 %copy-start.7 = (f32[64,9,128]{2,1,0:T(8,128)S(1)}, f32[64,9,128]{2,1,0:T(8,128)}, u32[]{:S(2)}) copy-start(f32[64,9,128]{2,1,0:T(8,128)} %copy-done.6) | copy-start | bytes 884740 | tf_op jit(solution)/shard_map/jvp()/while/body/eval_jaxpr/cond
  81.4 4.9 %copy-start.91 = (s32[128]{0:T(128)S(1)}, s32[128]{0:T(128)}, u32[]{:S(2)}) copy-start(s32[128]{0:T(128)} %copy-done.90) | copy-start | bytes 1540 | tf_op jit(solution)/shard_map/jvp()/while/body/eval_jaxpr/cond
  81.4 4.9 %copy-start.3 = (f32[64,9,128]{0,2,1:T(8,128)S(1)}, f32[64,9,128]{0,2,1:T(8,128)}, u32[]{:S(2)}) copy-start(f32[64,9,128]{0,2,1:T(8,128)} %copy-done.2) | copy-start | bytes 884740 | tf_op jit(solution)/shard_map/jvp()/while/body/eval_jaxpr/cond
  87.0 2.2 copy-start.52
  87.0 2.2 copy-start.83
  87.0 2.2 copy-start.92
  92.2 1.8 copy-start.33
  94.8 2.9 copy-start.20
  94.8 2.9 copy-start.51
  95.7 3.9 %copy-start.34 = (f32[512]{0:T(512)S(1)}, f32[512]{0:T(512)}, u32[]{:S(2)}) copy-start(f32[512]{0:T(512)} %copy-done.33) | copy-start | bytes 6148 | tf_op jit(solution)/shard_map/transpose(jvp())/while/body/eval_jaxpr/cond
  126.8 2.4 copy-start.13
  129.2 1.5 copy-start.9
  131.5 2.5 copy-start
  131.6 1.3 copy-start.10
  131.9 4.0 %copy-start.28 = (bf16[1,512]{1,0:T(2,128)(2,1)S(1)}, bf16[1,512]{1,0:T(2,128)(2,1)}, u32[]{:S(2)}) copy-start(bf16[1,512]{1,0:T(2,128)(2,1)} %get-tuple-element.3775) | copy-start | bytes 3076 | tf_op jit(solution)/shard_map/jvp()/while/body/eval_jaxpr/cond
  131.9 4.0 %copy-start.55 = (f32[1,128]{1,0:T(1,128)S(1)}, f32[1,128]{1,0:T(1,128)}, u32[]{:S(2)}) copy-start(f32[1,128]{1,0:T(1,128)} %get-tuple-element.3773) | copy-start | bytes 1540 | tf_op jit(solution)/shard_map/jvp()/while/body/eval_jaxpr/cond
  134.0 5.9 %copy-start.5 = (f32[64,9,128]{2,1,0:T(8,128)S(1)}, f32[64,9,128]{2,1,0:T(8,128)}, u32[]{:S(2)}) copy-start(f32[64,9,128]{2,1,0:T(8,128)} %copy-done.4) | copy-start | bytes 884740 | tf_op jit(solution)/shard_map/jvp()/while/body/eval_jaxpr/cond
  134.0 5.9 %copy-start.1 = (f32[64,9,128]{0,2,1:T(8,128)S(1)}, f32[64,9,128]{0,2,1:T(8,128)}, u32[]{:S(2)}) copy-start(f32[64,9,128]{0,2,1:T(8,128)} %copy-done) | copy-start | bytes 884740 | tf_op jit(solution)/shard_map/jvp()/while/body/eval_jaxpr/cond
  134.0 5.9 %copy-start.88 = (s32[128]{0:T(128)S(1)}, s32[128]{0:T(128)}, u32[]{:S(2)}) copy-start(s32[128]{0:T(128)} %copy-done.87) | copy-start | bytes 1540 | tf_op jit(solution)/shard_map/jvp()/while/body/eval_jaxpr/cond
  140.6 5.2 %copy-start.89 = (s32[128,1]{0,1:T(1,128)}, s32[128,1]{0,1:T(1,128)S(1)}, u32[]{:S(2)}) copy-start(s32[128,1]{0,1:T(1,128)S(1)} %get-tuple-element.2201) | copy-start | bytes 1540 | tf_op jit(solution)/shard_map/transpose(jvp())/while/body/eval_jaxpr/cond
  183.0 6.6 %collective-permute-start.6 = (f32[1,3,3,3,128]{4,0,3,2,1:T(1,128)S(1)}, f32[1,3,3,3,128]{4,0,3,2,1:T(1,128)S(1)}, u32[]{:S(2)}, u32[]{:S(2)}) collective-permute-start(f32[1,3,3,3,128]{4,0,3,2,1:T(1,128)S(1)} %copy.454), channel_id=1, source_target_pairs={{0,64},{64,128},{128,192},{192,256},{256,320},{320,384},{384,448},... | collective-permute-start | bytes 41480 | tf_op jit(solution)/shard_map/ppermute | solution.py:27
  185.0 5.4 %collective-permute-start.7 = (f32[1,3,3,3,128]{4,0,3,2,1:T(1,128)S(1)}, f32[1,3,3,3,128]{4,0,3,2,1:T(1,128)S(1)}, u32[]{:S(2)}, u32[]{:S(2)}) collective-permute-start(f32[1,3,3,3,128]{4,0,3,2,1:T(1,128)S(1)} %copy.455), channel_id=1, source_target_pairs={{64,0},{128,64},{192,128},{256,192},{320,256},{384,320},{448,384},... | collective-permute-start | bytes 41480 | tf_op jit(solution)/shard_map/ppermute | solution.py:29
  190.5 10.5 %collective-permute-start.9 = (f32[5,1,3,3,128]{4,1,3,2,0:T(1,128)S(1)}, f32[5,1,3,3,128]{4,1,3,2,0:T(1,128)S(1)}, u32[]{:S(2)}, u32[]{:S(2)}) collective-permute-start(f32[5,1,3,3,128]{4,1,3,2,0:T(1,128)S(1)} %copy.442), channel_id=1, source_target_pairs={{8,0},{16,8},{24,16},{32,24},{40,32},{48,40},{56,48},{0,56},{9,1},... | collective-permute-start | bytes 69128 | tf_op jit(solution)/shard_map/ppermute | solution.py:29
  199.0 3.1 collective-permute-start.8
  202.3 109.0 %collective-permute-start.11 = (f32[5,5,1,3,128]{4,2,3,1,0:T(1,128)S(1)}, f32[5,5,1,3,128]{4,2,3,1,0:T(1,128)S(1)}, u32[]{:S(2)}, u32[]{:S(2)}) collective-permute-start(f32[5,5,1,3,128]{4,2,3,1,0:T(1,128)S(1)} %copy.446), channel_id=1, source_target_pairs={{1,0},{2,1},{3,2},{4,3},{5,4},{6,5},{7,6},{0,7},{9,8},{10,9},{11,1... | collective-permute-start | bytes 115208 | tf_op jit(solution)/shard_map/ppermute | solution.py:29
  205.0 106.4 %collective-permute-start.10 = (f32[5,5,1,3,128]{4,2,3,1,0:T(1,128)S(1)}, f32[5,5,1,3,128]{4,2,3,1,0:T(1,128)S(1)}, u32[]{:S(2)}, u32[]{:S(2)}) collective-permute-start(f32[5,5,1,3,128]{4,2,3,1,0:T(1,128)S(1)} %copy.445), channel_id=1, source_target_pairs={{0,1},{1,2},{2,3},{3,4},{4,5},{5,6},{6,7},{7,0},{8,9},{9,10},{10,1... | collective-permute-start | bytes 115208 | tf_op jit(solution)/shard_map/ppermute | solution.py:27
  (95 other events, 90.8 us)
where the time goes:
time: 316 us; the launch traced here: 313 us
  blocking collectives  99.1 us (31%)
  other arithmetic  61.9 us (20%)
  starting transfers between devices  53.9 us (17%)
  local copies, waits for them, and re-layouts  53.2 us (17%)
  matrix products  25.9 us (8%)
  waiting for transfers between devices  11.6 us (4%)
  between operations  5.48 us (2%)
    psum x1, blocking collectives, body(): total = lax.psum(first_energy + second_energy, ('gx', 'gy', 'gz'))  99.1 us
    ppermute x6, starting transfers between devices, extended(): lax.ppermute(head, axis, [((i + 1) % count, i) for i in range(count)])  37.8 us
    ppermute x6, starting transfers between devices, extended(): lax.ppermute(tail, axis, [(i, (i + 1) % count) for i in range(count)])  16.2 us
    another operation x25, local copies, waits for them, and re-layouts  13.7 us
    ppermute x6, waiting for transfers between devices, extended(): lax.ppermute(tail, axis, [(i, (i + 1) % count) for i in range(count)])  10.8 us
    unnamed x202, local copies, waits for them, and re-layouts  7.87 us
    scatter-add x2, other arithmetic, edge_terms(): jnp.take(coords_flat, neighbour, axis=1)  7.8 us
    dot_general x4, matrix products, edge_terms(): jnp.dot(w_two_in, features, preferred_element_type=jnp.float32)  6.37 us
  transfers between devices with their start and end apart: 12, of which 5 were waited for; matrix products, arithmetic and copies ran while one was open for 1% of the time, Pallas kernels for 0%

commit v1 on v0

v1 whole, which is shorter than its diff:
```python
import math

import jax
import jax.numpy as jnp
from jax import lax
from jax.experimental import pallas as pl
from jax.experimental.pallas import tpu as pltpu
from jax.sharding import PartitionSpec as P

F32 = jnp.float32
BF16 = jnp.bfloat16
CUTOFF = 6.0
SOFTEN = 0.01
ENV_NORM = 0.25
EXTENT = (16.0, 16.0, 4.0)
ROOT3 = math.sqrt(3.0)
ROOT5 = math.sqrt(5.0)
ROOT15 = math.sqrt(15.0)
DEGREE = (0, 1, 1, 1, 2, 2, 2, 2, 2)
RING = 8
LAT = 512
CH = 64
PAIRS = 256
ATOMS = 128
ROWS = 64
ENERGY_ROW = 27


def column_sum(block):
    return jnp.sum(block, axis=0, keepdims=True)


def folded(block):
    return jnp.sum(block.reshape(block.shape[0] // 8, 8, block.shape[1]), axis=0)


def silu_parts(z):
    gate = 0.5 * jnp.tanh(0.5 * z) + 0.5
    value = z * gate
    return value, gate + value * (1.0 - gate)


def split_dot(block, square):
    high = block.astype(BF16)
    low = (block - high.astype(F32)).astype(BF16)
    return jnp.dot(high, square, preferred_element_type=F32) + jnp.dot(
        low, square, preferred_element_type=F32
    )


def split_dot_nt(block, other):
    dims = (((1,), (1,)), ((), ()))
    high = block.astype(BF16)
    low = (block - high.astype(F32)).astype(BF16)
    return lax.dot_general(high, other, dims, preferred_element_type=F32) + lax.dot_general(
        low, other, dims, preferred_element_type=F32
    )


def force_kernel(
    place_ref,
    counts_ref,
    ids_ref,
    below_ref,
    level_ref,
    above_ref,
    same_ref,
    w_in_ref,
    w_in_t_ref,
    w_hid_ref,
    w_hid_t_ref,
    w_env_ref,
    w_env_t_ref,
    w_lat_ref,
    w_lat_t_ref,
    w_out_ref,
    out_ref,
    z1_ref,
    z2_ref,
    z3_ref,
    hidden_ref,
    joined_ref,
    grad_ref,
    dz_ref,
    vec_ref,
    env_ref,
    dvec_ref,
    dlat_ref,
):
    centre = ids_ref[0:1, :]
    neighbour = ids_ref[1:2, :]
    slot = neighbour >> 7
    atom = neighbour & 127
    step_x = (slot * 57) >> 9
    rest = slot - 9 * step_x
    step_y = (rest * 11) >> 5
    step_z = rest - 3 * step_y

    near, own = [], []
    for half in range(2):
        lanes = slice(half * ATOMS, (half + 1) * ATOMS)
        pick = jnp.broadcast_to(atom[:, lanes], (4, ATOMS))
        slot_half = jnp.broadcast_to(slot[:, lanes], (4, ATOMS))
        total = jnp.zeros((4, ATOMS), F32)
        for at_y, slab in enumerate((below_ref, level_ref, above_ref)):
            for at_x in range(3):
                for at_z in range(3):
                    rows = jnp.take_along_axis(slab[at_x * 3 + at_z], pick, axis=1)
                    number = 9 * at_x + 3 * at_y + at_z
                    total = jnp.where(slot_half == number, rows, total)
        near.append(total)
        pick = jnp.broadcast_to(centre[:, lanes], (4, ATOMS))
        own.append(jnp.take_along_axis(level_ref[4], pick, axis=1))
    near = jnp.concatenate(near, axis=1)
    own = jnp.concatenate(own, axis=1)
    delta = [
        near[axis : axis + 1, :]
        + (step - 1).astype(F32) * EXTENT[axis]
        - own[axis : axis + 1, :]
        for axis, step in enumerate((step_x, step_y, step_z))
    ]

    lane = lax.broadcasted_iota(jnp.int32, (1, PAIRS), 1)
    half_live = jnp.where(lane < ATOMS, counts_ref[0], counts_ref[1] + ATOMS)
    live = jnp.where(lane < half_live, 1.0, 0.0)
    radius = jnp.sqrt(delta[0] * delta[0] + delta[1] * delta[1] + delta[2] * delta[2] + SOFTEN)
    inverse = 1.0 / radius
    ratio = radius * (1.0 / CUTOFF)
    inside = jnp.where(ratio < 1.0, live, 0.0)
    square = ratio * ratio
    fifth = square * square * ratio
    sixth = fifth * ratio
    cut = inside * (1.0 + sixth * (-28.0 + 48.0 * ratio - 21.0 * square))
    slope = inside * (-168.0 / CUTOFF) * fifth * (1.0 - ratio) * (1.0 - ratio)

    row8 = lax.broadcasted_iota(jnp.int32, (8, PAIRS), 0)
    order = (row8 + 1).astype(F32)
    turns = order * ratio
    whole = jnp.floor(turns + 0.5)
    sign = 1.0 - 2.0 * (whole.astype(jnp.int32) & 1).astype(F32)
    angle = (turns - whole) * math.pi
    angle2 = angle * angle
    sine = jnp.zeros_like(angle)
    for power in (11, 9, 7, 5, 3, 1):
        sine = sine * angle2 + (-1.0) ** (power // 2) / math.factorial(power)
    sine = sine * angle * sign
    cosine = jnp.zeros_like(angle)
    for power in (12, 10, 8, 6, 4, 2, 0):
        cosine = cosine * angle2 + (-1.0) ** (power // 2) / math.factorial(power)
    cosine = cosine * sign
    front = math.sqrt(2.0 / CUTOFF)
    bessel = front * sine * inverse
    bessel_slope = (front * math.pi / CUTOFF) * order * cosine * inverse - bessel * inverse

    kind_at = jnp.where(row8 < 2, own[3:4, :], near[3:4, :])
    kind = jnp.where((row8 < 4) & (kind_at == (row8 & 1).astype(F32)), 1.0, 0.0)
    features = jnp.concatenate([bessel * cut, kind], axis=0).astype(BF16)

    z1_ref[...] = jnp.dot(w_in_ref[...], features, preferred_element_type=F32)
    for start in range(0, LAT, ROWS):
        rows = pl.ds(start, ROWS)
        value, gate = silu_parts(z1_ref[rows, :])
        hidden_ref[rows, :] = value.astype(BF16)
        z1_ref[rows, :] = gate
    z2_ref[...] = jnp.dot(w_hid_ref[...], hidden_ref[...], preferred_element_type=F32)
    for start in range(0, LAT, ROWS):
        rows = pl.ds(start, ROWS)
        value, unused = silu_parts(z2_ref[rows, :])
        joined_ref[rows, :] = (value * cut).astype(BF16)

    unit = [part * inverse for part in delta]
    along_x, along_y, along_z = unit
    shapes = [
        None,
        ROOT3 * along_x,
        ROOT3 * along_y,
        ROOT3 * along_z,
        ROOT15 * along_x * along_y,
        ROOT15 * along_y * along_z,
        0.5 * ROOT5 * (2.0 * along_z * along_z - along_x * along_x - along_y * along_y),
        ROOT15 * along_x * along_z,
        0.5 * ROOT15 * (along_x * along_x - along_y * along_y),
    ]
    same = same_ref[...]
    weight = jnp.dot(w_env_ref[...], joined_ref[0:LAT, :], preferred_element_type=F32)
    for m in range(9):
        vec_ref[m * CH : (m + 1) * CH, :] = weight if m == 0 else weight * shapes[m]
    env_ref[...] = split_dot(vec_ref[...], same)
    for degree in range(3):
        total = None
        for m in range(9):
            if DEGREE[m] == degree:
                rows = slice(m * CH, (m + 1) * CH)
                term = env_ref[rows, :] * vec_ref[rows, :]
                total = term if total is None else total + term
        joined_ref[LAT + degree * CH : LAT + (degree + 1) * CH, :] = total.astype(BF16)

    z3_ref[...] = jnp.dot(w_lat_ref[...], joined_ref[...], preferred_element_type=F32)
    energy = jnp.zeros((8, PAIRS), F32)
    cut_grad = jnp.zeros((8, PAIRS), F32)
    for start in range(0, LAT, ROWS):
        rows = pl.ds(start, ROWS)
        value, gate = silu_parts(z3_ref[rows, :])
        readout = w_out_ref[rows, :].astype(F32)
        readout = jnp.concatenate([readout, readout], axis=1)
        updated = (joined_ref[rows, :].astype(F32) + value * cut).astype(BF16).astype(F32)
        energy = energy + folded(readout * updated)
        cut_grad = cut_grad + folded(readout * value)
        dz_ref[rows, :] = (readout * cut * gate).astype(BF16)

    grad_ref[...] = jnp.dot(w_lat_t_ref[...], dz_ref[...], preferred_element_type=F32)
    for m in range(9):
        rows = slice(m * CH, (m + 1) * CH)
        start = LAT + DEGREE[m] * CH
        dvec_ref[rows, :] = grad_ref[start : start + CH, :] * vec_ref[rows, :]
    dvec_ref[...] = split_dot(dvec_ref[...], same)
    weight_grad = None
    shape_grad = [None]
    for m in range(9):
        rows = slice(m * CH, (m + 1) * CH)
        start = LAT + DEGREE[m] * CH
        dvec = grad_ref[start : start + CH, :] * env_ref[rows, :] + dvec_ref[rows, :]
        if m == 0:
            weight_grad = dvec
        else:
            weight_grad = weight_grad + dvec * shapes[m]
            shape_grad.append(column_sum(dvec * weight))
    dlat_ref[...] = jnp.dot(
        w_env_t_ref[...], weight_grad.astype(BF16), preferred_element_type=F32
    )
    for start in range(0, LAT, ROWS):
        rows = pl.ds(start, ROWS)
        readout = w_out_ref[rows, :].astype(F32)
        readout = jnp.concatenate([readout, readout], axis=1)
        value, gate = silu_parts(z2_ref[rows, :])
        dlat = readout + grad_ref[rows, :] + dlat_ref[rows, :]
        cut_grad = cut_grad + folded(dlat * value)
        dz_ref[rows, :] = (dlat * cut * gate).astype(BF16)
    dlat_ref[...] = jnp.dot(w_hid_t_ref[...], dz_ref[...], preferred_element_type=F32)
    for start in range(0, LAT, ROWS):
        rows = pl.ds(start, ROWS)
        dz_ref[rows, :] = (dlat_ref[rows, :] * z1_ref[rows, :]).astype(BF16)
    feature_grad = jnp.dot(w_in_t_ref[...], dz_ref[...], preferred_element_type=F32)[0:8, :]

    cut_grad = column_sum(cut_grad + feature_grad * bessel)
    radius_grad = cut_grad * slope + cut * column_sum(feature_grad * bessel_slope)
    g1, g2, g3, g4, g5, g6, g7, g8 = shape_grad[1:]
    unit_grad = [
        ROOT3 * g1 + ROOT15 * (along_y * g4 + along_z * g7 + along_x * g8) - ROOT5 * along_x * g6,
        ROOT3 * g2 + ROOT15 * (along_x * g4 + along_z * g5 - along_y * g8) - ROOT5 * along_y * g6,
        ROOT3 * g3 + ROOT15 * (along_y * g5 + along_x * g7) + 2.0 * ROOT5 * along_z * g6,
    ]
    radial = sum(g * u for g, u in zip(unit_grad, unit))
    radius_grad = radius_grad - radial * inverse
    push = [g * inverse + radius_grad * u for g, u in zip(unit_grad, unit)]

    row = lax.broadcasted_iota(jnp.int32, (32, PAIRS), 0)
    cell = (row * 11) >> 5
    axis = row - 3 * cell
    cell_y = (cell * 11) >> 5
    wanted = 3 * cell_y + (cell - 3 * cell_y)
    moved = jnp.where(axis == 0, push[0], jnp.where(axis == 1, push[1], push[2]))
    moved = jnp.where(row < ENERGY_ROW, moved, 0.0)
    atom_row = lax.broadcasted_iota(jnp.int32, (ATOMS, PAIRS), 0)
    hit_near = jnp.where(atom_row == atom, 1.0, 0.0).astype(BF16)
    hit_own = jnp.where(atom_row == centre, 1.0, 0.0).astype(BF16)
    spread = jnp.concatenate(
        [jnp.where(slot == wanted + 9 * at_x, -moved, 0.0) for at_x in range(3)], axis=0
    )
    spread = split_dot_nt(spread, hit_near)
    home = split_dot_nt(jnp.where(cell == 4, moved, 0.0), hit_own)
    energy = column_sum(energy)
    energy = energy[:, 0:ATOMS] + energy[:, ATOMS:PAIRS]
    is_energy = lax.broadcasted_iota(jnp.int32, (32, ATOMS), 0) == ENERGY_ROW
    blank = jnp.where(is_energy, energy, 0.0)
    for peer in range(RING):
        out_ref[peer] = blank
    place = place_ref[0]
    for at_x in range(3):
        block = spread[32 * at_x : 32 * (at_x + 1), :]
        if at_x == 1:
            block = block + home
        out_ref[(place + (at_x + RING - 1)) & (RING - 1)] = jnp.where(is_energy, energy, block)


def both_sides(block, axis):
    up = [(i, (i + 1) % RING) for i in range(RING)]
    down = [((i + 1) % RING, i) for i in range(RING)]
    return lax.ppermute(block, axis, up), lax.ppermute(block, axis, down)


def addressed(total, axis, count):
    place = lax.axis_index(axis)
    peer = lax.broadcasted_iota(jnp.int32, (RING, 1, 1), 0)
    rows = jnp.zeros((RING, count, ATOMS), F32)
    for at in range(3):
        here = peer == (place + (at + RING - 1)) % RING
        rows = jnp.where(here, total[None, at * count : (at + 1) * count, :], rows)
    energies = jnp.broadcast_to(total[None, 3 * count : 3 * count + 1, :], (RING, 1, ATOMS))
    return jnp.concatenate([rows, energies], axis=1)


def body(coords, species, pair_ids, live_counts, w_two_in, w_two_hid, w_env, w_latent, w_out):
    ids = pair_ids[0, 0, 0]
    counts = live_counts[0, 0, 0]
    frame = jnp.concatenate([coords[0, 0, 0], species[0, 0, 0].astype(F32)[None]], axis=0)
    low, high = both_sides(frame, "gz")
    column = jnp.stack([low, frame, high], axis=0)
    low, high = both_sides(column, "gx")
    plane = jnp.concatenate([low, column, high], axis=0)
    below, above = both_sides(plane, "gy")

    same = jnp.where(ids[0][:, None] == ids[0][None, :], ENV_NORM, 0.0).astype(BF16)
    w_in = jnp.pad(w_two_in, ((0, 0), (0, 4)))
    readout = jnp.broadcast_to(w_out.reshape(LAT, 1), (LAT, ATOMS))
    place = lax.axis_index("gx").astype(jnp.int32).reshape(1)
    vmem = pl.BlockSpec(memory_space=pltpu.VMEM)
    smem = pl.BlockSpec(memory_space=pltpu.SMEM)
    sent = pl.pallas_call(
        force_kernel,
        out_shape=jax.ShapeDtypeStruct((RING, 32, ATOMS), F32),
        in_specs=[smem, smem] + [vmem] * 14,
        out_specs=vmem,
        scratch_shapes=[
            pltpu.VMEM((LAT, PAIRS), F32),
            pltpu.VMEM((LAT, PAIRS), F32),
            pltpu.VMEM((LAT, PAIRS), F32),
            pltpu.VMEM((LAT, PAIRS), BF16),
            pltpu.VMEM((LAT + 3 * CH, PAIRS), BF16),
            pltpu.VMEM((LAT + 3 * CH, PAIRS), F32),
            pltpu.VMEM((LAT, PAIRS), BF16),
            pltpu.VMEM((9 * CH, PAIRS), F32),
            pltpu.VMEM((9 * CH, PAIRS), F32),
            pltpu.VMEM((9 * CH, PAIRS), F32),
            pltpu.VMEM((LAT, PAIRS), F32),
        ],
        compiler_params=pltpu.CompilerParams(vmem_limit_bytes=24 * 1024 * 1024),
        name="forces_of_pairs",
    )(
        place,
        counts,
        ids,
        below,
        plane,
        above,
        same,
        w_in,
        w_in.T,
        w_two_hid,
        w_two_hid.T,
        w_env,
        w_env.T,
        w_latent,
        w_latent.T,
        readout,
    )
    total = jnp.sum(lax.all_to_all(sent, "gx", 0, 0), axis=0)
    total = jnp.sum(lax.all_to_all(addressed(total, "gy", 9), "gy", 0, 0), axis=0)
    total = jnp.sum(lax.all_to_all(addressed(total, "gz", 3), "gz", 0, 0), axis=0)
    forces = total[0:3].reshape(1, 1, 1, 3, ATOMS)
    return forces, jnp.sum(total[3]) * (1.0 / (ATOMS * RING**3))


def solution(mesh):
    in_specs = (
        P("gx", "gy", "gz", None, None),
        P("gx", "gy", "gz", None),
        P("gx", "gy", "gz", None, None),
        P("gx", "gy", "gz", None),
        P(),
        P(),
        P(),
        P(),
        P(),
    )
    out_specs = (P("gx", "gy", "gz", None, None), P())
    return jax.shard_map(body, mesh=mesh, in_specs=in_specs, out_specs=out_specs, check_vma=False)
```

time: 316 us -> 93.6 us (0.30)
  blocking collectives: 99.1 us -> 11.3 us
  other arithmetic: 61.9 us -> 2.32 us
  local copies, waits for them, and re-layouts: 53.2 us -> 3.83 us
  matrix products: 25.9 us -> 0 us
  waiting for transfers between devices: 11.6 us -> 22.6 us
  starting transfers between devices: 53.9 us -> 45.5 us
  Pallas kernels: 0 us -> 4.63 us
    psum x1 -> x0, blocking collectives: 99.1 us -> none  [body(): total = lax.psum(first_energy + second_energy, ('gx', 'gy', 'gz'))]
    dot_general x16 -> x0, matrix products: 25.9 us -> none  [the longest x4 6.37 us: edge_terms(): jnp.dot(w_two_in, features, preferred_element_type=jnp.float32)]
    ppermute x12 -> x6, starting transfers between devices: 53.9 us -> 31.1 us  [both_sides(): return (lax.ppermute(block, axis, up), lax.ppermute(block, axis, down))]
    scatter-add x8 -> x0, other arithmetic: 16.4 us -> none  [the longest x2 7.8 us: edge_terms(): jnp.take(coords_flat, neighbour, axis=1)]
    mul x29 -> x0, other arithmetic: 15.6 us -> none  [the longest x2 3.76 us: pair_energy(): jax.nn.silu(jnp.dot(w_latent, joined, preferred_element_type=jnp.float32))]
    another operation x28 -> x0, local copies, waits for them, and re-layouts: 14.9 us -> none
    all_to_all x0 -> x2, starting transfers between devices: none -> 14.4 us  [the longest x1 7.41 us: body(): lax.all_to_all(addressed(total, 'gy', 9), 'gy', 0, 0)]
    gather x16 -> x0, local copies, waits for them, and re-layouts: 14.2 us -> none  [the longest x4 4.38 us: edge_terms(): jnp.take(coords_flat, neighbour, axis=1)]
  transfers between devices with their start and end apart: 12 -> 8, of which waited for: 5 -> 5; matrix products, arithmetic and copies ran while one was open for 1% -> 2% of each run, Pallas kernels for 0% -> 0%
where the time goes in v1:
time: 93.6 us; the launch traced here: 93 us
  starting transfers between devices  45.5 us (49%)
  waiting for transfers between devices  22.6 us (24%)
  blocking collectives  11.3 us (12%)
  Pallas kernels  4.63 us (5%)
  local copies, waits for them, and re-layouts  3.83 us (4%)
  between operations  2.79 us (3%)
  other arithmetic  2.32 us (2%)
    ppermute x6, starting transfers between devices, both_sides(): return (lax.ppermute(block, axis, up), lax.ppermute(block, axis, down))  31.1 us
    all_to_all x1, blocking collectives, body(): lax.all_to_all(addressed(total, 'gz', 3), 'gz', 0, 0)  11.3 us
    ppermute x6, waiting for transfers between devices, both_sides(): return (lax.ppermute(block, axis, up), lax.ppermute(block, axis, down))  9.59 us
    all_to_all x1, waiting for transfers between devices, body(): total = jnp.sum(lax.all_to_all(sent, 'gx', 0, 0), axis=0)  7.95 us
    all_to_all x1, starting transfers between devices, body(): lax.all_to_all(addressed(total, 'gy', 9), 'gy', 0, 0)  7.41 us
    all_to_all x1, starting transfers between devices, body(): total = jnp.sum(lax.all_to_all(sent, 'gx', 0, 0), axis=0)  7.02 us
    all_to_all x1, waiting for transfers between devices, body(): lax.all_to_all(addressed(total, 'gy', 9), 'gy', 0, 0)  5.07 us
    pallas_call x1, Pallas kernels, body(): pl.pallas_call(force_kernel, out_shape=jax.ShapeDtypeStruct((RING, 32, AT...  4.63 us
  transfers between devices with their start and end apart: 8, of which 5 were waited for; matrix products, arithmetic and copies ran while one was open for 2% of the time, Pallas kernels for 0%

profile of v1, /device:TPU:1, one launch (start us, length us, event | category | flops | bytes accessed | tf_op | source)
XLA Modules:
  0.0 93.0 jit_solution(7271430524414612027)
XLA Ops:
  0.6 0.0 copy-start.7
  0.6 0.7 convert_bitcast_fusion
  1.3 0.0 copy-done.7
  1.3 13.7 %collective-permute-start.1 = (f32[4,128]{1,0:T(4,128)S(1)}, f32[4,128]{1,0:T(4,128)S(1)}, u32[]{:S(2)}, u32[]{:S(2)}) collective-permute-start(f32[4,128]{1,0:T(4,128)S(1)} %pad_maximum_fusion.3), channel_id=1, source_target_pairs={{1,0},{2,1},{3,2},{4,3},{5,4},{6,5},{7,6},{0,7},{9,8},{10,9},{11,1... | collective-permute-start | bytes 6152 | tf_op jit(solution)/shard_map/ppermute | solution.py:289
  15.0 1.9 %collective-permute-start = (f32[4,128]{1,0:T(4,128)S(1)}, f32[4,128]{1,0:T(4,128)S(1)}, u32[]{:S(2)}, u32[]{:S(2)}) collective-permute-start(f32[4,128]{1,0:T(4,128)S(1)} %pad_maximum_fusion.3), channel_id=1, source_target_pairs={{0,1},{1,2},{2,3},{3,4},{4,5},{5,6},{6,7},{7,0},{8,9},{9,10},{10,1... | collective-permute-start | bytes 6152 | tf_op jit(solution)/shard_map/ppermute | solution.py:289
  16.9 0.0 collective-permute-done.1
  16.9 8.4 %collective-permute-done = f32[4,128]{1,0:T(4,128)S(1)} collective-permute-done((f32[4,128]{1,0:T(4,128)S(1)}, f32[4,128]{1,0:T(4,128)S(1)}, u32[]{:S(2)}, u32[]{:S(2)}) %collective-permute-start) | collective-permute-done | bytes 2080 | tf_op jit(solution)/shard_map/ppermute | solution.py:289
  25.3 0.0 slice-start
  25.3 3.3 %collective-permute-start.2 = (f32[3,4,128]{2,1,0:T(4,128)S(1)}, f32[3,4,128]{2,1,0:T(4,128)S(1)}, u32[]{:S(2)}, u32[]{:S(2)}) collective-permute-start(f32[3,4,128]{2,1,0:T(4,128)S(1)} %pad_maximum_fusion.2), channel_id=1, source_target_pairs={{0,64},{64,128},{128,192},{192,256},{256,320},{320,384},{384,448},... | collective-permute-start | bytes 18440 | tf_op jit(solution)/shard_map/ppermute | solution.py:289
  28.7 0.0 slice-done
  28.7 0.1 select_convert_fusion.same_ref
  28.8 0.0 copy-start.5
  28.8 3.8 %collective-permute-start.3 = (f32[3,4,128]{2,1,0:T(4,128)S(1)}, f32[3,4,128]{2,1,0:T(4,128)S(1)}, u32[]{:S(2)}, u32[]{:S(2)}) collective-permute-start(f32[3,4,128]{2,1,0:T(4,128)S(1)} %pad_maximum_fusion.2), channel_id=1, source_target_pairs={{64,0},{128,64},{192,128},{256,192},{320,256},{384,320},{448,384},... | collective-permute-start | bytes 18440 | tf_op jit(solution)/shard_map/ppermute | solution.py:289
  32.6 0.0 collective-permute-done.2
  32.7 0.7 collective-permute-done.3
  33.4 0.0 copy-start
  33.4 6.4 %collective-permute-start.4 = (f32[9,4,128]{2,1,0:T(4,128)S(1)}, f32[9,4,128]{2,1,0:T(4,128)S(1)}, u32[]{:S(2)}, u32[]{:S(2)}) collective-permute-start(f32[9,4,128]{2,1,0:T(4,128)S(1)} %constant_dynamic-update-slice_fusion.level_ref), channel_id=1, source_target_pairs={{0,8},{8,16},{16,24},{24,32},{32,40},{40,48},{48,56},{56,0},{1,9},... | collective-permute-start | bytes 55304 | tf_op jit(solution)/shard_map/ppermute | solution.py:289
  39.8 1.9 %collective-permute-start.5 = (f32[9,4,128]{2,1,0:T(4,128)S(1)}, f32[9,4,128]{2,1,0:T(4,128)S(1)}, u32[]{:S(2)}, u32[]{:S(2)}) collective-permute-start(f32[9,4,128]{2,1,0:T(4,128)S(1)} %constant_dynamic-update-slice_fusion.level_ref), channel_id=1, source_target_pairs={{8,0},{16,8},{24,16},{32,24},{40,32},{48,40},{56,48},{0,56},{9,1},... | collective-permute-start | bytes 55304 | tf_op jit(solution)/shard_map/ppermute | solution.py:289
  41.8 0.0 copy-done.5
  41.8 0.2 copy.37
  42.0 0.0 copy-start.2
  42.0 1.3 %copy.20 = bf16[512,512]{0,1:T(8,128)(2,1)S(1)} copy(bf16[512,512]{1,0:T(8,128)(2,1)} %w_hid_ref.1) | data formatting | bytes 1048576 | tf_op args[5]
  43.3 0.0 copy-done.2
  43.3 0.1 copy.21
  43.4 0.0 copy-done
  43.4 0.0 copy-start.1
  43.4 0.3 copy.23.w_lat_ref
  43.7 0.0 copy-start.6
  43.8 0.6 copy-done.6
  44.4 0.0 collective-permute-done.4.below_ref
  44.4 0.5 collective-permute-done.5.above_ref
  44.9 0.0 copy-start.3
  44.9 0.0 copy-start.4
  44.9 0.1 broadcast_in_dim.121.w_out_ref
  45.1 0.0 copy-done.1
  45.1 0.5 copy-done.3
  45.6 0.0 copy-done.4
  45.6 4.6 %forces_of_pairs.1 = f32[8,32,128]{2,1,0:T(8,128)} custom-call(s32[1]{0:T(128)} %bitcast.place_ref, s32[2]{0:T(128)S(1)} %bitcast.32, s32[2,256]{1,0:T(2,128)S(1)} %bitcast.30, f32[9,4,128]{2,1,0:T(4,128)S(1)} %collective-permute-done.4.below_ref, f32[9,4,128]{2,1,0:T(4,128)S(1)} %constant_dynamic-update-slice_fusion.level_ref, ...), custom_call_target="tpu_custom_call" | custom-call | tf_op jit(solution)/shard_map/forces_of_pairs/pallas_call | solution.py:319
  50.2 7.0 %all-to-all-start = ((f32[8,32,128]{2,1,0:T(8,128)}), f32[8,32,128]{2,1,0:T(8,128)S(1)}, u32[]{:S(2)}, u32[]{:S(2)}) async-start(f32[8,32,128]{2,1,0:T(8,128)} %forces_of_pairs.1), calls=%async_computation | async-start | bytes 262144 | tf_op jit(solution)/shard_map/all_to_all | solution.py:357
  57.3 7.9 %all-to-all-done = f32[8,32,128]{2,1,0:T(8,128)S(1)} async-done(((f32[8,32,128]{2,1,0:T(8,128)}), f32[8,32,128]{2,1,0:T(8,128)S(1)}, u32[]{:S(2)}, u32[]{:S(2)}) %all-to-all-start) | async-done | bytes 131104 | tf_op jit(solution)/shard_map/all_to_all | solution.py:357
  65.3 0.1 select_select_fusion
  65.4 0.6 pad_maximum_fusion
  66.1 7.4 %all-to-all-start.1 = ((f32[8,10,128]{2,1,0:T(8,128)}), f32[8,10,128]{2,1,0:T(8,128)S(1)}, u32[]{:S(2)}, u32[]{:S(2)}) async-start(f32[8,10,128]{2,1,0:T(8,128)} %pad_maximum_fusion), calls=%async_computation.1 | async-start | bytes 131072 | tf_op jit(solution)/shard_map/all_to_all | solution.py:358
  73.5 5.1 %all-to-all-done.1 = f32[8,10,128]{2,1,0:T(8,128)S(1)} async-done(((f32[8,10,128]{2,1,0:T(8,128)}), f32[8,10,128]{2,1,0:T(8,128)S(1)}, u32[]{:S(2)}, u32[]{:S(2)}) %all-to-all-start.1) | async-done | bytes 40992 | tf_op jit(solution)/shard_map/all_to_all | solution.py:358
  78.6 0.1 select_select_fusion.1
  78.7 11.3 %all_to_all.15 = f32[8,4,128]{2,1,0:T(4,128)S(1)} all-to-all(f32[8,4,128]{2,1,0:T(4,128)S(1)} %pad_maximum_fusion.1), channel_id=1, replica_groups=mesh['gx'=8,'gy'=8,'gz'=8] {'gz'}, dimensions={0} | all-to-all | bytes 32768 | tf_op jit(solution)/shard_map/all_to_all | solution.py:359
  90.1 0.6 slice_reduce_fusion
  90.7 0.6 copy.26
  (27 shorter events, 0.2 us)
Async XLA Ops:
  0.6 0.7 copy-start.7
  1.3 15.6 %collective-permute-start.1 = (f32[4,128]{1,0:T(4,128)S(1)}, f32[4,128]{1,0:T(4,128)S(1)}, u32[]{:S(2)}, u32[]{:S(2)}) collective-permute-start(f32[4,128]{1,0:T(4,128)S(1)} %pad_maximum_fusion.3), channel_id=1, source_target_pairs={{1,0},{2,1},{3,2},{4,3},{5,4},{6,5},{7,6},{0,7},{9,8},{10,9},{11,1... | collective-permute-start | bytes 6152 | tf_op jit(solution)/shard_map/ppermute | solution.py:289
  15.0 10.3 %collective-permute-start = (f32[4,128]{1,0:T(4,128)S(1)}, f32[4,128]{1,0:T(4,128)S(1)}, u32[]{:S(2)}, u32[]{:S(2)}) collective-permute-start(f32[4,128]{1,0:T(4,128)S(1)} %pad_maximum_fusion.3), channel_id=1, source_target_pairs={{0,1},{1,2},{2,3},{3,4},{4,5},{5,6},{6,7},{7,0},{8,9},{9,10},{10,1... | collective-permute-start | bytes 6152 | tf_op jit(solution)/shard_map/ppermute | solution.py:289
  25.3 3.3 %slice-start = ((s32[1,1,1,2,256]{4,3,2,1,0:T(2,128)}), s32[1,1,1,1,256]{4,3,2,1,0:T(1,128)S(1)}, s32[]{:S(2)}) async-start(s32[1,1,1,2,256]{4,3,2,1,0:T(2,128)} %param.11), calls=%async_computation.3 | async-start | bytes 2048 | tf_op jit(solution)/shard_map/slice | solution.py:313
  25.3 7.3 %collective-permute-start.2 = (f32[3,4,128]{2,1,0:T(4,128)S(1)}, f32[3,4,128]{2,1,0:T(4,128)S(1)}, u32[]{:S(2)}, u32[]{:S(2)}) collective-permute-start(f32[3,4,128]{2,1,0:T(4,128)S(1)} %pad_maximum_fusion.2), channel_id=1, source_target_pairs={{0,64},{64,128},{128,192},{192,256},{256,320},{320,384},{384,448},... | collective-permute-start | bytes 18440 | tf_op jit(solution)/shard_map/ppermute | solution.py:289
  28.8 13.0 %copy-start.5 = (bf16[512,12]{0,1:T(8,128)(2,1)S(1)}, bf16[512,12]{0,1:T(8,128)(2,1)}, u32[]{:S(2)}) copy-start(bf16[512,12]{0,1:T(8,128)(2,1)} %param.13) | copy-start | bytes 36868
  28.8 4.6 %collective-permute-start.3 = (f32[3,4,128]{2,1,0:T(4,128)S(1)}, f32[3,4,128]{2,1,0:T(4,128)S(1)}, u32[]{:S(2)}, u32[]{:S(2)}) collective-permute-start(f32[3,4,128]{2,1,0:T(4,128)S(1)} %pad_maximum_fusion.2), channel_id=1, source_target_pairs={{64,0},{128,64},{192,128},{256,192},{320,256},{384,320},{448,384},... | collective-permute-start | bytes 18440 | tf_op jit(solution)/shard_map/ppermute | solution.py:289
  33.4 10.0 %copy-start = (bf16[512,704]{0,1:T(8,128)(2,1)S(1)}, bf16[512,704]{0,1:T(8,128)(2,1)}, u32[]{:S(2)}) copy-start(bf16[512,704]{0,1:T(8,128)(2,1)} %param.16) | copy-start | bytes 2162692
  33.4 11.0 %collective-permute-start.4 = (f32[9,4,128]{2,1,0:T(4,128)S(1)}, f32[9,4,128]{2,1,0:T(4,128)S(1)}, u32[]{:S(2)}, u32[]{:S(2)}) collective-permute-start(f32[9,4,128]{2,1,0:T(4,128)S(1)} %constant_dynamic-update-slice_fusion.level_ref), channel_id=1, source_target_pairs={{0,8},{8,16},{16,24},{24,32},{32,40},{40,48},{48,56},{56,0},{1,9},... | collective-permute-start | bytes 55304 | tf_op jit(solution)/shard_map/ppermute | solution.py:289
  39.8 5.1 %collective-permute-start.5 = (f32[9,4,128]{2,1,0:T(4,128)S(1)}, f32[9,4,128]{2,1,0:T(4,128)S(1)}, u32[]{:S(2)}, u32[]{:S(2)}) collective-permute-start(f32[9,4,128]{2,1,0:T(4,128)S(1)} %constant_dynamic-update-slice_fusion.level_ref), channel_id=1, source_target_pairs={{8,0},{16,8},{24,16},{32,24},{40,32},{48,40},{56,48},{0,56},{9,1},... | collective-permute-start | bytes 55304 | tf_op jit(solution)/shard_map/ppermute | solution.py:289
  42.0 1.3 %copy-start.2 = (bf16[64,512]{1,0:T(8,128)(2,1)S(1)}, bf16[64,512]{1,0:T(8,128)(2,1)}, u32[]{:S(2)}) copy-start(bf16[64,512]{1,0:T(8,128)(2,1)} %w_env_ref.1) | copy-start | bytes 196612
  43.4 1.7 %copy-start.1 = (bf16[512,512]{1,0:T(8,128)(2,1)S(1)}, bf16[512,512]{1,0:T(8,128)(2,1)}, u32[]{:S(2)}) copy-start(bf16[512,512]{1,0:T(8,128)(2,1)} %w_hid_ref.1) | copy-start | bytes 1572868
  43.7 0.7 copy-start.6
  44.9 0.7 copy-start.3
  44.9 0.7 copy-start.4
  50.2 15.1 %all-to-all-start = ((f32[8,32,128]{2,1,0:T(8,128)}), f32[8,32,128]{2,1,0:T(8,128)S(1)}, u32[]{:S(2)}, u32[]{:S(2)}) async-start(f32[8,32,128]{2,1,0:T(8,128)} %forces_of_pairs.1), calls=%async_computation | async-start | bytes 262144 | tf_op jit(solution)/shard_map/all_to_all | solution.py:357
  66.1 12.5 %all-to-all-start.1 = ((f32[8,10,128]{2,1,0:T(8,128)}), f32[8,10,128]{2,1,0:T(8,128)S(1)}, u32[]{:S(2)}, u32[]{:S(2)}) async-start(f32[8,10,128]{2,1,0:T(8,128)} %pad_maximum_fusion), calls=%async_computation.1 | async-start | bytes 131072 | tf_op jit(solution)/shard_map/all_to_all | solution.py:358

commit v2 on v1

--- a/solution.py
+++ b/solution.py
@@ -23,7 +23,6 @@
 PAIRS = 256
 ATOMS = 128
 ROWS = 64
-ENERGY_ROW = 27
 
 
 def column_sum(block):
@@ -57,13 +56,46 @@
     )
 
 
+def pack_kernel(coords_ref, species_ref, out_ref):
+    block = jnp.concatenate([coords_ref[...], species_ref[...].astype(F32)], axis=0)
+    out_ref[...] = jnp.broadcast_to(block[None], out_ref.shape)
+
+
+def around():
+    at_y, at_z = lax.axis_index("gy"), lax.axis_index("gz")
+    return [
+        ((at_y + (RING + step_y)) & (RING - 1)) * RING + ((at_z + (RING + step_z)) & (RING - 1))
+        for step_y in (-1, 0, 1)
+        for step_z in (-1, 0, 1)
+    ]
+
+
+def pick_kernel(received_ref, out_ref):
+    for cell, number in enumerate(around()):
+        out_ref[cell] = received_ref[number]
+
+
+def address_kernel(received_ref, out_ref):
+    total = jnp.sum(received_ref[...], axis=0)
+    is_energy = lax.broadcasted_iota(jnp.int32, (4, ATOMS), 0) == 3
+    blank = jnp.where(is_energy, total[4], 0.0)
+    out_ref[...] = jnp.broadcast_to(blank[None], out_ref.shape)
+    for cell, number in enumerate(around()):
+        out_ref[number] = total[cell]
+
+
+def finish_kernel(received_ref, forces_ref, energy_ref):
+    total = jnp.sum(received_ref[...], axis=0)
+    forces_ref[...] = total[0:3]
+    energy_ref[0] = jnp.sum(total[3:4]) * (1.0 / (ATOMS * RING**3))
+
+
 def force_kernel(
-    place_ref,
     counts_ref,
     ids_ref,
-    below_ref,
+    even_ref,
     level_ref,
-    above_ref,
+    odd_ref,
     same_ref,
     w_in_ref,
     w_in_t_ref,
@@ -96,18 +128,18 @@
     step_y = (rest * 11) >> 5
     step_z = rest - 3 * step_y
 
+    place = lax.axis_index("gx")
+    parity = place & 1
     near, own = [], []
     for half in range(2):
         lanes = slice(half * ATOMS, (half + 1) * ATOMS)
         pick = jnp.broadcast_to(atom[:, lanes], (4, ATOMS))
         slot_half = jnp.broadcast_to(slot[:, lanes], (4, ATOMS))
         total = jnp.zeros((4, ATOMS), F32)
-        for at_y, slab in enumerate((below_ref, level_ref, above_ref)):
-            for at_x in range(3):
-                for at_z in range(3):
-                    rows = jnp.take_along_axis(slab[at_x * 3 + at_z], pick, axis=1)
-                    number = 9 * at_x + 3 * at_y + at_z
-                    total = jnp.where(slot_half == number, rows, total)
+        for slab, base in ((even_ref, 18 * (1 - parity)), (level_ref, 9), (odd_ref, 18 * parity)):
+            for cell in range(9):
+                rows = jnp.take_along_axis(slab[cell], pick, axis=1)
+                total = jnp.where(slot_half == base + cell, rows, total)
         near.append(total)
         pick = jnp.broadcast_to(centre[:, lanes], (4, ATOMS))
         own.append(jnp.take_along_axis(level_ref[4], pick, axis=1))
@@ -254,72 +286,63 @@
     radius_grad = radius_grad - radial * inverse
     push = [g * inverse + radius_grad * u for g, u in zip(unit_grad, unit)]
 
-    row = lax.broadcasted_iota(jnp.int32, (32, PAIRS), 0)
-    cell = (row * 11) >> 5
-    axis = row - 3 * cell
-    cell_y = (cell * 11) >> 5
-    wanted = 3 * cell_y + (cell - 3 * cell_y)
+    row = lax.broadcasted_iota(jnp.int32, (112, PAIRS), 0)
+    axis = row & 3
     moved = jnp.where(axis == 0, push[0], jnp.where(axis == 1, push[1], push[2]))
-    moved = jnp.where(row < ENERGY_ROW, moved, 0.0)
+    moved = jnp.where(axis == 3, 0.0, moved)
     atom_row = lax.broadcasted_iota(jnp.int32, (ATOMS, PAIRS), 0)
     hit_near = jnp.where(atom_row == atom, 1.0, 0.0).astype(BF16)
     hit_own = jnp.where(atom_row == centre, 1.0, 0.0).astype(BF16)
-    spread = jnp.concatenate(
-        [jnp.where(slot == wanted + 9 * at_x, -moved, 0.0) for at_x in range(3)], axis=0
-    )
-    spread = split_dot_nt(spread, hit_near)
-    home = split_dot_nt(jnp.where(cell == 4, moved, 0.0), hit_own)
+    spread = split_dot_nt(jnp.where((row >> 2) == slot, -moved, 0.0), hit_near)
+    home = split_dot_nt(moved[0:8], hit_own)[0:4]
+    spread = spread.reshape(28, 4, ATOMS)
     energy = column_sum(energy)
     energy = energy[:, 0:ATOMS] + energy[:, ATOMS:PAIRS]
-    is_energy = lax.broadcasted_iota(jnp.int32, (32, ATOMS), 0) == ENERGY_ROW
+    is_energy = lax.broadcasted_iota(jnp.int32, (4, ATOMS), 0) == 3
     blank = jnp.where(is_energy, energy, 0.0)
-    for peer in range(RING):
-        out_ref[peer] = blank
-    place = place_ref[0]
+    out_ref[...] = jnp.broadcast_to(blank[None, None], out_ref.shape)
     for at_x in range(3):
-        block = spread[32 * at_x : 32 * (at_x + 1), :]
-        if at_x == 1:
-            block = block + home
-        out_ref[(place + (at_x + RING - 1)) & (RING - 1)] = jnp.where(is_energy, energy, block)
-
-
-def both_sides(block, axis):
-    up = [(i, (i + 1) % RING) for i in range(RING)]
-    down = [((i + 1) % RING, i) for i in range(RING)]
-    return lax.ppermute(block, axis, up), lax.ppermute(block, axis, down)
-
-
-def addressed(total, axis, count):
-    place = lax.axis_index(axis)
-    peer = lax.broadcasted_iota(jnp.int32, (RING, 1, 1), 0)
-    rows = jnp.zeros((RING, count, ATOMS), F32)
-    for at in range(3):
-        here = peer == (place + (at + RING - 1)) % RING
-        rows = jnp.where(here, total[None, at * count : (at + 1) * count, :], rows)
-    energies = jnp.broadcast_to(total[None, 3 * count : 3 * count + 1, :], (RING, 1, ATOMS))
-    return jnp.concatenate([rows, energies], axis=1)
+        number = (place + (at_x + RING - 1)) & (RING - 1)
+        for cell in range(9):
+            block = spread[9 * at_x + cell]
+            if 9 * at_x + cell == 13:
+                block = block + home
+            out_ref[number, cell] = block + blank
+
+
+EVEN = [(i, i ^ 1) for i in range(RING)]
+ODD = [(i, (((i + 1) ^ 1) - 1) % RING) for i in range(RING)]
 
 
 def body(coords, species, pair_ids, live_counts, w_two_in, w_two_hid, w_env, w_latent, w_out):
     ids = pair_ids[0, 0, 0]
     counts = live_counts[0, 0, 0]
-    frame = jnp.concatenate([coords[0, 0, 0], species[0, 0, 0].astype(F32)[None]], axis=0)
-    low, high = both_sides(frame, "gz")
-    column = jnp.stack([low, frame, high], axis=0)
-    low, high = both_sides(column, "gx")
-    plane = jnp.concatenate([low, column, high], axis=0)
-    below, above = both_sides(plane, "gy")
+    vmem = pl.BlockSpec(memory_space=pltpu.VMEM)
+    smem = pl.BlockSpec(memory_space=pltpu.SMEM)
+    packed = pl.pallas_call(
+        pack_kernel,
+        out_shape=jax.ShapeDtypeStruct((RING * RING, 4, ATOMS), F32),
+        in_specs=[vmem] * 2,
+        out_specs=vmem,
+        name="pack_frame",
+    )(coords[0, 0, 0], species.reshape(1, ATOMS))
+    plane = pl.pallas_call(
+        pick_kernel,
+        out_shape=jax.ShapeDtypeStruct((9, 4, ATOMS), F32),
+        in_specs=[vmem],
+        out_specs=vmem,
+        name="pick_plane",
+    )(lax.all_to_all(packed, ("gy", "gz"), 0, 0))
+    even = lax.ppermute(plane, "gx", EVEN)
+    odd = lax.ppermute(plane, "gx", ODD)
 
     same = jnp.where(ids[0][:, None] == ids[0][None, :], ENV_NORM, 0.0).astype(BF16)
     w_in = jnp.pad(w_two_in, ((0, 0), (0, 4)))
     readout = jnp.broadcast_to(w_out.reshape(LAT, 1), (LAT, ATOMS))
-    place = lax.axis_index("gx").astype(jnp.int32).reshape(1)
-    vmem = pl.BlockSpec(memory_space=pltpu.VMEM)
-    smem = pl.BlockSpec(memory_space=pltpu.SMEM)
     sent = pl.pallas_call(
         force_kernel,
-        out_shape=jax.ShapeDtypeStruct((RING, 32, ATOMS), F32),
-        in_specs=[smem, smem] + [vmem] * 14,
+        out_shape=jax.ShapeDtypeStruct((RING, 9, 4, ATOMS), F32),
+        in_specs=[smem] + [vmem] * 14,
         out_specs=vmem,
         scratch_shapes=[
             pltpu.VMEM((LAT, PAIRS), F32),
@@ -337,12 +360,11 @@
         compiler_params=pltpu.CompilerParams(vmem_limit_bytes=24 * 1024 * 1024),
         name="forces_of_pairs",
     )(
-        place,
         counts,
         ids,
-        below,
+        even,
         plane,
-        above,
+        odd,
         same,
         w_in,
         w_in.T,
@@ -354,11 +376,21 @@
         w_latent.T,
         readout,
     )
-    total = jnp.sum(lax.all_to_all(sent, "gx", 0, 0), axis=0)
-    total = jnp.sum(lax.all_to_all(addressed(total, "gy", 9), "gy", 0, 0), axis=0)
-    total = jnp.sum(lax.all_to_all(addressed(total, "gz", 3), "gz", 0, 0), axis=0)
-    forces = total[0:3].reshape(1, 1, 1, 3, ATOMS)
-    return forces, jnp.sum(total[3]) * (1.0 / (ATOMS * RING**3))
+    addressed = pl.pallas_call(
+        address_kernel,
+        out_shape=jax.ShapeDtypeStruct((RING * RING, 4, ATOMS), F32),
+        in_specs=[vmem],
+        out_specs=vmem,
+        name="address_plane",
+    )(lax.all_to_all(sent, "gx", 0, 0))
+    forces, energy = pl.pallas_call(
+        finish_kernel,
+        out_shape=(jax.ShapeDtypeStruct((3, ATOMS), F32), jax.ShapeDtypeStruct((1,), F32)),
+        in_specs=[vmem],
+        out_specs=(vmem, smem),
+        name="finish",
+    )(lax.all_to_all(addressed, ("gy", "gz"), 0, 0))
+    return forces.reshape(1, 1, 1, 3, ATOMS), energy.reshape(())
 
 
 def solution(mesh):

time: 93.6 us -> 81.5 us (0.87)
  starting transfers between devices: 45.5 us -> 22 us
  blocking collectives: 11.3 us -> 30.9 us
  waiting for transfers between devices: 22.6 us -> 11.9 us
  Pallas kernels: 4.63 us -> 10.1 us
  other arithmetic: 2.32 us -> 0.12 us
  between operations: 2.79 us -> 0.81 us
  local copies, waits for them, and re-layouts: 3.83 us -> 5.15 us
    ppermute x6 -> x2, starting transfers between devices: 31.1 us -> 7.14 us  [the longest x1 5.22 us: body(): odd = lax.ppermute(plane, 'gx', ODD)]
    all_to_all x1 -> x2, blocking collectives: 11.3 us -> 30.9 us  [the longest x1 18.7 us: body(): lax.all_to_all(addressed, ('gy', 'gz'), 0, 0)]
    ppermute x6 -> x2, waiting for transfers between devices: 9.59 us -> 1.5 us  [the longest x1 1.5 us: body(): even = lax.ppermute(plane, 'gx', EVEN)]
    pallas_call x1 -> x5, Pallas kernels: 4.63 us -> 10.1 us  [the longest x1 3.98 us: body(): pl.pallas_call(force_kernel, out_shape=jax.ShapeDtypeStruct((RING, 9, 4,...]
    all_to_all x2 -> x1, waiting for transfers between devices: 13 us -> 10.4 us  [body(): lax.all_to_all(packed, ('gy', 'gz'), 0, 0)]
    unnamed x25 -> x26, local copies, waits for them, and re-layouts: 3.62 us -> 4.98 us
    all_to_all x2 -> x1, starting transfers between devices: 14.4 us -> 14.8 us  [body(): lax.all_to_all(packed, ('gy', 'gz'), 0, 0)]
  transfers between devices with their start and end apart: 8 -> 3, of which waited for: 5 -> 2; matrix products, arithmetic and copies ran while one was open for 2% -> 1% of each run, Pallas kernels for 0% -> 0%
where the time goes in v2:
time: 81.5 us; the launch traced here: 80.9 us
  blocking collectives  30.9 us (38%)
  starting transfers between devices  22 us (27%)
  waiting for transfers between devices  11.9 us (15%)
  Pallas kernels  10.1 us (12%)
  local copies, waits for them, and re-layouts  5.15 us (6%)
    all_to_all x1, blocking collectives, body(): lax.all_to_all(addressed, ('gy', 'gz'), 0, 0)  18.7 us
    all_to_all x1, starting transfers between devices, body(): lax.all_to_all(packed, ('gy', 'gz'), 0, 0)  14.8 us
    all_to_all x1, blocking collectives, body(): lax.all_to_all(sent, 'gx', 0, 0)  12.2 us
    all_to_all x1, waiting for transfers between devices, body(): lax.all_to_all(packed, ('gy', 'gz'), 0, 0)  10.4 us
    ppermute x1, starting transfers between devices, body(): odd = lax.ppermute(plane, 'gx', ODD)  5.22 us
    unnamed x26, local copies, waits for them, and re-layouts  4.98 us
    pallas_call x1, Pallas kernels, body(): pl.pallas_call(force_kernel, out_shape=jax.ShapeDtypeStruct((RING, 9, 4,...  3.98 us
    ppermute x1, starting transfers between devices, body(): even = lax.ppermute(plane, 'gx', EVEN)  1.92 us
  transfers between devices with their start and end apart: 3, of which 2 were waited for; matrix products, arithmetic and copies ran while one was open for 1% of the time, Pallas kernels for 0%

profile of v2, /device:TPU:1, one launch (start us, length us, event | category | flops | bytes accessed | tf_op | source)
XLA Modules:
  0.0 80.9 jit_solution(1697539970065946550)
XLA Ops:
  0.6 0.0 slice-start
  0.6 1.3 %copy.19 = f32[1,1,1,3,128]{4,3,2,1,0:T(4,128)} copy(f32[1,1,1,3,128]{4,2,3,1,0:T(1,128)} %param.9) | data formatting | bytes 3072
  1.9 0.0 copy-start.1
  1.9 1.4 %pack_frame.1 = f32[64,4,128]{2,1,0:T(4,128)} custom-call(f32[3,128]{1,0:T(4,128)} %bitcast.20, s32[1,128]{1,0:T(1,128)} %bitcast.22), custom_call_target="tpu_custom_call" | custom-call | tf_op jit(solution)/shard_map/pack_frame/pallas_call | solution.py:322
  3.3 14.8 %all-to-all-start = ((f32[64,4,128]{2,1,0:T(4,128)}), f32[64,4,128]{2,1,0:T(4,128)S(1)}, u32[]{:S(2)}, u32[]{:S(2)}) async-start(f32[64,4,128]{2,1,0:T(4,128)} %pack_frame.1), calls=%async_computation | async-start | bytes 262144 | tf_op jit(solution)/shard_map/all_to_all | solution.py:335
  18.1 0.0 slice-done
  18.2 0.1 select_convert_fusion.same_ref
  18.3 0.0 copy-start.7
  18.3 10.4 %all-to-all-done.received_ref = f32[64,4,128]{2,1,0:T(4,128)S(1)} async-done(((f32[64,4,128]{2,1,0:T(4,128)}), f32[64,4,128]{2,1,0:T(4,128)S(1)}, u32[]{:S(2)}, u32[]{:S(2)}) %all-to-all-start) | async-done | bytes 131104 | tf_op jit(solution)/shard_map/all_to_all | solution.py:335
  28.7 0.0 copy-start.6
  28.7 0.6 copy-done.6
  29.3 0.0 copy-start.2
  29.3 1.5 %pick_plane.1.level_ref = f32[9,4,128]{2,1,0:T(4,128)} custom-call(f32[64,4,128]{2,1,0:T(4,128)} %copy-done.6), custom_call_target="tpu_custom_call" | custom-call | tf_op jit(solution)/shard_map/pick_plane/pallas_call | solution.py:329
  30.9 0.0 copy-start
  30.9 5.2 %collective-permute-start.1 = (f32[9,4,128]{2,1,0:T(4,128)}, f32[9,4,128]{2,1,0:T(4,128)S(1)}, u32[]{:S(2)}, u32[]{:S(2)}) collective-permute-start(f32[9,4,128]{2,1,0:T(4,128)} %pick_plane.1.level_ref), channel_id=1, source_target_pairs={{0,448},{64,128},{128,64},{192,256},{256,192},{320,384},{384,320},... | collective-permute-start | bytes 55304 | tf_op jit(solution)/shard_map/ppermute | solution.py:337
  36.1 1.9 %collective-permute-start = (f32[9,4,128]{2,1,0:T(4,128)}, f32[9,4,128]{2,1,0:T(4,128)S(1)}, u32[]{:S(2)}, u32[]{:S(2)}) collective-permute-start(f32[9,4,128]{2,1,0:T(4,128)} %pick_plane.1.level_ref), channel_id=1, source_target_pairs={{0,64},{64,0},{128,192},{192,128},{256,320},{320,256},{384,448},{4... | collective-permute-start | bytes 55304 | tf_op jit(solution)/shard_map/ppermute | solution.py:336
  38.0 0.0 copy-done.7
  38.0 0.2 copy.18
  38.2 0.0 copy-done.2
  38.2 0.1 copy.12
  38.3 0.0 copy-done.1
  38.3 0.2 copy.11
  38.6 0.0 copy-done
  38.6 0.0 copy-start.8
  38.6 0.3 copy.14.w_lat_ref
  38.9 0.4 copy-done.8
  39.3 0.0 collective-permute-done.1.odd_ref
  39.3 1.5 %collective-permute-done.even_ref = f32[9,4,128]{2,1,0:T(4,128)S(1)} collective-permute-done((f32[9,4,128]{2,1,0:T(4,128)}, f32[9,4,128]{2,1,0:T(4,128)S(1)}, u32[]{:S(2)}, u32[]{:S(2)}) %collective-permute-start) | collective-permute-done | bytes 18464 | tf_op jit(solution)/shard_map/ppermute | solution.py:336
  40.8 0.0 copy-start.3
  40.8 0.1 broadcast_in_dim.18.w_out_ref
  41.0 0.0 copy-start.4
  41.0 0.0 copy-start.5
  41.0 0.6 copy-done.3
  41.5 0.1 copy-done.4
  41.6 0.0 copy-done.5
  41.6 4.0 %forces_of_pairs.1 = f32[8,9,4,128]{3,2,1,0:T(4,128)S(1)} custom-call(s32[2]{0:T(128)S(1)} %bitcast.19, s32[2,256]{1,0:T(2,128)S(1)} %bitcast.17, f32[9,4,128]{2,1,0:T(4,128)S(1)} %collective-permute-done.even_ref, f32[9,4,128]{2,1,0:T(4,128)S(1)} %copy-done.3, f32[9,4,128]{2,1,0:T(4,128)S(1)} %collective-permute-done.1.odd_ref, ...), custom_call_target="tpu_custom_call" | custom-call | tf_op jit(solution)/shard_map/forces_of_pairs/pallas_call | solution.py:342
  45.6 12.2 %all_to_all.15.received_ref = f32[8,9,4,128]{3,2,1,0:T(4,128)} all-to-all(f32[8,9,4,128]{3,2,1,0:T(4,128)S(1)} %forces_of_pairs.1), channel_id=1, replica_groups=mesh['gx'=8,'gy'=8,'gz'=8] {'gx'}, dimensions={0} | all-to-all | bytes 294912 | tf_op jit(solution)/shard_map/all_to_all | solution.py:385
  57.8 1.6 %address_plane.1 = f32[64,4,128]{2,1,0:T(4,128)} custom-call(f32[8,9,4,128]{3,2,1,0:T(4,128)} %all_to_all.15.received_ref), custom_call_target="tpu_custom_call" | custom-call | tf_op jit(solution)/shard_map/address_plane/pallas_call | solution.py:379
  59.4 18.7 %all_to_all.16.received_ref = f32[64,4,128]{2,1,0:T(4,128)} all-to-all(f32[64,4,128]{2,1,0:T(4,128)} %address_plane.1), channel_id=1, replica_groups=mesh['gx'=8,'gy'=8,'gz'=8] {'gy','gz'}, dimensions={0} | all-to-all | bytes 262144 | tf_op jit(solution)/shard_map/all_to_all | solution.py:392
  78.1 1.6 %finish.1 = (f32[3,128]{1,0:T(4,128)}, f32[1]{0:T(128)}) custom-call(f32[64,4,128]{2,1,0:T(4,128)} %all_to_all.16.received_ref), custom_call_target="tpu_custom_call" | custom-call | tf_op jit(solution)/shard_map/finish/pallas_call | solution.py:386
  79.7 0.0 copy-start.9
  79.7 0.7 copy-done.9
  80.4 0.6 copy.15
  (3 shorter events, 0.1 us)
Async XLA Ops:
  0.6 17.5 %slice-start = ((s32[1,1,1,2,256]{4,3,2,1,0:T(2,128)}), s32[1,1,1,1,256]{4,3,2,1,0:T(1,128)S(1)}, s32[]{:S(2)}) async-start(s32[1,1,1,2,256]{4,3,2,1,0:T(2,128)} %param.11), calls=%async_computation.3 | async-start | bytes 2048 | tf_op jit(solution)/shard_map/slice | solution.py:339
  1.9 36.4 %copy-start.1 = (bf16[512,512]{1,0:T(8,128)(2,1)S(1)}, bf16[512,512]{1,0:T(8,128)(2,1)}, u32[]{:S(2)}) copy-start(bf16[512,512]{1,0:T(8,128)(2,1)} %w_hid_ref.1) | copy-start | bytes 1572868
  3.3 25.4 %all-to-all-start = ((f32[64,4,128]{2,1,0:T(4,128)}), f32[64,4,128]{2,1,0:T(4,128)S(1)}, u32[]{:S(2)}, u32[]{:S(2)}) async-start(f32[64,4,128]{2,1,0:T(4,128)} %pack_frame.1), calls=%async_computation | async-start | bytes 262144 | tf_op jit(solution)/shard_map/all_to_all | solution.py:335
  18.3 19.8 %copy-start.7 = (bf16[512,12]{0,1:T(8,128)(2,1)S(1)}, bf16[512,12]{0,1:T(8,128)(2,1)}, u32[]{:S(2)}) copy-start(bf16[512,12]{0,1:T(8,128)(2,1)} %param.13) | copy-start | bytes 36868
  28.7 0.7 copy-start.6
  29.3 8.9 %copy-start.2 = (bf16[64,512]{1,0:T(8,128)(2,1)S(1)}, bf16[64,512]{1,0:T(8,128)(2,1)}, u32[]{:S(2)}) copy-start(bf16[64,512]{1,0:T(8,128)(2,1)} %w_env_ref.1) | copy-start | bytes 196612
  30.9 7.7 %copy-start = (bf16[512,704]{0,1:T(8,128)(2,1)S(1)}, bf16[512,704]{0,1:T(8,128)(2,1)}, u32[]{:S(2)}) copy-start(bf16[512,704]{0,1:T(8,128)(2,1)} %param.16) | copy-start | bytes 2162692
  30.9 8.4 %collective-permute-start.1 = (f32[9,4,128]{2,1,0:T(4,128)}, f32[9,4,128]{2,1,0:T(4,128)S(1)}, u32[]{:S(2)}, u32[]{:S(2)}) collective-permute-start(f32[9,4,128]{2,1,0:T(4,128)} %pick_plane.1.level_ref), channel_id=1, source_target_pairs={{0,448},{64,128},{128,64},{192,256},{256,192},{320,384},{384,320},... | collective-permute-start | bytes 55304 | tf_op jit(solution)/shard_map/ppermute | solution.py:337
  36.1 4.7 %collective-permute-start = (f32[9,4,128]{2,1,0:T(4,128)}, f32[9,4,128]{2,1,0:T(4,128)S(1)}, u32[]{:S(2)}, u32[]{:S(2)}) collective-permute-start(f32[9,4,128]{2,1,0:T(4,128)} %pick_plane.1.level_ref), channel_id=1, source_target_pairs={{0,64},{64,0},{128,192},{192,128},{256,320},{320,256},{384,448},{4... | collective-permute-start | bytes 55304 | tf_op jit(solution)/shard_map/ppermute | solution.py:336
  38.6 0.7 copy-start.8
  40.8 0.7 copy-start.3
  41.0 0.7 copy-start.4
  41.0 0.7 copy-start.5
  79.7 0.7 copy-start.9

commit v3 on v2

--- a/solution.py
+++ b/solution.py
@@ -57,7 +57,8 @@
 
 
 def pack_kernel(coords_ref, species_ref, out_ref):
-    block = jnp.concatenate([coords_ref[...], species_ref[...].astype(F32)], axis=0)
+    rows = [coords_ref[axis] for axis in range(3)] + [species_ref[...].astype(F32)]
+    block = jnp.concatenate(rows, axis=0)
     out_ref[...] = jnp.broadcast_to(block[None], out_ref.shape)
 
 
@@ -86,7 +87,8 @@
 
 def finish_kernel(received_ref, forces_ref, energy_ref):
     total = jnp.sum(received_ref[...], axis=0)
-    forces_ref[...] = total[0:3]
+    for axis in range(3):
+        forces_ref[axis] = total[axis : axis + 1]
     energy_ref[0] = jnp.sum(total[3:4]) * (1.0 / (ATOMS * RING**3))
 
 
@@ -310,6 +312,7 @@
             out_ref[number, cell] = block + blank
 
 
+SMALL = pltpu.CompilerParams(vmem_limit_bytes=2 * 1024 * 1024)
 EVEN = [(i, i ^ 1) for i in range(RING)]
 ODD = [(i, (((i + 1) ^ 1) - 1) % RING) for i in range(RING)]
 
@@ -324,13 +327,15 @@
         out_shape=jax.ShapeDtypeStruct((RING * RING, 4, ATOMS), F32),
         in_specs=[vmem] * 2,
         out_specs=vmem,
+        compiler_params=SMALL,
         name="pack_frame",
-    )(coords[0, 0, 0], species.reshape(1, ATOMS))
+    )(coords.reshape(3, 1, ATOMS), species.reshape(1, ATOMS))
     plane = pl.pallas_call(
         pick_kernel,
         out_shape=jax.ShapeDtypeStruct((9, 4, ATOMS), F32),
         in_specs=[vmem],
         out_specs=vmem,
+        compiler_params=SMALL,
         name="pick_plane",
     )(lax.all_to_all(packed, ("gy", "gz"), 0, 0))
     even = lax.ppermute(plane, "gx", EVEN)
@@ -381,13 +386,15 @@
         out_shape=jax.ShapeDtypeStruct((RING * RING, 4, ATOMS), F32),
         in_specs=[vmem],
         out_specs=vmem,
+        compiler_params=SMALL,
         name="address_plane",
     )(lax.all_to_all(sent, "gx", 0, 0))
     forces, energy = pl.pallas_call(
         finish_kernel,
-        out_shape=(jax.ShapeDtypeStruct((3, ATOMS), F32), jax.ShapeDtypeStruct((1,), F32)),
+        out_shape=(jax.ShapeDtypeStruct((3, 1, ATOMS), F32), jax.ShapeDtypeStruct((1,), F32)),
         in_specs=[vmem],
         out_specs=(vmem, smem),
+        compiler_params=SMALL,
         name="finish",
     )(lax.all_to_all(addressed, ("gy", "gz"), 0, 0))
     return forces.reshape(1, 1, 1, 3, ATOMS), energy.reshape(())

time: 81.5 us -> 72.7 us (0.89)
  Pallas kernels: 10.1 us -> 5.39 us
  local copies, waits for them, and re-layouts: 5.15 us -> 3.36 us
  blocking collectives: 30.9 us -> 29.6 us
  waiting for transfers between devices: 11.9 us -> 11 us
    unnamed x26 -> x22, local copies, waits for them, and re-layouts: 4.98 us -> 2.51 us
    pallas_call x1, Pallas kernels: 1.6 us -> 0.04 us  [body(): pl.pallas_call(address_kernel, out_shape=jax.ShapeDtypeStruct((RING * RIN...]
    pallas_call x1, Pallas kernels: 1.54 us -> 0.01 us  [body(): pl.pallas_call(pick_kernel, out_shape=jax.ShapeDtypeStruct((9, 4, ATOMS),...]
    all_to_all x1, blocking collectives: 18.7 us -> 17.5 us  [body(): lax.all_to_all(addressed, ('gy', 'gz'), 0, 0)]
    pallas_call x1, Pallas kernels: 1.61 us -> 0.7 us  [body(): pl.pallas_call(finish_kernel, out_shape=(jax.ShapeDtypeStruct((3, 1, ATOM...]
  transfers between devices with their start and end apart: 3 -> 3, of which waited for: 2 -> 2; matrix products, arithmetic and copies ran while one was open for 1% -> 2% of each run, Pallas kernels for 0% -> 0%
where the time goes in v3:
time: 72.7 us; the launch traced here: 72.3 us
  blocking collectives  29.6 us (41%)
  starting transfers between devices  22 us (30%)
  waiting for transfers between devices  11 us (15%)
  Pallas kernels  5.39 us (7%)
  local copies, waits for them, and re-layouts  3.36 us (5%)
  between operations  0.8 us (1%)
    all_to_all x1, blocking collectives, body(): lax.all_to_all(addressed, ('gy', 'gz'), 0, 0)  17.5 us
    all_to_all x1, starting transfers between devices, body(): lax.all_to_all(packed, ('gy', 'gz'), 0, 0)  14.8 us
    all_to_all x1, blocking collectives, body(): lax.all_to_all(sent, 'gx', 0, 0)  12.1 us
    all_to_all x1, waiting for transfers between devices, body(): lax.all_to_all(packed, ('gy', 'gz'), 0, 0)  9.72 us
    ppermute x1, starting transfers between devices, body(): odd = lax.ppermute(plane, 'gx', ODD)  5.23 us
    pallas_call x1, Pallas kernels, body(): pl.pallas_call(force_kernel, out_shape=jax.ShapeDtypeStruct((RING, 9, 4,...  3.98 us
    unnamed x22, local copies, waits for them, and re-layouts  2.51 us
    ppermute x1, starting transfers between devices, body(): even = lax.ppermute(plane, 'gx', EVEN)  1.92 us
  transfers between devices with their start and end apart: 3, of which 2 were waited for; matrix products, arithmetic and copies ran while one was open for 2% of the time, Pallas kernels for 0%

profile of v3, /device:TPU:1, one launch (start us, length us, event | category | flops | bytes accessed | tf_op | source)
XLA Modules:
  0.0 72.3 jit_solution(3837716272763655260)
XLA Ops:
  0.6 0.0 copy-start.4
  0.6 0.0 copy-start.5
  0.6 0.7 copy-done.4
  1.3 0.0 copy-done.5
  1.3 0.0 copy-start.1
  1.3 0.7 pack_frame.1
  2.0 14.8 %all-to-all-start = ((f32[64,4,128]{2,1,0:T(4,128)}), f32[64,4,128]{2,1,0:T(4,128)S(1)}, u32[]{:S(2)}, u32[]{:S(2)}) async-start(f32[64,4,128]{2,1,0:T(4,128)} %pack_frame.1), calls=%async_computation | async-start | bytes 262144 | tf_op jit(solution)/shard_map/all_to_all | solution.py:340
  16.8 0.7 slice.5
  17.5 0.1 select_convert_fusion.same_ref
  17.6 0.0 copy-start.7
  17.6 9.7 %all-to-all-done.received_ref = f32[64,4,128]{2,1,0:T(4,128)S(1)} async-done(((f32[64,4,128]{2,1,0:T(4,128)}), f32[64,4,128]{2,1,0:T(4,128)S(1)}, u32[]{:S(2)}, u32[]{:S(2)}) %all-to-all-start) | async-done | bytes 131104 | tf_op jit(solution)/shard_map/all_to_all | solution.py:340
  27.3 0.0 copy-start.2
  27.4 0.0 copy-start
  27.4 5.2 %collective-permute-start.1 = (f32[9,4,128]{2,1,0:T(4,128)S(1)}, f32[9,4,128]{2,1,0:T(4,128)S(1)}, u32[]{:S(2)}, u32[]{:S(2)}) collective-permute-start(f32[9,4,128]{2,1,0:T(4,128)S(1)} %pick_plane.1.level_ref), channel_id=1, source_target_pairs={{0,448},{64,128},{128,64},{192,256},{256,192},{320,384},{384,320},... | collective-permute-start | bytes 55304 | tf_op jit(solution)/shard_map/ppermute | solution.py:342
  32.6 1.9 %collective-permute-start = (f32[9,4,128]{2,1,0:T(4,128)S(1)}, f32[9,4,128]{2,1,0:T(4,128)S(1)}, u32[]{:S(2)}, u32[]{:S(2)}) collective-permute-start(f32[9,4,128]{2,1,0:T(4,128)S(1)} %pick_plane.1.level_ref), channel_id=1, source_target_pairs={{0,64},{64,0},{128,192},{192,128},{256,320},{320,256},{384,448},{4... | collective-permute-start | bytes 55304 | tf_op jit(solution)/shard_map/ppermute | solution.py:341
  34.5 0.0 copy-done.7
  34.6 0.2 copy.16
  34.7 0.0 copy-done.2
  34.7 0.1 copy.12
  34.8 0.0 copy-done.1
  34.9 0.2 copy.11
  35.1 0.0 copy-done
  35.1 0.0 copy-start.8
  35.1 0.3 copy.14.w_lat_ref
  35.4 0.4 copy-done.8
  35.8 0.0 collective-permute-done.1.odd_ref
  35.8 1.3 %collective-permute-done.even_ref = f32[9,4,128]{2,1,0:T(4,128)S(1)} collective-permute-done((f32[9,4,128]{2,1,0:T(4,128)S(1)}, f32[9,4,128]{2,1,0:T(4,128)S(1)}, u32[]{:S(2)}, u32[]{:S(2)}) %collective-permute-start) | collective-permute-done | bytes 18464 | tf_op jit(solution)/shard_map/ppermute | solution.py:341
  37.1 0.1 broadcast_in_dim.18.w_out_ref
  37.3 0.0 copy-start.3
  37.3 0.0 copy-start.6
  37.3 0.7 copy-done.3
  37.9 0.0 copy-done.6
  37.9 4.0 %forces_of_pairs.1 = f32[8,9,4,128]{3,2,1,0:T(4,128)S(1)} custom-call(s32[2]{0:T(128)S(1)} %bitcast.20, s32[2,256]{1,0:T(2,128)S(1)} %bitcast.17, f32[9,4,128]{2,1,0:T(4,128)S(1)} %collective-permute-done.even_ref, f32[9,4,128]{2,1,0:T(4,128)S(1)} %pick_plane.1.level_ref, f32[9,4,128]{2,1,0:T(4,128)S(1)} %collective-permute-done.1.odd_ref, ...), custom_call_target="tpu_custom_call" | custom-call | tf_op jit(solution)/shard_map/forces_of_pairs/pallas_call | solution.py:347
  41.9 12.1 %all_to_all.15.received_ref = f32[8,9,4,128]{3,2,1,0:T(4,128)S(1)} all-to-all(f32[8,9,4,128]{3,2,1,0:T(4,128)S(1)} %forces_of_pairs.1), channel_id=1, replica_groups=mesh['gx'=8,'gy'=8,'gz'=8] {'gx'}, dimensions={0} | all-to-all | bytes 294912 | tf_op jit(solution)/shard_map/all_to_all | solution.py:391
  54.1 17.5 %all_to_all.16.received_ref = f32[64,4,128]{2,1,0:T(4,128)S(1)} all-to-all(f32[64,4,128]{2,1,0:T(4,128)S(1)} %address_plane.1), channel_id=1, replica_groups=mesh['gx'=8,'gy'=8,'gz'=8] {'gy','gz'}, dimensions={0} | all-to-all | bytes 262144 | tf_op jit(solution)/shard_map/all_to_all | solution.py:399
  71.6 0.7 finish.1
  (5 shorter events, 0.1 us)
Async XLA Ops:
  0.6 0.7 copy-start.4
  0.6 0.7 copy-start.5
  1.3 33.5 %copy-start.1 = (bf16[512,512]{1,0:T(8,128)(2,1)S(1)}, bf16[512,512]{1,0:T(8,128)(2,1)}, u32[]{:S(2)}) copy-start(bf16[512,512]{1,0:T(8,128)(2,1)} %w_hid_ref.1) | copy-start | bytes 1572868
  2.0 25.4 %all-to-all-start = ((f32[64,4,128]{2,1,0:T(4,128)}), f32[64,4,128]{2,1,0:T(4,128)S(1)}, u32[]{:S(2)}, u32[]{:S(2)}) async-start(f32[64,4,128]{2,1,0:T(4,128)} %pack_frame.1), calls=%async_computation | async-start | bytes 262144 | tf_op jit(solution)/shard_map/all_to_all | solution.py:340
  17.6 16.9 %copy-start.7 = (bf16[512,12]{0,1:T(8,128)(2,1)S(1)}, bf16[512,12]{0,1:T(8,128)(2,1)}, u32[]{:S(2)}) copy-start(bf16[512,12]{0,1:T(8,128)(2,1)} %param.13) | copy-start | bytes 36868
  27.3 7.4 %copy-start.2 = (bf16[64,512]{1,0:T(8,128)(2,1)S(1)}, bf16[64,512]{1,0:T(8,128)(2,1)}, u32[]{:S(2)}) copy-start(bf16[64,512]{1,0:T(8,128)(2,1)} %w_env_ref.1) | copy-start | bytes 196612
  27.4 7.7 %copy-start = (bf16[512,704]{0,1:T(8,128)(2,1)S(1)}, bf16[512,704]{0,1:T(8,128)(2,1)}, u32[]{:S(2)}) copy-start(bf16[512,704]{0,1:T(8,128)(2,1)} %param.16) | copy-start | bytes 2162692
  27.4 8.4 %collective-permute-start.1 = (f32[9,4,128]{2,1,0:T(4,128)S(1)}, f32[9,4,128]{2,1,0:T(4,128)S(1)}, u32[]{:S(2)}, u32[]{:S(2)}) collective-permute-start(f32[9,4,128]{2,1,0:T(4,128)S(1)} %pick_plane.1.level_ref), channel_id=1, source_target_pairs={{0,448},{64,128},{128,64},{192,256},{256,192},{320,384},{384,320},... | collective-permute-start | bytes 55304 | tf_op jit(solution)/shard_map/ppermute | solution.py:342
  32.6 4.5 %collective-permute-start = (f32[9,4,128]{2,1,0:T(4,128)S(1)}, f32[9,4,128]{2,1,0:T(4,128)S(1)}, u32[]{:S(2)}, u32[]{:S(2)}) collective-permute-start(f32[9,4,128]{2,1,0:T(4,128)S(1)} %pick_plane.1.level_ref), channel_id=1, source_target_pairs={{0,64},{64,0},{128,192},{192,128},{256,320},{320,256},{384,448},{4... | collective-permute-start | bytes 55304 | tf_op jit(solution)/shard_map/ppermute | solution.py:341
  35.1 0.7 copy-start.8
  37.3 0.7 copy-start.3
  37.3 0.7 copy-start.6

commit v4 on v3

--- a/solution.py
+++ b/solution.py
@@ -39,12 +39,8 @@
     return value, gate + value * (1.0 - gate)
 
 
-def split_dot(block, square):
-    high = block.astype(BF16)
-    low = (block - high.astype(F32)).astype(BF16)
-    return jnp.dot(high, square, preferred_element_type=F32) + jnp.dot(
-        low, square, preferred_element_type=F32
-    )
+def dot_tn(left, right):
+    return lax.dot_general(left, right, (((0,), (0,)), ((), ())), preferred_element_type=F32)
 
 
 def split_dot_nt(block, other):
@@ -92,9 +88,24 @@
     energy_ref[0] = jnp.sum(total[3:4]) * (1.0 / (ATOMS * RING**3))
 
 
+def prepare_kernel(counts_ref, ids_ref, w_out_ref, pairs_ref, hits_ref, same_ref, readout_ref):
+    centre = ids_ref[0:1, :]
+    neighbour = ids_ref[1:2, :]
+    lane = lax.broadcasted_iota(jnp.int32, (1, PAIRS), 1)
+    live = lane < jnp.where(lane < ATOMS, counts_ref[0], counts_ref[1] + ATOMS)
+    rows = [centre, neighbour >> 7, neighbour & 127, live.astype(jnp.int32)]
+    pairs_ref[...] = jnp.concatenate(rows + rows, axis=0)
+    atom_row = lax.broadcasted_iota(jnp.int32, (ATOMS, PAIRS), 0)
+    hits_ref[0] = jnp.where(atom_row == rows[2], 1.0, 0.0).astype(BF16)
+    hits_ref[1] = jnp.where(atom_row == centre, 1.0, 0.0).astype(BF16)
+    across = jnp.broadcast_to(centre.astype(F32), (PAIRS, PAIRS))
+    same_ref[...] = jnp.where(across == across.T, ENV_NORM, 0.0).astype(BF16)
+    readout_ref[...] = jnp.broadcast_to(w_out_ref[...].astype(F32), (ATOMS, LAT)).T.astype(BF16)
+
+
 def force_kernel(
-    counts_ref,
-    ids_ref,
+    pairs_ref,
+    hits_ref,
     even_ref,
     level_ref,
     odd_ref,
@@ -116,15 +127,12 @@
     joined_ref,
     grad_ref,
     dz_ref,
-    vec_ref,
-    env_ref,
-    dvec_ref,
     dlat_ref,
 ):
-    centre = ids_ref[0:1, :]
-    neighbour = ids_ref[1:2, :]
-    slot = neighbour >> 7
-    atom = neighbour & 127
+    centre = pairs_ref[0:1, :]
+    slot = pairs_ref[1:2, :]
+    atom = pairs_ref[2:3, :]
+    live = pairs_ref[3:4, :].astype(F32)
     step_x = (slot * 57) >> 9
     rest = slot - 9 * step_x
     step_y = (rest * 11) >> 5
@@ -140,11 +148,11 @@
         total = jnp.zeros((4, ATOMS), F32)
         for slab, base in ((even_ref, 18 * (1 - parity)), (level_ref, 9), (odd_ref, 18 * parity)):
             for cell in range(9):
-                rows = jnp.take_along_axis(slab[cell], pick, axis=1)
+                rows = jnp.take_along_axis(slab[cell], pick, axis=1, mode="promise_in_bounds")
                 total = jnp.where(slot_half == base + cell, rows, total)
         near.append(total)
         pick = jnp.broadcast_to(centre[:, lanes], (4, ATOMS))
-        own.append(jnp.take_along_axis(level_ref[4], pick, axis=1))
+        own.append(jnp.take_along_axis(level_ref[4], pick, axis=1, mode="promise_in_bounds"))
     near = jnp.concatenate(near, axis=1)
     own = jnp.concatenate(own, axis=1)
     delta = [
@@ -154,9 +162,6 @@
         for axis, step in enumerate((step_x, step_y, step_z))
     ]
 
-    lane = lax.broadcasted_iota(jnp.int32, (1, PAIRS), 1)
-    half_live = jnp.where(lane < ATOMS, counts_ref[0], counts_ref[1] + ATOMS)
-    live = jnp.where(lane < half_live, 1.0, 0.0)
     radius = jnp.sqrt(delta[0] * delta[0] + delta[1] * delta[1] + delta[2] * delta[2] + SOFTEN)
     inverse = 1.0 / radius
     ratio = radius * (1.0 / CUTOFF)
@@ -204,32 +209,34 @@
 
     unit = [part * inverse for part in delta]
     along_x, along_y, along_z = unit
-    shapes = [
-        None,
-        ROOT3 * along_x,
-        ROOT3 * along_y,
-        ROOT3 * along_z,
+    zero = jnp.zeros_like(along_x)
+    first = [ROOT3 * along_x, ROOT3 * along_y, ROOT3 * along_z]
+    second = [
         ROOT15 * along_x * along_y,
         ROOT15 * along_y * along_z,
         0.5 * ROOT5 * (2.0 * along_z * along_z - along_x * along_x - along_y * along_y),
         ROOT15 * along_x * along_z,
         0.5 * ROOT15 * (along_x * along_x - along_y * along_y),
     ]
+    shapes = [
+        jnp.concatenate(rows + [zero] * (16 - len(rows)), axis=0).astype(BF16)
+        for rows in (first, second)
+    ]
     same = same_ref[...]
+    links = [same] + [dot_tn(rows, rows).astype(BF16) * same for rows in shapes]
     weight = jnp.dot(w_env_ref[...], joined_ref[0:LAT, :], preferred_element_type=F32)
-    for m in range(9):
-        vec_ref[m * CH : (m + 1) * CH, :] = weight if m == 0 else weight * shapes[m]
-    env_ref[...] = split_dot(vec_ref[...], same)
+    z3_ref[...] = jnp.dot(
+        w_lat_ref[:, 0:LAT], joined_ref[0:LAT, :], preferred_element_type=F32
+    )
+    weight_b = weight.astype(BF16)
+    sums = [jnp.dot(weight_b, link, preferred_element_type=F32) for link in links]
     for degree in range(3):
-        total = None
-        for m in range(9):
-            if DEGREE[m] == degree:
-                rows = slice(m * CH, (m + 1) * CH)
-                term = env_ref[rows, :] * vec_ref[rows, :]
-                total = term if total is None else total + term
-        joined_ref[LAT + degree * CH : LAT + (degree + 1) * CH, :] = total.astype(BF16)
-
-    z3_ref[...] = jnp.dot(w_lat_ref[...], joined_ref[...], preferred_element_type=F32)
+        rows = slice(LAT + degree * CH, LAT + (degree + 1) * CH)
+        joined_ref[rows, :] = (weight * sums[degree]).astype(BF16)
+
+    z3_ref[...] += jnp.dot(
+        w_lat_ref[:, LAT:], joined_ref[LAT:, :], preferred_element_type=F32
+    )
     energy = jnp.zeros((8, PAIRS), F32)
     cut_grad = jnp.zeros((8, PAIRS), F32)
     for start in range(0, LAT, ROWS):
@@ -242,23 +249,16 @@
         cut_grad = cut_grad + folded(readout * value)
         dz_ref[rows, :] = (readout * cut * gate).astype(BF16)
 
-    grad_ref[...] = jnp.dot(w_lat_t_ref[...], dz_ref[...], preferred_element_type=F32)
-    for m in range(9):
-        rows = slice(m * CH, (m + 1) * CH)
-        start = LAT + DEGREE[m] * CH
-        dvec_ref[rows, :] = grad_ref[start : start + CH, :] * vec_ref[rows, :]
-    dvec_ref[...] = split_dot(dvec_ref[...], same)
-    weight_grad = None
-    shape_grad = [None]
-    for m in range(9):
-        rows = slice(m * CH, (m + 1) * CH)
-        start = LAT + DEGREE[m] * CH
-        dvec = grad_ref[start : start + CH, :] * env_ref[rows, :] + dvec_ref[rows, :]
-        if m == 0:
-            weight_grad = dvec
-        else:
-            weight_grad = weight_grad + dvec * shapes[m]
-            shape_grad.append(column_sum(dvec * weight))
+    grad_ref[LAT:, :] = jnp.dot(w_lat_t_ref[LAT:, :], dz_ref[...], preferred_element_type=F32)
+    grad_ref[0:LAT, :] = jnp.dot(w_lat_t_ref[0:LAT, :], dz_ref[...], preferred_element_type=F32)
+    weight_grad = jnp.zeros_like(weight)
+    passes = []
+    for degree in range(3):
+        inv_grad = grad_ref[LAT + degree * CH : LAT + (degree + 1) * CH, :]
+        passed = (inv_grad * weight).astype(BF16)
+        weight_grad = weight_grad + inv_grad * sums[degree]
+        weight_grad = weight_grad + jnp.dot(passed, links[degree], preferred_element_type=F32)
+        passes.append(passed)
     dlat_ref[...] = jnp.dot(
         w_env_t_ref[...], weight_grad.astype(BF16), preferred_element_type=F32
     )
@@ -270,6 +270,15 @@
         dlat = readout + grad_ref[rows, :] + dlat_ref[rows, :]
         cut_grad = cut_grad + folded(dlat * value)
         dz_ref[rows, :] = (dlat * cut * gate).astype(BF16)
+    shape_grad = []
+    for degree in (1, 2):
+        passed = passes[degree]
+        both = dot_tn(
+            jnp.concatenate([weight_b, passed], axis=0),
+            jnp.concatenate([passed, weight_b], axis=0),
+        )
+        both = both.astype(BF16) * same
+        shape_grad.append(jnp.dot(shapes[degree - 1], both, preferred_element_type=F32))
     dlat_ref[...] = jnp.dot(w_hid_t_ref[...], dz_ref[...], preferred_element_type=F32)
     for start in range(0, LAT, ROWS):
         rows = pl.ds(start, ROWS)
@@ -278,7 +287,8 @@
 
     cut_grad = column_sum(cut_grad + feature_grad * bessel)
     radius_grad = cut_grad * slope + cut * column_sum(feature_grad * bessel_slope)
-    g1, g2, g3, g4, g5, g6, g7, g8 = shape_grad[1:]
+    g1, g2, g3 = [shape_grad[0][i : i + 1] for i in range(3)]
+    g4, g5, g6, g7, g8 = [shape_grad[1][i : i + 1] for i in range(5)]
     unit_grad = [
         ROOT3 * g1 + ROOT15 * (along_y * g4 + along_z * g7 + along_x * g8) - ROOT5 * along_x * g6,
         ROOT3 * g2 + ROOT15 * (along_x * g4 + along_z * g5 - along_y * g8) - ROOT5 * along_y * g6,
@@ -292,11 +302,8 @@
     axis = row & 3
     moved = jnp.where(axis == 0, push[0], jnp.where(axis == 1, push[1], push[2]))
     moved = jnp.where(axis == 3, 0.0, moved)
-    atom_row = lax.broadcasted_iota(jnp.int32, (ATOMS, PAIRS), 0)
-    hit_near = jnp.where(atom_row == atom, 1.0, 0.0).astype(BF16)
-    hit_own = jnp.where(atom_row == centre, 1.0, 0.0).astype(BF16)
-    spread = split_dot_nt(jnp.where((row >> 2) == slot, -moved, 0.0), hit_near)
-    home = split_dot_nt(moved[0:8], hit_own)[0:4]
+    spread = split_dot_nt(jnp.where((row >> 2) == slot, -moved, 0.0), hits_ref[0])
+    home = split_dot_nt(moved[0:8], hits_ref[1])[0:4]
     spread = spread.reshape(28, 4, ATOMS)
     energy = column_sum(energy)
     energy = energy[:, 0:ATOMS] + energy[:, ATOMS:PAIRS]
@@ -310,6 +317,28 @@
             if 9 * at_x + cell == 13:
                 block = block + home
             out_ref[number, cell] = block + blank
+
+
+def pair_forces(*operands):
+    vmem = pl.BlockSpec(memory_space=pltpu.VMEM)
+    return pl.pallas_call(
+        force_kernel,
+        out_shape=jax.ShapeDtypeStruct((RING, 9, 4, ATOMS), F32),
+        in_specs=[vmem] * 15,
+        out_specs=vmem,
+        scratch_shapes=[
+            pltpu.VMEM((LAT, PAIRS), F32),
+            pltpu.VMEM((LAT, PAIRS), F32),
+            pltpu.VMEM((LAT, PAIRS), F32),
+            pltpu.VMEM((LAT, PAIRS), BF16),
+            pltpu.VMEM((LAT + 3 * CH, PAIRS), BF16),
+            pltpu.VMEM((LAT + 3 * CH, PAIRS), F32),
+            pltpu.VMEM((LAT, PAIRS), BF16),
+            pltpu.VMEM((LAT, PAIRS), F32),
+        ],
+        compiler_params=pltpu.CompilerParams(vmem_limit_bytes=24 * 1024 * 1024),
+        name="forces_of_pairs",
+    )(*operands)
 
 
 SMALL = pltpu.CompilerParams(vmem_limit_bytes=2 * 1024 * 1024)
@@ -341,32 +370,23 @@
     even = lax.ppermute(plane, "gx", EVEN)
     odd = lax.ppermute(plane, "gx", ODD)
 
-    same = jnp.where(ids[0][:, None] == ids[0][None, :], ENV_NORM, 0.0).astype(BF16)
+    pairs, hits, same, readout = pl.pallas_call(
+        prepare_kernel,
+        out_shape=(
+            jax.ShapeDtypeStruct((8, PAIRS), jnp.int32),
+            jax.ShapeDtypeStruct((2, ATOMS, PAIRS), BF16),
+            jax.ShapeDtypeStruct((PAIRS, PAIRS), BF16),
+            jax.ShapeDtypeStruct((LAT, ATOMS), BF16),
+        ),
+        in_specs=[smem, vmem, vmem],
+        out_specs=(vmem,) * 4,
+        compiler_params=SMALL,
+        name="prepare_pairs",
+    )(counts, ids, w_out)
     w_in = jnp.pad(w_two_in, ((0, 0), (0, 4)))
-    readout = jnp.broadcast_to(w_out.reshape(LAT, 1), (LAT, ATOMS))
-    sent = pl.pallas_call(
-        force_kernel,
-        out_shape=jax.ShapeDtypeStruct((RING, 9, 4, ATOMS), F32),
-        in_specs=[smem] + [vmem] * 14,
-        out_specs=vmem,
-        scratch_shapes=[
-            pltpu.VMEM((LAT, PAIRS), F32),
-            pltpu.VMEM((LAT, PAIRS), F32),
-            pltpu.VMEM((LAT, PAIRS), F32),
-            pltpu.VMEM((LAT, PAIRS), BF16),
-            pltpu.VMEM((LAT + 3 * CH, PAIRS), BF16),
-            pltpu.VMEM((LAT + 3 * CH, PAIRS), F32),
-            pltpu.VMEM((LAT, PAIRS), BF16),
-            pltpu.VMEM((9 * CH, PAIRS), F32),
-            pltpu.VMEM((9 * CH, PAIRS), F32),
-            pltpu.VMEM((9 * CH, PAIRS), F32),
-            pltpu.VMEM((LAT, PAIRS), F32),
-        ],
-        compiler_params=pltpu.CompilerParams(vmem_limit_bytes=24 * 1024 * 1024),
-        name="forces_of_pairs",
-    )(
-        counts,
-        ids,
+    sent = pair_forces(
+        pairs,
+        hits,
         even,
         plane,
         odd,

time: 72.7 us -> 70.5 us (0.970)
  blocking collectives: 29.6 us -> 54.8 us
  starting transfers between devices: 22 us -> 7.15 us
  waiting for transfers between devices: 11 us -> 0.29 us
  Pallas kernels: 5.39 us -> 4.35 us
    all_to_all x0 -> x1, blocking collectives: none -> 25.2 us  [body(): lax.all_to_all(packed, ('gy', 'gz'), 0, 0)]
    all_to_all x1 -> x0, starting transfers between devices: 14.8 us -> none  [body(): lax.all_to_all(packed, ('gy', 'gz'), 0, 0)]
    all_to_all x1 -> x0, waiting for transfers between devices: 9.72 us -> none  [body(): lax.all_to_all(packed, ('gy', 'gz'), 0, 0)]
    ppermute x1, waiting for transfers between devices: 1.28 us -> 0.29 us  [body(): even = lax.ppermute(plane, 'gx', EVEN)]
    pallas_call x1 -> x2, Pallas kernels: 3.98 us -> 3.58 us  [the longest x1 2.86 us: pair_forces(): pl.pallas_call(force_kernel, out_shape=jax.ShapeDtypeStruct((RING, 9, 4,...]
  transfers between devices with their start and end apart: 3 -> 2, of which waited for: 2 -> 1; matrix products, arithmetic and copies ran while one was open for 2% -> 1% of each run, Pallas kernels for 0% -> 1%
where the time goes in v4:
time: 70.5 us; the launch traced here: 70.1 us
  blocking collectives  54.8 us (78%)
  starting transfers between devices  7.15 us (10%)
  Pallas kernels  4.35 us (6%)
  local copies, waits for them, and re-layouts  2.8 us (4%)
  between operations  0.79 us (1%)
    all_to_all x1, blocking collectives, body(): lax.all_to_all(packed, ('gy', 'gz'), 0, 0)  25.2 us
    all_to_all x1, blocking collectives, body(): lax.all_to_all(addressed, ('gy', 'gz'), 0, 0)  17.4 us
    all_to_all x1, blocking collectives, body(): lax.all_to_all(sent, 'gx', 0, 0)  12.1 us
    ppermute x1, starting transfers between devices, body(): odd = lax.ppermute(plane, 'gx', ODD)  5.23 us
    pallas_call x1, Pallas kernels, pair_forces(): pl.pallas_call(force_kernel, out_shape=jax.ShapeDtypeStruct((RING, 9, 4,...  2.86 us
    unnamed x22, local copies, waits for them, and re-layouts  2.77 us
    ppermute x1, starting transfers between devices, body(): even = lax.ppermute(plane, 'gx', EVEN)  1.92 us
  transfers between devices with their start and end apart: 2, of which 1 were waited for; matrix products, arithmetic and copies ran while one was open for 1% of the time, Pallas kernels for 1%

profile of v4, /device:TPU:1, one launch (start us, length us, event | category | flops | bytes accessed | tf_op | source)
XLA Modules:
  0.0 70.1 jit_solution(10167227136143315236)
XLA Ops:
  0.6 0.0 copy-start.5
  0.6 0.0 copy-start.1
  0.6 0.7 copy-done.5
  1.3 0.0 copy-start.6
  1.3 0.7 copy-done.6
  2.0 0.0 copy-start.8
  2.0 25.2 %all_to_all.15.received_ref = f32[64,4,128]{2,1,0:T(4,128)S(1)} all-to-all(f32[64,4,128]{2,1,0:T(4,128)S(1)} %pack_frame.1), channel_id=1, replica_groups=mesh['gx'=8,'gy'=8,'gz'=8] {'gy','gz'}, dimensions={0} | all-to-all | bytes 262144 | tf_op jit(solution)/shard_map/all_to_all | solution.py:369
  27.2 0.0 copy-start.2
  27.2 0.0 copy-start
  27.2 5.2 %collective-permute-start.1 = (f32[9,4,128]{2,1,0:T(4,128)S(1)}, f32[9,4,128]{2,1,0:T(4,128)S(1)}, u32[]{:S(2)}, u32[]{:S(2)}) collective-permute-start(f32[9,4,128]{2,1,0:T(4,128)S(1)} %pick_plane.1.level_ref), channel_id=1, source_target_pairs={{0,448},{64,128},{128,64},{192,256},{256,192},{320,384},{384,320},... | collective-permute-start | bytes 55304 | tf_op jit(solution)/shard_map/ppermute | solution.py:371
  32.4 1.9 %collective-permute-start = (f32[9,4,128]{2,1,0:T(4,128)S(1)}, f32[9,4,128]{2,1,0:T(4,128)S(1)}, u32[]{:S(2)}, u32[]{:S(2)}) collective-permute-start(f32[9,4,128]{2,1,0:T(4,128)S(1)} %pick_plane.1.level_ref), channel_id=1, source_target_pairs={{0,64},{64,0},{128,192},{192,128},{256,320},{320,256},{384,448},{4... | collective-permute-start | bytes 55304 | tf_op jit(solution)/shard_map/ppermute | solution.py:370
  34.4 0.0 copy-done.8
  34.4 0.2 copy.16
  34.5 0.0 copy-done.2
  34.5 0.1 copy.12
  34.7 0.0 copy-done.1
  34.7 0.2 copy.11
  34.9 0.0 copy-done
  34.9 0.3 copy.14.w_lat_ref
  35.2 0.0 copy-start.4
  35.2 0.0 copy-start.3
  35.2 0.0 copy-start.7
  35.3 0.6 copy-done.4
  35.9 0.0 copy-done.3
  35.9 0.0 copy-done.7
  35.9 0.7 %prepare_pairs.1 = (s32[8,256]{1,0:T(8,128)S(1)}, bf16[2,128,256]{2,1,0:T(8,128)(2,1)S(1)}, bf16[256,256]{1,0:T(8,128)(2,1)S(1)}, bf16[512,128]{1,0:T(8,128)(2,1)S(1)}) custom-call(s32[2]{0:T(128)S(1)} %bitcast.19, s32[2,256]{1,0:T(2,128)S(1)} %bitcast.16, bf16[1,512]{1,0:T(2,128)(2,1)S(1)} %copy-done.4), custom_call_target="tpu_custom_call" | custom-call | tf_op jit(solution)/shard_map/prepare_pairs/pallas_call | solution.py:373
  36.6 0.0 collective-permute-done.1.odd_ref
  36.7 0.3 collective-permute-done.even_ref
  36.9 2.9 %forces_of_pairs.1 = f32[8,9,4,128]{3,2,1,0:T(4,128)S(1)} custom-call(s32[8,256]{1,0:T(8,128)S(1)} %get-tuple-element.8.pairs_ref, bf16[2,128,256]{2,1,0:T(8,128)(2,1)S(1)} %get-tuple-element.9.hits_ref, f32[9,4,128]{2,1,0:T(4,128)S(1)} %collective-permute-done.even_ref, f32[9,4,128]{2,1,0:T(4,128)S(1)} %pick_plane.1.level_ref, ...), custom_call_target="tpu_custom_call" | custom-call | tf_op jit(solution)/shard_map/forces_of_pairs/pallas_call | solution.py:324
  39.8 12.1 %all_to_all.16.received_ref = f32[8,9,4,128]{3,2,1,0:T(4,128)S(1)} all-to-all(f32[8,9,4,128]{3,2,1,0:T(4,128)S(1)} %forces_of_pairs.1), channel_id=1, replica_groups=mesh['gx'=8,'gy'=8,'gz'=8] {'gx'}, dimensions={0} | all-to-all | bytes 294912 | tf_op jit(solution)/shard_map/all_to_all | solution.py:411
  52.0 17.4 %all_to_all.17.received_ref = f32[64,4,128]{2,1,0:T(4,128)S(1)} all-to-all(f32[64,4,128]{2,1,0:T(4,128)S(1)} %address_plane.1), channel_id=1, replica_groups=mesh['gx'=8,'gy'=8,'gz'=8] {'gy','gz'}, dimensions={0} | all-to-all | bytes 262144 | tf_op jit(solution)/shard_map/all_to_all | solution.py:419
  69.4 0.7 %finish.1 = (f32[3,1,128]{2,1,0:T(1,128)}, f32[1]{0:T(128)}) custom-call(f32[64,4,128]{2,1,0:T(4,128)S(1)} %all_to_all.17.received_ref), custom_call_target="tpu_custom_call" | custom-call | tf_op jit(solution)/shard_map/finish/pallas_call | solution.py:412
  (5 shorter events, 0.1 us)
Async XLA Ops:
  0.6 0.7 copy-start.5
  0.6 34.0 %copy-start.1 = (bf16[512,512]{1,0:T(8,128)(2,1)S(1)}, bf16[512,512]{1,0:T(8,128)(2,1)}, u32[]{:S(2)}) copy-start(bf16[512,512]{1,0:T(8,128)(2,1)} %w_hid_ref.1) | copy-start | bytes 1572868
  1.3 0.7 copy-start.6
  2.0 32.4 %copy-start.8 = (bf16[512,12]{0,1:T(8,128)(2,1)S(1)}, bf16[512,12]{0,1:T(8,128)(2,1)}, u32[]{:S(2)}) copy-start(bf16[512,12]{0,1:T(8,128)(2,1)} %param.13) | copy-start | bytes 36868
  27.2 7.4 %copy-start.2 = (bf16[64,512]{1,0:T(8,128)(2,1)S(1)}, bf16[64,512]{1,0:T(8,128)(2,1)}, u32[]{:S(2)}) copy-start(bf16[64,512]{1,0:T(8,128)(2,1)} %w_env_ref.1) | copy-start | bytes 196612
  27.2 7.7 %copy-start = (bf16[512,704]{0,1:T(8,128)(2,1)S(1)}, bf16[512,704]{0,1:T(8,128)(2,1)}, u32[]{:S(2)}) copy-start(bf16[512,704]{0,1:T(8,128)(2,1)} %param.16) | copy-start | bytes 2162692
  27.2 9.4 %collective-permute-start.1 = (f32[9,4,128]{2,1,0:T(4,128)S(1)}, f32[9,4,128]{2,1,0:T(4,128)S(1)}, u32[]{:S(2)}, u32[]{:S(2)}) collective-permute-start(f32[9,4,128]{2,1,0:T(4,128)S(1)} %pick_plane.1.level_ref), channel_id=1, source_target_pairs={{0,448},{64,128},{128,64},{192,256},{256,192},{320,384},{384,320},... | collective-permute-start | bytes 55304 | tf_op jit(solution)/shard_map/ppermute | solution.py:371
  32.4 4.5 %collective-permute-start = (f32[9,4,128]{2,1,0:T(4,128)S(1)}, f32[9,4,128]{2,1,0:T(4,128)S(1)}, u32[]{:S(2)}, u32[]{:S(2)}) collective-permute-start(f32[9,4,128]{2,1,0:T(4,128)S(1)} %pick_plane.1.level_ref), channel_id=1, source_target_pairs={{0,64},{64,0},{128,192},{192,128},{256,320},{320,256},{384,448},{4... | collective-permute-start | bytes 55304 | tf_op jit(solution)/shard_map/ppermute | solution.py:370
  35.2 0.7 copy-start.4
  35.2 0.7 copy-start.3
  35.2 0.7 copy-start.7

commit v5 on v4

--- a/solution.py
+++ b/solution.py
@@ -52,10 +52,8 @@
     )
 
 
-def pack_kernel(coords_ref, species_ref, out_ref):
-    rows = [coords_ref[axis] for axis in range(3)] + [species_ref[...].astype(F32)]
-    block = jnp.concatenate(rows, axis=0)
-    out_ref[...] = jnp.broadcast_to(block[None], out_ref.shape)
+def pack_kernel(frame_ref, out_ref):
+    out_ref[...] = jnp.broadcast_to(frame_ref[...][None], out_ref.shape)
 
 
 def around():
@@ -354,11 +352,11 @@
     packed = pl.pallas_call(
         pack_kernel,
         out_shape=jax.ShapeDtypeStruct((RING * RING, 4, ATOMS), F32),
-        in_specs=[vmem] * 2,
+        in_specs=[vmem],
         out_specs=vmem,
         compiler_params=SMALL,
         name="pack_frame",
-    )(coords.reshape(3, 1, ATOMS), species.reshape(1, ATOMS))
+    )(jnp.concatenate([coords[0, 0, 0], species[0, 0, 0].astype(F32)[None]], axis=0))
     plane = pl.pallas_call(
         pick_kernel,
         out_shape=jax.ShapeDtypeStruct((9, 4, ATOMS), F32),

time: 70.5 us -> 69.9 us (level)
  local copies, waits for them, and re-layouts: 2.8 us -> 1.49 us
  other arithmetic: 0 us -> 0.73 us
    unnamed x22 -> x21, local copies, waits for them, and re-layouts: 2.77 us -> 1.45 us
    convert_element_type x0 -> x1, other arithmetic: none -> 0.72 us  [body(): species[0, 0, 0].astype(F32)[None]]
where the time goes in v5:
time: 69.9 us; the launch traced here: 69.6 us
  blocking collectives  54.8 us (78%)
  starting transfers between devices  7.15 us (10%)
  Pallas kernels  4.35 us (6%)
  local copies, waits for them, and re-layouts  1.49 us (2%)
  between operations  0.79 us (1%)
  other arithmetic  0.73 us (1%)
    all_to_all x1, blocking collectives, body(): lax.all_to_all(packed, ('gy', 'gz'), 0, 0)  25.2 us
    all_to_all x1, blocking collectives, body(): lax.all_to_all(addressed, ('gy', 'gz'), 0, 0)  17.5 us
    all_to_all x1, blocking collectives, body(): lax.all_to_all(sent, 'gx', 0, 0)  12.2 us
    ppermute x1, starting transfers between devices, body(): odd = lax.ppermute(plane, 'gx', ODD)  5.23 us
    pallas_call x1, Pallas kernels, pair_forces(): pl.pallas_call(force_kernel, out_shape=jax.ShapeDtypeStruct((RING, 9, 4,...  2.85 us
    ppermute x1, starting transfers between devices, body(): even = lax.ppermute(plane, 'gx', EVEN)  1.92 us
    unnamed x21, local copies, waits for them, and re-layouts  1.45 us
  transfers between devices with their start and end apart: 2, of which 1 were waited for; matrix products, arithmetic and copies ran while one was open for 1% of the time, Pallas kernels for 1%

profile of v5, /device:TPU:1, one launch (start us, length us, event | category | flops | bytes accessed | tf_op | source)
XLA Modules:
  0.0 69.6 jit_solution(18164307559975918345)
XLA Ops:
  0.6 0.0 copy-start.7
  0.6 0.0 copy-start.1
  0.6 0.7 %convert_bitcast_fusion = f32[1,128]{1,0:T(1,128)S(1)} fusion(s32[1,1,1,128]{3,2,1,0:T(1,128)} %param.10), kind=kLoop, calls=%fused_computation.2 | loop fusion | flops 128 | bytes 1024 | tf_op jit(solution)/shard_map/convert_element_type | solution.py:359
  1.4 0.0 copy-done.7
  1.4 0.0 copy-start.6
  1.4 25.2 %all_to_all.15.received_ref = f32[64,4,128]{2,1,0:T(4,128)S(1)} all-to-all(f32[64,4,128]{2,1,0:T(4,128)S(1)} %pack_frame.1), channel_id=1, replica_groups=mesh['gx'=8,'gy'=8,'gz'=8] {'gy','gz'}, dimensions={0} | all-to-all | bytes 262144 | tf_op jit(solution)/shard_map/all_to_all | solution.py:367
  26.6 0.0 copy-start.2
  26.6 0.0 copy-start
  26.6 5.2 %collective-permute-start.1 = (f32[9,4,128]{2,1,0:T(4,128)S(1)}, f32[9,4,128]{2,1,0:T(4,128)S(1)}, u32[]{:S(2)}, u32[]{:S(2)}) collective-permute-start(f32[9,4,128]{2,1,0:T(4,128)S(1)} %pick_plane.1.level_ref), channel_id=1, source_target_pairs={{0,448},{64,128},{128,64},{192,256},{256,192},{320,384},{384,320},... | collective-permute-start | bytes 55304 | tf_op jit(solution)/shard_map/ppermute | solution.py:369
  31.9 1.9 %collective-permute-start = (f32[9,4,128]{2,1,0:T(4,128)S(1)}, f32[9,4,128]{2,1,0:T(4,128)S(1)}, u32[]{:S(2)}, u32[]{:S(2)}) collective-permute-start(f32[9,4,128]{2,1,0:T(4,128)S(1)} %pick_plane.1.level_ref), channel_id=1, source_target_pairs={{0,64},{64,0},{128,192},{192,128},{256,320},{320,256},{384,448},{4... | collective-permute-start | bytes 55304 | tf_op jit(solution)/shard_map/ppermute | solution.py:368
  33.8 0.0 copy-done.6
  33.8 0.2 copy.18
  34.0 0.0 copy-done.2
  34.0 0.1 copy.12
  34.1 0.0 copy-done.1
  34.1 0.2 copy.11
  34.3 0.0 copy-done
  34.3 0.3 copy.14.w_lat_ref
  34.6 0.0 copy-start.4
  34.6 0.0 copy-start.3
  34.7 0.0 copy-start.5
  34.7 0.6 copy-done.4
  35.3 0.0 copy-done.3
  35.3 0.0 copy-done.5
  35.3 0.7 %prepare_pairs.1 = (s32[8,256]{1,0:T(8,128)S(1)}, bf16[2,128,256]{2,1,0:T(8,128)(2,1)S(1)}, bf16[256,256]{1,0:T(8,128)(2,1)S(1)}, bf16[512,128]{1,0:T(8,128)(2,1)S(1)}) custom-call(s32[2]{0:T(128)S(1)} %bitcast.20, s32[2,256]{1,0:T(2,128)S(1)} %bitcast.19, bf16[1,512]{1,0:T(2,128)(2,1)S(1)} %copy-done.4), custom_call_target="tpu_custom_call" | custom-call | tf_op jit(solution)/shard_map/prepare_pairs/pallas_call | solution.py:371
  36.1 0.0 collective-permute-done.1.odd_ref
  36.1 0.3 collective-permute-done.even_ref
  36.4 2.9 %forces_of_pairs.1 = f32[8,9,4,128]{3,2,1,0:T(4,128)S(1)} custom-call(s32[8,256]{1,0:T(8,128)S(1)} %get-tuple-element.8.pairs_ref, bf16[2,128,256]{2,1,0:T(8,128)(2,1)S(1)} %get-tuple-element.9.hits_ref, f32[9,4,128]{2,1,0:T(4,128)S(1)} %collective-permute-done.even_ref, f32[9,4,128]{2,1,0:T(4,128)S(1)} %pick_plane.1.level_ref, ...), custom_call_target="tpu_custom_call" | custom-call | tf_op jit(solution)/shard_map/forces_of_pairs/pallas_call | solution.py:322
  39.2 12.2 %all_to_all.16.received_ref = f32[8,9,4,128]{3,2,1,0:T(4,128)S(1)} all-to-all(f32[8,9,4,128]{3,2,1,0:T(4,128)S(1)} %forces_of_pairs.1), channel_id=1, replica_groups=mesh['gx'=8,'gy'=8,'gz'=8] {'gx'}, dimensions={0} | all-to-all | bytes 294912 | tf_op jit(solution)/shard_map/all_to_all | solution.py:409
  51.4 17.5 %all_to_all.17.received_ref = f32[64,4,128]{2,1,0:T(4,128)S(1)} all-to-all(f32[64,4,128]{2,1,0:T(4,128)S(1)} %address_plane.1), channel_id=1, replica_groups=mesh['gx'=8,'gy'=8,'gz'=8] {'gy','gz'}, dimensions={0} | all-to-all | bytes 262144 | tf_op jit(solution)/shard_map/all_to_all | solution.py:417
  68.9 0.7 %finish.1 = (f32[3,1,128]{2,1,0:T(1,128)}, f32[1]{0:T(128)}) custom-call(f32[64,4,128]{2,1,0:T(4,128)S(1)} %all_to_all.17.received_ref), custom_call_target="tpu_custom_call" | custom-call | tf_op jit(solution)/shard_map/finish/pallas_call | solution.py:410
  (7 shorter events, 0.1 us)
Async XLA Ops:
  0.6 0.7 %copy-start.7 = (f32[1,1,1,3,128]{4,2,3,1,0:T(1,128)S(1)}, f32[1,1,1,3,128]{4,2,3,1,0:T(1,128)}, u32[]{:S(2)}) copy-start(f32[1,1,1,3,128]{4,2,3,1,0:T(1,128)} %param.9) | copy-start | bytes 4612
  0.6 33.4 %copy-start.1 = (bf16[512,512]{1,0:T(8,128)(2,1)S(1)}, bf16[512,512]{1,0:T(8,128)(2,1)}, u32[]{:S(2)}) copy-start(bf16[512,512]{1,0:T(8,128)(2,1)} %w_hid_ref.1) | copy-start | bytes 1572868
  1.4 32.4 %copy-start.6 = (bf16[512,12]{0,1:T(8,128)(2,1)S(1)}, bf16[512,12]{0,1:T(8,128)(2,1)}, u32[]{:S(2)}) copy-start(bf16[512,12]{0,1:T(8,128)(2,1)} %param.13) | copy-start | bytes 36868
  26.6 7.4 %copy-start.2 = (bf16[64,512]{1,0:T(8,128)(2,1)S(1)}, bf16[64,512]{1,0:T(8,128)(2,1)}, u32[]{:S(2)}) copy-start(bf16[64,512]{1,0:T(8,128)(2,1)} %w_env_ref.1) | copy-start | bytes 196612
  26.6 7.7 %copy-start = (bf16[512,704]{0,1:T(8,128)(2,1)S(1)}, bf16[512,704]{0,1:T(8,128)(2,1)}, u32[]{:S(2)}) copy-start(bf16[512,704]{0,1:T(8,128)(2,1)} %param.16) | copy-start | bytes 2162692
  26.6 9.4 %collective-permute-start.1 = (f32[9,4,128]{2,1,0:T(4,128)S(1)}, f32[9,4,128]{2,1,0:T(4,128)S(1)}, u32[]{:S(2)}, u32[]{:S(2)}) collective-permute-start(f32[9,4,128]{2,1,0:T(4,128)S(1)} %pick_plane.1.level_ref), channel_id=1, source_target_pairs={{0,448},{64,128},{128,64},{192,256},{256,192},{320,384},{384,320},... | collective-permute-start | bytes 55304 | tf_op jit(solution)/shard_map/ppermute | solution.py:369
  31.9 4.5 %collective-permute-start = (f32[9,4,128]{2,1,0:T(4,128)S(1)}, f32[9,4,128]{2,1,0:T(4,128)S(1)}, u32[]{:S(2)}, u32[]{:S(2)}) collective-permute-start(f32[9,4,128]{2,1,0:T(4,128)S(1)} %pick_plane.1.level_ref), channel_id=1, source_target_pairs={{0,64},{64,0},{128,192},{192,128},{256,320},{320,256},{384,448},{4... | collective-permute-start | bytes 55304 | tf_op jit(solution)/shard_map/ppermute | solution.py:368
  34.6 0.7 copy-start.4
  34.6 0.7 copy-start.3
  34.7 0.7 copy-start.5

commit v6 on v5

--- a/solution.py
+++ b/solution.py
@@ -16,7 +16,6 @@
 ROOT3 = math.sqrt(3.0)
 ROOT5 = math.sqrt(5.0)
 ROOT15 = math.sqrt(15.0)
-DEGREE = (0, 1, 1, 1, 2, 2, 2, 2, 2)
 RING = 8
 LAT = 512
 CH = 64
@@ -54,6 +53,11 @@
 
 def pack_kernel(frame_ref, out_ref):
     out_ref[...] = jnp.broadcast_to(frame_ref[...][None], out_ref.shape)
+
+
+def place_of():
+    at_z = lax.axis_index("gz")
+    return lax.axis_index("gx"), lax.axis_index("gy"), at_z >> 1, at_z & 1
 
 
 def around():
@@ -65,9 +69,37 @@
     ]
 
 
-def pick_kernel(received_ref, out_ref):
-    for cell, number in enumerate(around()):
-        out_ref[cell] = received_ref[number]
+def relay_kernel(near_ref, out_ref):
+    at_x, at_y, chip, high = place_of()
+    own, other = (at_x & 1) * 16, (1 - (at_x & 1)) * 16
+    side = 1 - (at_x & 1)
+    out_ref[...] = jnp.zeros(out_ref.shape, F32)
+    chip_third = (chip + 5 - 2 * high) & 3
+    for row in range(3):
+        number = ((at_y + (RING - 1 + row)) & (RING - 1)) * 2
+        for level in range(2):
+            out_ref[(1 - side) * 4 + chip, 2 * row + level] = near_ref[own + number + level]
+        for to in (side, 1 - side):
+            out_ref[to * 4 + chip_third, row] = near_ref[own + number + 1 - high]
+            out_ref[to * 4 + chip_third, 3 + row] = near_ref[other + number + 1 - high]
+
+
+def pick_kernel(near_ref, far_ref, even_ref, level_ref, odd_ref):
+    at_x, at_y, chip, high = place_of()
+    own, other = (at_x & 1) * 16, (1 - (at_x & 1)) * 16
+    side = 1 - (at_x & 1)
+    chip_third = (chip + 3 + 2 * high) & 3
+    for row in range(3):
+        number = ((at_y + (RING - 1 + row)) & (RING - 1)) * 2
+        for level in range(2):
+            cell = 3 * row + 1 + level - high
+            level_ref[cell] = near_ref[own + number + level]
+            even_ref[cell] = near_ref[other + number + level]
+            odd_ref[cell] = far_ref[(1 - side) * 4 + chip, 2 * row + level]
+        cell = 3 * row + 2 * high
+        level_ref[cell] = far_ref[side * 4 + chip_third, row]
+        even_ref[cell] = far_ref[side * 4 + chip_third, 3 + row]
+        odd_ref[cell] = far_ref[(1 - side) * 4 + chip_third, row]
 
 
 def address_kernel(received_ref, out_ref):
@@ -340,8 +372,24 @@
 
 
 SMALL = pltpu.CompilerParams(vmem_limit_bytes=2 * 1024 * 1024)
-EVEN = [(i, i ^ 1) for i in range(RING)]
-ODD = [(i, (((i + 1) ^ 1) - 1) % RING) for i in range(RING)]
+AXES = ("gx", "gy", "gz")
+
+
+def flat(at_x, at_y, chip, high):
+    return ((at_x % RING) * RING + at_y) * RING + 2 * chip + high
+
+
+NEAR = [
+    [flat(2 * pair + i, at_y, chip, high) for i in range(2) for at_y in range(8) for high in range(2)]
+    for pair in range(4)
+    for chip in range(4)
+]
+FAR = [
+    [flat(2 * pair + 1 + i, at_y, chip, high) for i in range(2) for chip in range(4)]
+    for pair in range(4)
+    for at_y in range(8)
+    for high in range(2)
+]
 
 
 def body(coords, species, pair_ids, live_counts, w_two_in, w_two_hid, w_env, w_latent, w_out):
@@ -351,22 +399,30 @@
     smem = pl.BlockSpec(memory_space=pltpu.SMEM)
     packed = pl.pallas_call(
         pack_kernel,
-        out_shape=jax.ShapeDtypeStruct((RING * RING, 4, ATOMS), F32),
+        out_shape=jax.ShapeDtypeStruct((32, 4, ATOMS), F32),
         in_specs=[vmem],
         out_specs=vmem,
         compiler_params=SMALL,
         name="pack_frame",
     )(jnp.concatenate([coords[0, 0, 0], species[0, 0, 0].astype(F32)[None]], axis=0))
-    plane = pl.pallas_call(
-        pick_kernel,
-        out_shape=jax.ShapeDtypeStruct((9, 4, ATOMS), F32),
+    near = lax.all_to_all(packed, AXES, 0, 0, axis_index_groups=NEAR)
+    relayed = pl.pallas_call(
+        relay_kernel,
+        out_shape=jax.ShapeDtypeStruct((8, 6, 4, ATOMS), F32),
         in_specs=[vmem],
         out_specs=vmem,
         compiler_params=SMALL,
-        name="pick_plane",
-    )(lax.all_to_all(packed, ("gy", "gz"), 0, 0))
-    even = lax.ppermute(plane, "gx", EVEN)
-    odd = lax.ppermute(plane, "gx", ODD)
+        name="relay_frames",
+    )(near)
+    far = lax.all_to_all(relayed, AXES, 0, 0, axis_index_groups=FAR)
+    even, plane, odd = pl.pallas_call(
+        pick_kernel,
+        out_shape=(jax.ShapeDtypeStruct((9, 4, ATOMS), F32),) * 3,
+        in_specs=[vmem] * 2,
+        out_specs=(vmem,) * 3,
+        compiler_params=SMALL,
+        name="pick_planes",
+    )(near, far)
 
     pairs, hits, same, readout = pl.pallas_call(
         prepare_kernel,

time: 69.9 us -> 68.9 us (0.986)
  blocking collectives: 54.8 us -> 51.7 us
  waiting for transfers between devices: 0.29 us -> 1.41 us
    ppermute x2 -> x0, starting transfers between devices: 7.15 us -> none  [the longest x1 5.23 us: body(): odd = lax.ppermute(plane, 'gx', ODD)]
    all_to_all x0 -> x1, starting transfers between devices: none -> 6.77 us  [body(): far = lax.all_to_all(relayed, AXES, 0, 0, axis_index_groups=FAR)]
    all_to_all x1, blocking collectives: 25.2 us -> 20.7 us  [body(): near = lax.all_to_all(packed, AXES, 0, 0, axis_index_groups=NEAR)]
    all_to_all x1, blocking collectives: 12.2 us -> 13.7 us  [body(): lax.all_to_all(sent, 'gx', 0, 0)]
    all_to_all x0 -> x1, waiting for transfers between devices: none -> 1.41 us  [body(): far = lax.all_to_all(relayed, AXES, 0, 0, axis_index_groups=FAR)]
  transfers between devices with their start and end apart: 2 -> 1, of which waited for: 1 -> 1; matrix products, arithmetic and copies ran while one was open for 1% -> 1% of each run, Pallas kernels for 1% -> 1%
where the time goes in v6:
time: 68.9 us; the launch traced here: 68.4 us
  blocking collectives  51.7 us (75%)
  starting transfers between devices  6.77 us (10%)
  Pallas kernels  5.01 us (7%)
  local copies, waits for them, and re-layouts  2.08 us (3%)
  waiting for transfers between devices  1.41 us (2%)
  between operations  0.74 us (1%)
  other arithmetic  0.73 us (1%)
    all_to_all x1, blocking collectives, body(): near = lax.all_to_all(packed, AXES, 0, 0, axis_index_groups=NEAR)  20.7 us
    all_to_all x1, blocking collectives, body(): lax.all_to_all(addressed, ('gy', 'gz'), 0, 0)  17.3 us
    all_to_all x1, blocking collectives, body(): lax.all_to_all(sent, 'gx', 0, 0)  13.7 us
    all_to_all x1, starting transfers between devices, body(): far = lax.all_to_all(relayed, AXES, 0, 0, axis_index_groups=FAR)  6.77 us
    pallas_call x1, Pallas kernels, pair_forces(): pl.pallas_call(force_kernel, out_shape=jax.ShapeDtypeStruct((RING, 9, 4,...  2.85 us
    unnamed x21, local copies, waits for them, and re-layouts  2.05 us
    all_to_all x1, waiting for transfers between devices, body(): far = lax.all_to_all(relayed, AXES, 0, 0, axis_index_groups=FAR)  1.41 us
  transfers between devices with their start and end apart: 1, of which 1 were waited for; matrix products, arithmetic and copies ran while one was open for 1% of the time, Pallas kernels for 1%

profile of v6, /device:TPU:1, one launch (start us, length us, event | category | flops | bytes accessed | tf_op | source)
XLA Modules:
  0.0 68.4 jit_solution(11637153645136736195)
XLA Ops:
  0.6 0.0 copy-start.7
  0.6 0.0 copy-start.1
  0.6 0.7 %convert_bitcast_fusion = f32[1,128]{1,0:T(1,128)S(1)} fusion(s32[1,1,1,128]{3,2,1,0:T(1,128)} %param.10), kind=kLoop, calls=%fused_computation.2 | loop fusion | flops 128 | bytes 1024 | tf_op jit(solution)/shard_map/convert_element_type | solution.py:407
  1.4 0.0 copy-done.7
  1.4 20.7 %all_to_all.20.near_ref = f32[32,4,128]{2,1,0:T(4,128)S(1)} all-to-all(f32[32,4,128]{2,1,0:T(4,128)S(1)} %pack_frame.1), channel_id=1, replica_groups={{0,1,8,9,16,17,24,25,32,33,40,41,48,49,56,57,64,65,72,73,80,81,88,89,96..., dimensions={0} | all-to-all | bytes 131072 | tf_op jit(solution)/shard_map/all_to_all | solution.py:408
  22.1 0.0 copy-start.6
  22.1 0.7 relay_frames.1
  22.8 0.0 copy-start.2
  22.8 6.8 %all-to-all-start.1 = ((f32[8,6,4,128]{3,2,1,0:T(4,128)}), f32[8,6,4,128]{3,2,1,0:T(4,128)S(1)}, u32[]{:S(2)}, u32[]{:S(2)}) async-start(f32[8,6,4,128]{3,2,1,0:T(4,128)} %relay_frames.1), calls=%async_computation.1 | async-start | bytes 196608 | tf_op jit(solution)/shard_map/all_to_all | solution.py:417
  29.6 0.0 copy-done.6
  29.6 0.0 copy-start
  29.6 0.2 copy.18
  29.7 0.0 copy-done.2
  29.7 0.1 copy.12
  29.9 0.0 copy-done.1
  29.9 0.2 copy.11
  30.1 0.6 copy-done
  30.7 0.3 copy.14.w_lat_ref
  31.0 0.0 copy-start.4
  31.0 0.0 copy-start.3
  31.0 0.0 copy-start.5
  31.1 0.6 copy-done.4
  31.7 0.0 copy-done.3
  31.7 0.0 copy-done.5
  31.7 0.7 %prepare_pairs.1 = (s32[8,256]{1,0:T(8,128)S(1)}, bf16[2,128,256]{2,1,0:T(8,128)(2,1)S(1)}, bf16[256,256]{1,0:T(8,128)(2,1)S(1)}, bf16[512,128]{1,0:T(8,128)(2,1)S(1)}) custom-call(s32[2]{0:T(128)S(1)} %bitcast.20, s32[2,256]{1,0:T(2,128)S(1)} %bitcast.19, bf16[1,512]{1,0:T(2,128)(2,1)S(1)} %copy-done.4), custom_call_target="tpu_custom_call" | custom-call | tf_op jit(solution)/shard_map/prepare_pairs/pallas_call | solution.py:427
  32.4 1.4 %all-to-all-done.1.far_ref = f32[8,6,4,128]{3,2,1,0:T(4,128)S(1)} async-done(((f32[8,6,4,128]{3,2,1,0:T(4,128)}), f32[8,6,4,128]{3,2,1,0:T(4,128)S(1)}, u32[]{:S(2)}, u32[]{:S(2)}) %all-to-all-start.1) | async-done | bytes 98336 | tf_op jit(solution)/shard_map/all_to_all | solution.py:417
  33.9 2.9 %forces_of_pairs.1 = f32[8,9,4,128]{3,2,1,0:T(4,128)S(1)} custom-call(s32[8,256]{1,0:T(8,128)S(1)} %get-tuple-element.11.pairs_ref, bf16[2,128,256]{2,1,0:T(8,128)(2,1)S(1)} %get-tuple-element.12.hits_ref, f32[9,4,128]{2,1,0:T(4,128)S(1)} %get-tuple-element.13.even_ref, f32[9,4,128]{2,1,0:T(4,128)S(1)} %get-tuple-element.14.level_ref, ...), custom_call_target="tpu_custom_call" | custom-call | tf_op jit(solution)/shard_map/forces_of_pairs/pallas_call | solution.py:354
  36.7 13.7 %all_to_all.21.received_ref = f32[8,9,4,128]{3,2,1,0:T(4,128)S(1)} all-to-all(f32[8,9,4,128]{3,2,1,0:T(4,128)S(1)} %forces_of_pairs.1), channel_id=1, replica_groups=mesh['gx'=8,'gy'=8,'gz'=8] {'gx'}, dimensions={0} | all-to-all | bytes 294912 | tf_op jit(solution)/shard_map/all_to_all | solution.py:465
  50.5 17.3 %all_to_all.22.received_ref = f32[64,4,128]{2,1,0:T(4,128)S(1)} all-to-all(f32[64,4,128]{2,1,0:T(4,128)S(1)} %address_plane.1), channel_id=1, replica_groups=mesh['gx'=8,'gy'=8,'gz'=8] {'gy','gz'}, dimensions={0} | all-to-all | bytes 262144 | tf_op jit(solution)/shard_map/all_to_all | solution.py:473
  67.7 0.7 %finish.1 = (f32[3,1,128]{2,1,0:T(1,128)}, f32[1]{0:T(128)}) custom-call(f32[64,4,128]{2,1,0:T(4,128)S(1)} %all_to_all.22.received_ref), custom_call_target="tpu_custom_call" | custom-call | tf_op jit(solution)/shard_map/finish/pallas_call | solution.py:466
  (7 shorter events, 0.1 us)
Async XLA Ops:
  0.6 0.7 %copy-start.7 = (f32[1,1,1,3,128]{4,2,3,1,0:T(1,128)S(1)}, f32[1,1,1,3,128]{4,2,3,1,0:T(1,128)}, u32[]{:S(2)}) copy-start(f32[1,1,1,3,128]{4,2,3,1,0:T(1,128)} %param.9) | copy-start | bytes 4612
  0.6 29.2 %copy-start.1 = (bf16[512,512]{1,0:T(8,128)(2,1)S(1)}, bf16[512,512]{1,0:T(8,128)(2,1)}, u32[]{:S(2)}) copy-start(bf16[512,512]{1,0:T(8,128)(2,1)} %w_hid_ref.1) | copy-start | bytes 1572868
  22.1 7.5 %copy-start.6 = (bf16[512,12]{0,1:T(8,128)(2,1)S(1)}, bf16[512,12]{0,1:T(8,128)(2,1)}, u32[]{:S(2)}) copy-start(bf16[512,12]{0,1:T(8,128)(2,1)} %param.13) | copy-start | bytes 36868
  22.8 6.9 %copy-start.2 = (bf16[64,512]{1,0:T(8,128)(2,1)S(1)}, bf16[64,512]{1,0:T(8,128)(2,1)}, u32[]{:S(2)}) copy-start(bf16[64,512]{1,0:T(8,128)(2,1)} %w_env_ref.1) | copy-start | bytes 196612
  22.8 11.0 %all-to-all-start.1 = ((f32[8,6,4,128]{3,2,1,0:T(4,128)}), f32[8,6,4,128]{3,2,1,0:T(4,128)S(1)}, u32[]{:S(2)}, u32[]{:S(2)}) async-start(f32[8,6,4,128]{3,2,1,0:T(4,128)} %relay_frames.1), calls=%async_computation.1 | async-start | bytes 196608 | tf_op jit(solution)/shard_map/all_to_all | solution.py:417
  29.6 1.1 %copy-start = (bf16[512,704]{0,1:T(8,128)(2,1)S(1)}, bf16[512,704]{0,1:T(8,128)(2,1)}, u32[]{:S(2)}) copy-start(bf16[512,704]{0,1:T(8,128)(2,1)} %param.16) | copy-start | bytes 2162692
  31.0 0.7 %copy-start.4 = (bf16[1,512]{1,0:T(2,128)(2,1)S(1)}, bf16[1,512]{1,0:T(2,128)(2,1)}, u32[]{:S(2)}) copy-start(bf16[1,512]{1,0:T(2,128)(2,1)} %w_out_ref.1) | copy-start | bytes 3076
  31.0 0.7 %copy-start.3 = (s32[1,1,1,2,256]{4,3,2,1,0:T(2,128)S(1)}, s32[1,1,1,2,256]{4,3,2,1,0:T(2,128)}, u32[]{:S(2)}) copy-start(s32[1,1,1,2,256]{4,3,2,1,0:T(2,128)} %param.11) | copy-start | bytes 6148
  31.0 0.7 copy-start.5

commit v7 on v6

--- a/solution.py
+++ b/solution.py
@@ -60,13 +60,9 @@
     return lax.axis_index("gx"), lax.axis_index("gy"), at_z >> 1, at_z & 1
 
 
-def around():
-    at_y, at_z = lax.axis_index("gy"), lax.axis_index("gz")
-    return [
-        ((at_y + (RING + step_y)) & (RING - 1)) * RING + ((at_z + (RING + step_z)) & (RING - 1))
-        for step_y in (-1, 0, 1)
-        for step_z in (-1, 0, 1)
-    ]
+def back_place(at_x):
+    turned = (at_x + (RING - 1)) & (RING - 1)
+    return (turned & 1) + 2 * (turned >> 2)
 
 
 def relay_kernel(near_ref, out_ref):
@@ -102,17 +98,43 @@
         odd_ref[cell] = far_ref[(1 - side) * 4 + chip_third, row]
 
 
-def address_kernel(received_ref, out_ref):
-    total = jnp.sum(received_ref[...], axis=0)
+def combine_kernel(received_ref, home_ref, out_ref):
+    at_x, at_y, chip, high = place_of()
+    own, other = (at_x & 1) * 16, (1 - (at_x & 1)) * 16
+    back = back_place(at_x)
+    beside = back ^ 1
+    chip_third = (chip + 5 - 2 * high) & 3
     is_energy = lax.broadcasted_iota(jnp.int32, (4, ATOMS), 0) == 3
-    blank = jnp.where(is_energy, total[4], 0.0)
+
+    def moved(member, cell):
+        return jnp.where(is_energy, 0.0, received_ref[member, cell])
+
+    total = received_ref[0, 0]
+    for member in range(1, 16):
+        total = total + received_ref[member, 0]
+    blank = jnp.where(is_energy, total, 0.0)
     out_ref[...] = jnp.broadcast_to(blank[None], out_ref.shape)
-    for cell, number in enumerate(around()):
-        out_ref[number] = total[cell]
+    for row in range(3):
+        number = ((at_y + (RING - 1 + row)) & (RING - 1)) * 2
+        for level in range(2):
+            cell = 2 * row + level
+            mine = home_ref[cell] + moved(beside * 4 + chip, cell)
+            out_ref[own + number + level] = blank + mine
+            out_ref[other + number + level] = blank + home_ref[6 + cell]
+        across = number + 1 - high
+        third = moved(back * 4 + chip_third, row) + moved(beside * 4 + chip_third, row)
+        out_ref[own + across] = out_ref[own + across] + third
+        out_ref[other + across] = out_ref[other + across] + moved(back * 4 + chip_third, 3 + row)
 
 
 def finish_kernel(received_ref, forces_ref, energy_ref):
-    total = jnp.sum(received_ref[...], axis=0)
+    halves = []
+    for start in (0, 16):
+        total = received_ref[start]
+        for member in range(start + 1, start + 16):
+            total = total + received_ref[member]
+        halves.append(total)
+    total = halves[0] + halves[1]
     for axis in range(3):
         forces_ref[axis] = total[axis : axis + 1]
     energy_ref[0] = jnp.sum(total[3:4]) * (1.0 / (ATOMS * RING**3))
@@ -150,6 +172,7 @@
     w_lat_t_ref,
     w_out_ref,
     out_ref,
+    home_ref,
     z1_ref,
     z2_ref,
     z3_ref,
@@ -158,6 +181,7 @@
     grad_ref,
     dz_ref,
     dlat_ref,
+    spread_ref,
 ):
     centre = pairs_ref[0:1, :]
     slot = pairs_ref[1:2, :]
@@ -168,8 +192,7 @@
     step_y = (rest * 11) >> 5
     step_z = rest - 3 * step_y
 
-    place = lax.axis_index("gx")
-    parity = place & 1
+    parity = lax.axis_index("gx") & 1
     near, own = [], []
     for half in range(2):
         lanes = slice(half * ATOMS, (half + 1) * ATOMS)
@@ -334,28 +357,40 @@
     moved = jnp.where(axis == 3, 0.0, moved)
     spread = split_dot_nt(jnp.where((row >> 2) == slot, -moved, 0.0), hits_ref[0])
     home = split_dot_nt(moved[0:8], hits_ref[1])[0:4]
-    spread = spread.reshape(28, 4, ATOMS)
+    spread_ref[...] = spread.reshape(28, 4, ATOMS)
+    spread_ref[13] = spread_ref[13] + home
     energy = column_sum(energy)
     energy = energy[:, 0:ATOMS] + energy[:, ATOMS:PAIRS]
     is_energy = lax.broadcasted_iota(jnp.int32, (4, ATOMS), 0) == 3
     blank = jnp.where(is_energy, energy, 0.0)
     out_ref[...] = jnp.broadcast_to(blank[None, None], out_ref.shape)
-    for at_x in range(3):
-        number = (place + (at_x + RING - 1)) & (RING - 1)
-        for cell in range(9):
-            block = spread[9 * at_x + cell]
-            if 9 * at_x + cell == 13:
-                block = block + home
-            out_ref[number, cell] = block + blank
+    at_x, unused, chip, high = place_of()
+    aligned, shifted = 18 * (1 - parity), 18 * parity
+    back = back_place(at_x)
+    beside = back ^ 1
+    chip_third = (chip + 3 + 2 * high) & 3
+    for row in range(3):
+        for level in range(2):
+            cell, slot_at = 2 * row + level, 3 * row + 1 + level - high
+            home_ref[cell] = spread_ref[9 + slot_at]
+            home_ref[6 + cell] = spread_ref[aligned + slot_at]
+            out_ref[beside * 4 + chip, cell] = blank + spread_ref[shifted + slot_at]
+        slot_at = 3 * row + 2 * high
+        out_ref[back * 4 + chip_third, row] = blank + spread_ref[9 + slot_at]
+        out_ref[back * 4 + chip_third, 3 + row] = blank + spread_ref[aligned + slot_at]
+        out_ref[beside * 4 + chip_third, row] = blank + spread_ref[shifted + slot_at]
 
 
 def pair_forces(*operands):
     vmem = pl.BlockSpec(memory_space=pltpu.VMEM)
     return pl.pallas_call(
         force_kernel,
-        out_shape=jax.ShapeDtypeStruct((RING, 9, 4, ATOMS), F32),
+        out_shape=(
+            jax.ShapeDtypeStruct((16, 6, 4, ATOMS), F32),
+            jax.ShapeDtypeStruct((12, 4, ATOMS), F32),
+        ),
         in_specs=[vmem] * 15,
-        out_specs=vmem,
+        out_specs=(vmem, vmem),
         scratch_shapes=[
             pltpu.VMEM((LAT, PAIRS), F32),
             pltpu.VMEM((LAT, PAIRS), F32),
@@ -365,6 +400,7 @@
             pltpu.VMEM((LAT + 3 * CH, PAIRS), F32),
             pltpu.VMEM((LAT, PAIRS), BF16),
             pltpu.VMEM((LAT, PAIRS), F32),
+            pltpu.VMEM((28, 4, ATOMS), F32),
         ],
         compiler_params=pltpu.CompilerParams(vmem_limit_bytes=24 * 1024 * 1024),
         name="forces_of_pairs",
@@ -387,6 +423,12 @@
 FAR = [
     [flat(2 * pair + 1 + i, at_y, chip, high) for i in range(2) for chip in range(4)]
     for pair in range(4)
+    for at_y in range(8)
+    for high in range(2)
+]
+BACK = [
+    [flat(base + i, at_y, chip, high) for i in (0, 1, 4, 5) for chip in range(4)]
+    for base in (1, 3)
     for at_y in range(8)
     for high in range(2)
 ]
@@ -438,7 +480,7 @@
         name="prepare_pairs",
     )(counts, ids, w_out)
     w_in = jnp.pad(w_two_in, ((0, 0), (0, 4)))
-    sent = pair_forces(
+    sent, home = pair_forces(
         pairs,
         hits,
         even,
@@ -455,14 +497,14 @@
         w_latent.T,
         readout,
     )
-    addressed = pl.pallas_call(
-        address_kernel,
-        out_shape=jax.ShapeDtypeStruct((RING * RING, 4, ATOMS), F32),
-        in_specs=[vmem],
+    combined = pl.pallas_call(
+        combine_kernel,
+        out_shape=jax.ShapeDtypeStruct((32, 4, ATOMS), F32),
+        in_specs=[vmem] * 2,
         out_specs=vmem,
         compiler_params=SMALL,
-        name="address_plane",
-    )(lax.all_to_all(sent, "gx", 0, 0))
+        name="combine_forces",
+    )(lax.all_to_all(sent, AXES, 0, 0, axis_index_groups=BACK), home)
     forces, energy = pl.pallas_call(
         finish_kernel,
         out_shape=(jax.ShapeDtypeStruct((3, 1, ATOMS), F32), jax.ShapeDtypeStruct((1,), F32)),
@@ -470,7 +512,7 @@
         out_specs=(vmem, smem),
         compiler_params=SMALL,
         name="finish",
-    )(lax.all_to_all(addressed, ("gy", "gz"), 0, 0))
+    )(lax.all_to_all(combined, AXES, 0, 0, axis_index_groups=NEAR))
     return forces.reshape(1, 1, 1, 3, ATOMS), energy.reshape(())
 
 

time: 68.9 us -> 66.7 us (0.968)
  blocking collectives: 51.7 us -> 49.6 us
    all_to_all x2, blocking collectives: 31 us -> 28.9 us  [the longest x1 14.5 us: body(): lax.all_to_all(sent, AXES, 0, 0, axis_index_groups=BACK)]
where the time goes in v7:
time: 66.7 us; the launch traced here: 66.3 us
  blocking collectives  49.6 us (74%)
  starting transfers between devices  6.77 us (10%)
  Pallas kernels  4.98 us (7%)
  local copies, waits for them, and re-layouts  2.08 us (3%)
  waiting for transfers between devices  1.41 us (2%)
  between operations  0.74 us (1%)
  other arithmetic  0.73 us (1%)
    all_to_all x1, blocking collectives, body(): near = lax.all_to_all(packed, AXES, 0, 0, axis_index_groups=NEAR)  20.7 us
    all_to_all x1, blocking collectives, body(): lax.all_to_all(sent, AXES, 0, 0, axis_index_groups=BACK)  14.5 us
    all_to_all x1, blocking collectives, body(): lax.all_to_all(combined, AXES, 0, 0, axis_index_groups=NEAR)  14.3 us
    all_to_all x1, starting transfers between devices, body(): far = lax.all_to_all(relayed, AXES, 0, 0, axis_index_groups=FAR)  6.77 us
    pallas_call x1, Pallas kernels, pair_forces(): pl.pallas_call(force_kernel, out_shape=(jax.ShapeDtypeStruct((16, 6, 4, A...  2.85 us
    unnamed x21, local copies, waits for them, and re-layouts  2.05 us
    all_to_all x1, waiting for transfers between devices, body(): far = lax.all_to_all(relayed, AXES, 0, 0, axis_index_groups=FAR)  1.41 us
  transfers between devices with their start and end apart: 1, of which 1 were waited for; matrix products, arithmetic and copies ran while one was open for 1% of the time, Pallas kernels for 1%

profile of v7, /device:TPU:1, one launch (start us, length us, event | category | flops | bytes accessed | tf_op | source)
XLA Modules:
  0.0 66.3 jit_solution(8392272090174673345)
XLA Ops:
  0.6 0.0 copy-start.7
  0.6 0.0 copy-start.1
  0.6 0.7 %convert_bitcast_fusion = f32[1,128]{1,0:T(1,128)S(1)} fusion(s32[1,1,1,128]{3,2,1,0:T(1,128)} %param.10), kind=kLoop, calls=%fused_computation.2 | loop fusion | flops 128 | bytes 1024 | tf_op jit(solution)/shard_map/convert_element_type | solution.py:449
  1.4 0.0 copy-done.7
  1.4 20.7 %all_to_all.20.near_ref = f32[32,4,128]{2,1,0:T(4,128)S(1)} all-to-all(f32[32,4,128]{2,1,0:T(4,128)S(1)} %pack_frame.1), channel_id=1, replica_groups={{0,1,8,9,16,17,24,25,32,33,40,41,48,49,56,57,64,65,72,73,80,81,88,89,96..., dimensions={0} | all-to-all | bytes 131072 | tf_op jit(solution)/shard_map/all_to_all | solution.py:450
  22.1 0.0 copy-start.6
  22.1 0.7 relay_frames.1
  22.8 0.0 copy-start.2
  22.8 6.8 %all-to-all-start.1 = ((f32[8,6,4,128]{3,2,1,0:T(4,128)}), f32[8,6,4,128]{3,2,1,0:T(4,128)S(1)}, u32[]{:S(2)}, u32[]{:S(2)}) async-start(f32[8,6,4,128]{3,2,1,0:T(4,128)} %relay_frames.1), calls=%async_computation.1 | async-start | bytes 196608 | tf_op jit(solution)/shard_map/all_to_all | solution.py:459
  29.6 0.0 copy-done.6
  29.6 0.0 copy-start
  29.6 0.2 copy.18
  29.7 0.0 copy-done.2
  29.7 0.1 copy.12
  29.9 0.0 copy-done.1
  29.9 0.2 copy.11
  30.1 0.6 copy-done
  30.7 0.3 copy.14.w_lat_ref
  31.0 0.0 copy-start.4
  31.0 0.0 copy-start.3
  31.0 0.0 copy-start.5
  31.0 0.6 copy-done.4
  31.7 0.0 copy-done.3
  31.7 0.0 copy-done.5
  31.7 0.7 %prepare_pairs.1 = (s32[8,256]{1,0:T(8,128)S(1)}, bf16[2,128,256]{2,1,0:T(8,128)(2,1)S(1)}, bf16[256,256]{1,0:T(8,128)(2,1)S(1)}, bf16[512,128]{1,0:T(8,128)(2,1)S(1)}) custom-call(s32[2]{0:T(128)S(1)} %bitcast.20, s32[2,256]{1,0:T(2,128)S(1)} %bitcast.19, bf16[1,512]{1,0:T(2,128)(2,1)S(1)} %copy-done.4), custom_call_target="tpu_custom_call" | custom-call | tf_op jit(solution)/shard_map/prepare_pairs/pallas_call | solution.py:469
  32.4 1.4 %all-to-all-done.1.far_ref = f32[8,6,4,128]{3,2,1,0:T(4,128)S(1)} async-done(((f32[8,6,4,128]{3,2,1,0:T(4,128)}), f32[8,6,4,128]{3,2,1,0:T(4,128)S(1)}, u32[]{:S(2)}, u32[]{:S(2)}) %all-to-all-start.1) | async-done | bytes 98336 | tf_op jit(solution)/shard_map/all_to_all | solution.py:459
  33.9 2.9 %forces_of_pairs.1 = (f32[16,6,4,128]{3,2,1,0:T(4,128)S(1)}, f32[12,4,128]{2,1,0:T(4,128)S(1)}) custom-call(s32[8,256]{1,0:T(8,128)S(1)} %get-tuple-element.13.pairs_ref, bf16[2,128,256]{2,1,0:T(8,128)(2,1)S(1)} %get-tuple-element.14.hits_ref, f32[9,4,128]{2,1,0:T(4,128)S(1)} %get-tuple-element.15.even_ref, f32[9,4,128]{2,1,0:T(4,128)S(1)} %get-tuple-element.16.level_ref, ...), custom_call_target="tpu_custom_call" | custom-call | tf_op jit(solution)/shard_map/forces_of_pairs/pallas_call | solution.py:386
  36.7 14.5 %all_to_all.21.received_ref = f32[16,6,4,128]{3,2,1,0:T(4,128)S(1)} all-to-all(f32[16,6,4,128]{3,2,1,0:T(4,128)S(1)} %get-tuple-element.20), channel_id=1, replica_groups={{64,66,68,70,128,130,132,134,320,322,324,326,384,386,388,390},{65,67,69..., dimensions={0} | all-to-all | bytes 393216 | tf_op jit(solution)/shard_map/all_to_all | solution.py:507
  51.2 0.1 combine_forces.1
  51.3 14.3 %all_to_all.22.received_ref = f32[32,4,128]{2,1,0:T(4,128)S(1)} all-to-all(f32[32,4,128]{2,1,0:T(4,128)S(1)} %combine_forces.1), channel_id=1, replica_groups={{0,1,8,9,16,17,24,25,32,33,40,41,48,49,56,57,64,65,72,73,80,81,88,89,96..., dimensions={0} | all-to-all | bytes 131072 | tf_op jit(solution)/shard_map/all_to_all | solution.py:515
  65.6 0.7 finish.1
  (6 shorter events, 0.1 us)
Async XLA Ops:
  0.6 0.7 %copy-start.7 = (f32[1,1,1,3,128]{4,2,3,1,0:T(1,128)S(1)}, f32[1,1,1,3,128]{4,2,3,1,0:T(1,128)}, u32[]{:S(2)}) copy-start(f32[1,1,1,3,128]{4,2,3,1,0:T(1,128)} %param.9) | copy-start | bytes 4612
  0.6 29.2 %copy-start.1 = (bf16[512,512]{1,0:T(8,128)(2,1)S(1)}, bf16[512,512]{1,0:T(8,128)(2,1)}, u32[]{:S(2)}) copy-start(bf16[512,512]{1,0:T(8,128)(2,1)} %w_hid_ref.1) | copy-start | bytes 1572868
  22.1 7.4 %copy-start.6 = (bf16[512,12]{0,1:T(8,128)(2,1)S(1)}, bf16[512,12]{0,1:T(8,128)(2,1)}, u32[]{:S(2)}) copy-start(bf16[512,12]{0,1:T(8,128)(2,1)} %param.13) | copy-start | bytes 36868
  22.8 6.9 %copy-start.2 = (bf16[64,512]{1,0:T(8,128)(2,1)S(1)}, bf16[64,512]{1,0:T(8,128)(2,1)}, u32[]{:S(2)}) copy-start(bf16[64,512]{1,0:T(8,128)(2,1)} %w_env_ref.1) | copy-start | bytes 196612
  22.8 11.0 %all-to-all-start.1 = ((f32[8,6,4,128]{3,2,1,0:T(4,128)}), f32[8,6,4,128]{3,2,1,0:T(4,128)S(1)}, u32[]{:S(2)}, u32[]{:S(2)}) async-start(f32[8,6,4,128]{3,2,1,0:T(4,128)} %relay_frames.1), calls=%async_computation.1 | async-start | bytes 196608 | tf_op jit(solution)/shard_map/all_to_all | solution.py:459
  29.6 1.1 %copy-start = (bf16[512,704]{0,1:T(8,128)(2,1)S(1)}, bf16[512,704]{0,1:T(8,128)(2,1)}, u32[]{:S(2)}) copy-start(bf16[512,704]{0,1:T(8,128)(2,1)} %param.16) | copy-start | bytes 2162692
  31.0 0.7 %copy-start.4 = (bf16[1,512]{1,0:T(2,128)(2,1)S(1)}, bf16[1,512]{1,0:T(2,128)(2,1)}, u32[]{:S(2)}) copy-start(bf16[1,512]{1,0:T(2,128)(2,1)} %w_out_ref.1) | copy-start | bytes 3076
  31.0 0.7 %copy-start.3 = (s32[1,1,1,2,256]{4,3,2,1,0:T(2,128)S(1)}, s32[1,1,1,2,256]{4,3,2,1,0:T(2,128)}, u32[]{:S(2)}) copy-start(s32[1,1,1,2,256]{4,3,2,1,0:T(2,128)} %param.11) | copy-start | bytes 6148
  31.0 0.7 %copy-start.5 = (s32[1,1,1,2]{3,2,1,0:T(1,128)S(1)}, s32[1,1,1,2]{3,2,1,0:T(1,128)}, u32[]{:S(2)}) copy-start(s32[1,1,1,2]{3,2,1,0:T(1,128)} %param.12) | copy-start | bytes 28

commit v8 on v7

--- a/solution.py
+++ b/solution.py
@@ -21,7 +21,7 @@
 CH = 64
 PAIRS = 256
 ATOMS = 128
-ROWS = 64
+ROWS = 128
 
 
 def column_sum(block):
@@ -248,16 +248,18 @@
     kind = jnp.where((row8 < 4) & (kind_at == (row8 & 1).astype(F32)), 1.0, 0.0)
     features = jnp.concatenate([bessel * cut, kind], axis=0).astype(BF16)
 
-    z1_ref[...] = jnp.dot(w_in_ref[...], features, preferred_element_type=F32)
     for start in range(0, LAT, ROWS):
         rows = pl.ds(start, ROWS)
-        value, gate = silu_parts(z1_ref[rows, :])
+        value, gate = silu_parts(
+            jnp.dot(w_in_ref[rows, :], features, preferred_element_type=F32)
+        )
         hidden_ref[rows, :] = value.astype(BF16)
         z1_ref[rows, :] = gate
-    z2_ref[...] = jnp.dot(w_hid_ref[...], hidden_ref[...], preferred_element_type=F32)
     for start in range(0, LAT, ROWS):
         rows = pl.ds(start, ROWS)
-        value, unused = silu_parts(z2_ref[rows, :])
+        z2 = jnp.dot(w_hid_ref[rows, :], hidden_ref[...], preferred_element_type=F32)
+        z2_ref[rows, :] = z2
+        value, unused = silu_parts(z2)
         joined_ref[rows, :] = (value * cut).astype(BF16)
 
     unit = [part * inverse for part in delta]
@@ -332,11 +334,11 @@
         )
         both = both.astype(BF16) * same
         shape_grad.append(jnp.dot(shapes[degree - 1], both, preferred_element_type=F32))
-    dlat_ref[...] = jnp.dot(w_hid_t_ref[...], dz_ref[...], preferred_element_type=F32)
     for start in range(0, LAT, ROWS):
         rows = pl.ds(start, ROWS)
-        dz_ref[rows, :] = (dlat_ref[rows, :] * z1_ref[rows, :]).astype(BF16)
-    feature_grad = jnp.dot(w_in_t_ref[...], dz_ref[...], preferred_element_type=F32)[0:8, :]
+        hidden_grad = jnp.dot(w_hid_t_ref[rows, :], dz_ref[...], preferred_element_type=F32)
+        hidden_ref[rows, :] = (hidden_grad * z1_ref[rows, :]).astype(BF16)
+    feature_grad = jnp.dot(w_in_t_ref[...], hidden_ref[...], preferred_element_type=F32)[0:8, :]
 
     cut_grad = column_sum(cut_grad + feature_grad * bessel)
     radius_grad = cut_grad * slope + cut * column_sum(feature_grad * bessel_slope)

time: 66.7 us -> 66.6 us (level)
  no operation moved by 1% of the time
where the time goes in v8:
time: 66.6 us; the launch traced here: 66.2 us
  blocking collectives  49.6 us (74%)
  starting transfers between devices  6.77 us (10%)
  Pallas kernels  4.88 us (7%)
  local copies, waits for them, and re-layouts  2.08 us (3%)
  waiting for transfers between devices  1.41 us (2%)
  between operations  0.74 us (1%)
  other arithmetic  0.73 us (1%)
    all_to_all x1, blocking collectives, body(): near = lax.all_to_all(packed, AXES, 0, 0, axis_index_groups=NEAR)  20.7 us
    all_to_all x1, blocking collectives, body(): lax.all_to_all(sent, AXES, 0, 0, axis_index_groups=BACK)  14.5 us
    all_to_all x1, blocking collectives, body(): lax.all_to_all(combined, AXES, 0, 0, axis_index_groups=NEAR)  14.3 us
    all_to_all x1, starting transfers between devices, body(): far = lax.all_to_all(relayed, AXES, 0, 0, axis_index_groups=FAR)  6.77 us
    pallas_call x1, Pallas kernels, pair_forces(): pl.pallas_call(force_kernel, out_shape=(jax.ShapeDtypeStruct((16, 6, 4, A...  2.76 us
    unnamed x21, local copies, waits for them, and re-layouts  2.05 us
    all_to_all x1, waiting for transfers between devices, body(): far = lax.all_to_all(relayed, AXES, 0, 0, axis_index_groups=FAR)  1.41 us
  transfers between devices with their start and end apart: 1, of which 1 were waited for; matrix products, arithmetic and copies ran while one was open for 1% of the time, Pallas kernels for 1%

profile of v8, /device:TPU:1, one launch (start us, length us, event | category | flops | bytes accessed | tf_op | source)
XLA Modules:
  0.0 66.2 jit_solution(9207394260043839124)
XLA Ops:
  0.6 0.0 copy-start.7
  0.6 0.0 copy-start.1
  0.6 0.7 %convert_bitcast_fusion = f32[1,128]{1,0:T(1,128)S(1)} fusion(s32[1,1,1,128]{3,2,1,0:T(1,128)} %param.10), kind=kLoop, calls=%fused_computation.2 | loop fusion | flops 128 | bytes 1024 | tf_op jit(solution)/shard_map/convert_element_type | solution.py:451
  1.4 0.0 copy-done.7
  1.4 20.7 %all_to_all.20.near_ref = f32[32,4,128]{2,1,0:T(4,128)S(1)} all-to-all(f32[32,4,128]{2,1,0:T(4,128)S(1)} %pack_frame.1), channel_id=1, replica_groups={{0,1,8,9,16,17,24,25,32,33,40,41,48,49,56,57,64,65,72,73,80,81,88,89,96..., dimensions={0} | all-to-all | bytes 131072 | tf_op jit(solution)/shard_map/all_to_all | solution.py:452
  22.1 0.0 copy-start.6
  22.1 0.7 %relay_frames.1 = f32[8,6,4,128]{3,2,1,0:T(4,128)} custom-call(f32[32,4,128]{2,1,0:T(4,128)S(1)} %all_to_all.20.near_ref), custom_call_target="tpu_custom_call" | custom-call | tf_op jit(solution)/shard_map/relay_frames/pallas_call | solution.py:453
  22.8 0.0 copy-start.2
  22.8 6.8 %all-to-all-start.1 = ((f32[8,6,4,128]{3,2,1,0:T(4,128)}), f32[8,6,4,128]{3,2,1,0:T(4,128)S(1)}, u32[]{:S(2)}, u32[]{:S(2)}) async-start(f32[8,6,4,128]{3,2,1,0:T(4,128)} %relay_frames.1), calls=%async_computation.1 | async-start | bytes 196608 | tf_op jit(solution)/shard_map/all_to_all | solution.py:461
  29.6 0.0 copy-done.6
  29.6 0.0 copy-start
  29.6 0.2 copy.18
  29.7 0.0 copy-done.2
  29.7 0.1 copy.12
  29.9 0.0 copy-done.1
  29.9 0.2 copy.11
  30.1 0.6 copy-done
  30.7 0.3 copy.14.w_lat_ref
  31.0 0.0 copy-start.4
  31.0 0.0 copy-start.3
  31.0 0.0 copy-start.5
  31.0 0.6 copy-done.4
  31.7 0.0 copy-done.3
  31.7 0.0 copy-done.5
  31.7 0.7 %prepare_pairs.1 = (s32[8,256]{1,0:T(8,128)S(1)}, bf16[2,128,256]{2,1,0:T(8,128)(2,1)S(1)}, bf16[256,256]{1,0:T(8,128)(2,1)S(1)}, bf16[512,128]{1,0:T(8,128)(2,1)S(1)}) custom-call(s32[2]{0:T(128)S(1)} %bitcast.20, s32[2,256]{1,0:T(2,128)S(1)} %bitcast.19, bf16[1,512]{1,0:T(2,128)(2,1)S(1)} %copy-done.4), custom_call_target="tpu_custom_call" | custom-call | tf_op jit(solution)/shard_map/prepare_pairs/pallas_call | solution.py:471
  32.4 1.4 %all-to-all-done.1.far_ref = f32[8,6,4,128]{3,2,1,0:T(4,128)S(1)} async-done(((f32[8,6,4,128]{3,2,1,0:T(4,128)}), f32[8,6,4,128]{3,2,1,0:T(4,128)S(1)}, u32[]{:S(2)}, u32[]{:S(2)}) %all-to-all-start.1) | async-done | bytes 98336 | tf_op jit(solution)/shard_map/all_to_all | solution.py:461
  33.9 2.8 %forces_of_pairs.1 = (f32[16,6,4,128]{3,2,1,0:T(4,128)S(1)}, f32[12,4,128]{2,1,0:T(4,128)S(1)}) custom-call(s32[8,256]{1,0:T(8,128)S(1)} %get-tuple-element.13.pairs_ref, bf16[2,128,256]{2,1,0:T(8,128)(2,1)S(1)} %get-tuple-element.14.hits_ref, f32[9,4,128]{2,1,0:T(4,128)S(1)} %get-tuple-element.15.even_ref, f32[9,4,128]{2,1,0:T(4,128)S(1)} %get-tuple-element.16.level_ref, ...), custom_call_target="tpu_custom_call" | custom-call | tf_op jit(solution)/shard_map/forces_of_pairs/pallas_call | solution.py:388
  36.6 14.5 %all_to_all.21.received_ref = f32[16,6,4,128]{3,2,1,0:T(4,128)S(1)} all-to-all(f32[16,6,4,128]{3,2,1,0:T(4,128)S(1)} %get-tuple-element.20), channel_id=1, replica_groups={{64,66,68,70,128,130,132,134,320,322,324,326,384,386,388,390},{65,67,69..., dimensions={0} | all-to-all | bytes 393216 | tf_op jit(solution)/shard_map/all_to_all | solution.py:509
  51.2 0.1 combine_forces.1
  51.2 14.3 %all_to_all.22.received_ref = f32[32,4,128]{2,1,0:T(4,128)S(1)} all-to-all(f32[32,4,128]{2,1,0:T(4,128)S(1)} %combine_forces.1), channel_id=1, replica_groups={{0,1,8,9,16,17,24,25,32,33,40,41,48,49,56,57,64,65,72,73,80,81,88,89,96..., dimensions={0} | all-to-all | bytes 131072 | tf_op jit(solution)/shard_map/all_to_all | solution.py:517
  65.6 0.7 finish.1
  (6 shorter events, 0.1 us)
Async XLA Ops:
  0.6 0.7 %copy-start.7 = (f32[1,1,1,3,128]{4,2,3,1,0:T(1,128)S(1)}, f32[1,1,1,3,128]{4,2,3,1,0:T(1,128)}, u32[]{:S(2)}) copy-start(f32[1,1,1,3,128]{4,2,3,1,0:T(1,128)} %param.9) | copy-start | bytes 4612
  0.6 29.2 %copy-start.1 = (bf16[512,512]{1,0:T(8,128)(2,1)S(1)}, bf16[512,512]{1,0:T(8,128)(2,1)}, u32[]{:S(2)}) copy-start(bf16[512,512]{1,0:T(8,128)(2,1)} %w_hid_ref.1) | copy-start | bytes 1572868
  22.1 7.4 %copy-start.6 = (bf16[512,12]{0,1:T(8,128)(2,1)S(1)}, bf16[512,12]{0,1:T(8,128)(2,1)}, u32[]{:S(2)}) copy-start(bf16[512,12]{0,1:T(8,128)(2,1)} %param.13) | copy-start | bytes 36868
  22.8 6.9 %copy-start.2 = (bf16[64,512]{1,0:T(8,128)(2,1)S(1)}, bf16[64,512]{1,0:T(8,128)(2,1)}, u32[]{:S(2)}) copy-start(bf16[64,512]{1,0:T(8,128)(2,1)} %w_env_ref.1) | copy-start | bytes 196612
  22.8 11.0 %all-to-all-start.1 = ((f32[8,6,4,128]{3,2,1,0:T(4,128)}), f32[8,6,4,128]{3,2,1,0:T(4,128)S(1)}, u32[]{:S(2)}, u32[]{:S(2)}) async-start(f32[8,6,4,128]{3,2,1,0:T(4,128)} %relay_frames.1), calls=%async_computation.1 | async-start | bytes 196608 | tf_op jit(solution)/shard_map/all_to_all | solution.py:461
  29.6 1.1 %copy-start = (bf16[512,704]{0,1:T(8,128)(2,1)S(1)}, bf16[512,704]{0,1:T(8,128)(2,1)}, u32[]{:S(2)}) copy-start(bf16[512,704]{0,1:T(8,128)(2,1)} %param.16) | copy-start | bytes 2162692
  31.0 0.7 %copy-start.4 = (bf16[1,512]{1,0:T(2,128)(2,1)S(1)}, bf16[1,512]{1,0:T(2,128)(2,1)}, u32[]{:S(2)}) copy-start(bf16[1,512]{1,0:T(2,128)(2,1)} %w_out_ref.1) | copy-start | bytes 3076
  31.0 0.7 %copy-start.3 = (s32[1,1,1,2,256]{4,3,2,1,0:T(2,128)S(1)}, s32[1,1,1,2,256]{4,3,2,1,0:T(2,128)}, u32[]{:S(2)}) copy-start(s32[1,1,1,2,256]{4,3,2,1,0:T(2,128)} %param.11) | copy-start | bytes 6148
  31.0 0.7 %copy-start.5 = (s32[1,1,1,2]{3,2,1,0:T(1,128)S(1)}, s32[1,1,1,2]{3,2,1,0:T(1,128)}, u32[]{:S(2)}) copy-start(s32[1,1,1,2]{3,2,1,0:T(1,128)} %param.12) | copy-start | bytes 28

commit v9 on v8

--- a/solution.py
+++ b/solution.py
@@ -62,7 +62,8 @@
 
 def back_place(at_x):
     turned = (at_x + (RING - 1)) & (RING - 1)
-    return (turned & 1) + 2 * (turned >> 2)
+    low, high = turned & 1, turned >> 2
+    return 2 * high + low * (3 - 4 * high)
 
 
 def relay_kernel(near_ref, out_ref):
@@ -102,7 +103,7 @@
     at_x, at_y, chip, high = place_of()
     own, other = (at_x & 1) * 16, (1 - (at_x & 1)) * 16
     back = back_place(at_x)
-    beside = back ^ 1
+    beside = 3 - back
     chip_third = (chip + 5 - 2 * high) & 3
     is_energy = lax.broadcasted_iota(jnp.int32, (4, ATOMS), 0) == 3
 
@@ -369,7 +370,7 @@
     at_x, unused, chip, high = place_of()
     aligned, shifted = 18 * (1 - parity), 18 * parity
     back = back_place(at_x)
-    beside = back ^ 1
+    beside = 3 - back
     chip_third = (chip + 3 + 2 * high) & 3
     for row in range(3):
         for level in range(2):
@@ -429,7 +430,7 @@
     for high in range(2)
 ]
 BACK = [
-    [flat(base + i, at_y, chip, high) for i in (0, 1, 4, 5) for chip in range(4)]
+    [flat(base + i, at_y, chip, high) for i in (0, 5, 4, 1) for chip in range(4)]
     for base in (1, 3)
     for at_y in range(8)
     for high in range(2)

time: 66.6 us -> 66.2 us (level)
  no operation moved by 1% of the time
where the time goes in v9:
time: 66.2 us; the launch traced here: 65.8 us
  blocking collectives  49.2 us (74%)
  starting transfers between devices  6.77 us (10%)
  Pallas kernels  4.88 us (7%)
  local copies, waits for them, and re-layouts  2.08 us (3%)
  waiting for transfers between devices  1.41 us (2%)
  between operations  0.74 us (1%)
  other arithmetic  0.73 us (1%)
    all_to_all x1, blocking collectives, body(): near = lax.all_to_all(packed, AXES, 0, 0, axis_index_groups=NEAR)  20.7 us
    all_to_all x1, blocking collectives, body(): lax.all_to_all(sent, AXES, 0, 0, axis_index_groups=BACK)  14.3 us
    all_to_all x1, blocking collectives, body(): lax.all_to_all(combined, AXES, 0, 0, axis_index_groups=NEAR)  14.2 us
    all_to_all x1, starting transfers between devices, body(): far = lax.all_to_all(relayed, AXES, 0, 0, axis_index_groups=FAR)  6.77 us
    pallas_call x1, Pallas kernels, pair_forces(): pl.pallas_call(force_kernel, out_shape=(jax.ShapeDtypeStruct((16, 6, 4, A...  2.76 us
    unnamed x21, local copies, waits for them, and re-layouts  2.05 us
    all_to_all x1, waiting for transfers between devices, body(): far = lax.all_to_all(relayed, AXES, 0, 0, axis_index_groups=FAR)  1.41 us
  transfers between devices with their start and end apart: 1, of which 1 were waited for; matrix products, arithmetic and copies ran while one was open for 1% of the time, Pallas kernels for 1%

profile of v9, /device:TPU:1, one launch (start us, length us, event | category | flops | bytes accessed | tf_op | source)
XLA Modules:
  0.0 65.8 jit_solution(376423222486596203)
XLA Ops:
  0.6 0.0 copy-start.7
  0.6 0.0 copy-start.1
  0.6 0.7 %convert_bitcast_fusion = f32[1,128]{1,0:T(1,128)S(1)} fusion(s32[1,1,1,128]{3,2,1,0:T(1,128)} %param.10), kind=kLoop, calls=%fused_computation.2 | loop fusion | flops 128 | bytes 1024 | tf_op jit(solution)/shard_map/convert_element_type | solution.py:452
  1.4 0.0 copy-done.7
  1.4 20.7 %all_to_all.20.near_ref = f32[32,4,128]{2,1,0:T(4,128)S(1)} all-to-all(f32[32,4,128]{2,1,0:T(4,128)S(1)} %pack_frame.1), channel_id=1, replica_groups={{0,1,8,9,16,17,24,25,32,33,40,41,48,49,56,57,64,65,72,73,80,81,88,89,96..., dimensions={0} | all-to-all | bytes 131072 | tf_op jit(solution)/shard_map/all_to_all | solution.py:453
  22.1 0.0 copy-start.6
  22.1 0.7 %relay_frames.1 = f32[8,6,4,128]{3,2,1,0:T(4,128)} custom-call(f32[32,4,128]{2,1,0:T(4,128)S(1)} %all_to_all.20.near_ref), custom_call_target="tpu_custom_call" | custom-call | tf_op jit(solution)/shard_map/relay_frames/pallas_call | solution.py:454
  22.8 0.0 copy-start.2
  22.8 6.8 %all-to-all-start.1 = ((f32[8,6,4,128]{3,2,1,0:T(4,128)}), f32[8,6,4,128]{3,2,1,0:T(4,128)S(1)}, u32[]{:S(2)}, u32[]{:S(2)}) async-start(f32[8,6,4,128]{3,2,1,0:T(4,128)} %relay_frames.1), calls=%async_computation.1 | async-start | bytes 196608 | tf_op jit(solution)/shard_map/all_to_all | solution.py:462
  29.6 0.0 copy-done.6
  29.6 0.0 copy-start
  29.6 0.2 copy.18
  29.7 0.0 copy-done.2
  29.7 0.1 copy.12
  29.9 0.0 copy-done.1
  29.9 0.2 copy.11
  30.1 0.6 copy-done
  30.7 0.3 copy.14.w_lat_ref
  31.0 0.0 copy-start.4
  31.0 0.0 copy-start.3
  31.0 0.0 copy-start.5
  31.0 0.6 copy-done.4
  31.7 0.0 copy-done.3
  31.7 0.0 copy-done.5
  31.7 0.7 %prepare_pairs.1 = (s32[8,256]{1,0:T(8,128)S(1)}, bf16[2,128,256]{2,1,0:T(8,128)(2,1)S(1)}, bf16[256,256]{1,0:T(8,128)(2,1)S(1)}, bf16[512,128]{1,0:T(8,128)(2,1)S(1)}) custom-call(s32[2]{0:T(128)S(1)} %bitcast.20, s32[2,256]{1,0:T(2,128)S(1)} %bitcast.19, bf16[1,512]{1,0:T(2,128)(2,1)S(1)} %copy-done.4), custom_call_target="tpu_custom_call" | custom-call | tf_op jit(solution)/shard_map/prepare_pairs/pallas_call | solution.py:472
  32.4 1.4 %all-to-all-done.1.far_ref = f32[8,6,4,128]{3,2,1,0:T(4,128)S(1)} async-done(((f32[8,6,4,128]{3,2,1,0:T(4,128)}), f32[8,6,4,128]{3,2,1,0:T(4,128)S(1)}, u32[]{:S(2)}, u32[]{:S(2)}) %all-to-all-start.1) | async-done | bytes 98336 | tf_op jit(solution)/shard_map/all_to_all | solution.py:462
  33.9 2.8 %forces_of_pairs.1 = (f32[16,6,4,128]{3,2,1,0:T(4,128)S(1)}, f32[12,4,128]{2,1,0:T(4,128)S(1)}) custom-call(s32[8,256]{1,0:T(8,128)S(1)} %get-tuple-element.13.pairs_ref, bf16[2,128,256]{2,1,0:T(8,128)(2,1)S(1)} %get-tuple-element.14.hits_ref, f32[9,4,128]{2,1,0:T(4,128)S(1)} %get-tuple-element.15.even_ref, f32[9,4,128]{2,1,0:T(4,128)S(1)} %get-tuple-element.16.level_ref, ...), custom_call_target="tpu_custom_call" | custom-call | tf_op jit(solution)/shard_map/forces_of_pairs/pallas_call | solution.py:389
  36.6 14.3 %all_to_all.21.received_ref = f32[16,6,4,128]{3,2,1,0:T(4,128)S(1)} all-to-all(f32[16,6,4,128]{3,2,1,0:T(4,128)S(1)} %get-tuple-element.20), channel_id=1, replica_groups={{64,66,68,70,384,386,388,390,320,322,324,326,128,130,132,134},{65,67,69..., dimensions={0} | all-to-all | bytes 393216 | tf_op jit(solution)/shard_map/all_to_all | solution.py:510
  50.9 0.1 combine_forces.1
  51.0 14.2 %all_to_all.22.received_ref = f32[32,4,128]{2,1,0:T(4,128)S(1)} all-to-all(f32[32,4,128]{2,1,0:T(4,128)S(1)} %combine_forces.1), channel_id=1, replica_groups={{0,1,8,9,16,17,24,25,32,33,40,41,48,49,56,57,64,65,72,73,80,81,88,89,96..., dimensions={0} | all-to-all | bytes 131072 | tf_op jit(solution)/shard_map/all_to_all | solution.py:518
  65.1 0.7 finish.1
  (6 shorter events, 0.1 us)
Async XLA Ops:
  0.6 0.7 %copy-start.7 = (f32[1,1,1,3,128]{4,2,3,1,0:T(1,128)S(1)}, f32[1,1,1,3,128]{4,2,3,1,0:T(1,128)}, u32[]{:S(2)}) copy-start(f32[1,1,1,3,128]{4,2,3,1,0:T(1,128)} %param.9) | copy-start | bytes 4612
  0.6 29.2 %copy-start.1 = (bf16[512,512]{1,0:T(8,128)(2,1)S(1)}, bf16[512,512]{1,0:T(8,128)(2,1)}, u32[]{:S(2)}) copy-start(bf16[512,512]{1,0:T(8,128)(2,1)} %w_hid_ref.1) | copy-start | bytes 1572868
  22.1 7.4 %copy-start.6 = (bf16[512,12]{0,1:T(8,128)(2,1)S(1)}, bf16[512,12]{0,1:T(8,128)(2,1)}, u32[]{:S(2)}) copy-start(bf16[512,12]{0,1:T(8,128)(2,1)} %param.13) | copy-start | bytes 36868
  22.8 6.9 %copy-start.2 = (bf16[64,512]{1,0:T(8,128)(2,1)S(1)}, bf16[64,512]{1,0:T(8,128)(2,1)}, u32[]{:S(2)}) copy-start(bf16[64,512]{1,0:T(8,128)(2,1)} %w_env_ref.1) | copy-start | bytes 196612
  22.8 11.0 %all-to-all-start.1 = ((f32[8,6,4,128]{3,2,1,0:T(4,128)}), f32[8,6,4,128]{3,2,1,0:T(4,128)S(1)}, u32[]{:S(2)}, u32[]{:S(2)}) async-start(f32[8,6,4,128]{3,2,1,0:T(4,128)} %relay_frames.1), calls=%async_computation.1 | async-start | bytes 196608 | tf_op jit(solution)/shard_map/all_to_all | solution.py:462
  29.6 1.1 %copy-start = (bf16[512,704]{0,1:T(8,128)(2,1)S(1)}, bf16[512,704]{0,1:T(8,128)(2,1)}, u32[]{:S(2)}) copy-start(bf16[512,704]{0,1:T(8,128)(2,1)} %param.16) | copy-start | bytes 2162692
  31.0 0.7 %copy-start.4 = (bf16[1,512]{1,0:T(2,128)(2,1)S(1)}, bf16[1,512]{1,0:T(2,128)(2,1)}, u32[]{:S(2)}) copy-start(bf16[1,512]{1,0:T(2,128)(2,1)} %w_out_ref.1) | copy-start | bytes 3076
  31.0 0.7 %copy-start.3 = (s32[1,1,1,2,256]{4,3,2,1,0:T(2,128)S(1)}, s32[1,1,1,2,256]{4,3,2,1,0:T(2,128)}, u32[]{:S(2)}) copy-start(s32[1,1,1,2,256]{4,3,2,1,0:T(2,128)} %param.11) | copy-start | bytes 6148
  31.0 0.7 %copy-start.5 = (s32[1,1,1,2]{3,2,1,0:T(1,128)S(1)}, s32[1,1,1,2]{3,2,1,0:T(1,128)}, u32[]{:S(2)}) copy-start(s32[1,1,1,2]{3,2,1,0:T(1,128)} %param.12) | copy-start | bytes 28
